TPU v7x, 512 devices: a whole 4x8x8 slice. The times are simulated.
512 devices in a mesh: grp: 16 (over z, core), rd: 32 (over y, x).
Axes of the slice: x: 4, y: 8, z: 8, core: 2. Of those that a mesh axis runs over, the one named last changes fastest.
Arguments:
- leaf_rows: float32 [32, 4096, 256], P('grp', 'rd'), may hold values from -0.46403883 to 0.46403883
- leaf_inverse: float32 [32, 256, 256], P('grp'), as said below
- block_pattern: int32 [32, 16], P('grp'), may hold values 0 or 1
- leaf_widths: int32 [32], P('grp'), may hold values from 128 to 256, as said below
- separator: float32 [4096, 4096], P('grp', 'rd'), as said below
Outputs:
- leaf_panels: bfloat16 [32, 4096, 256], P('grp', 'rd')
- level_panel: bfloat16 [256, 4096], P(None, 'rd')
- schur_next: float32 [4096, 4096], P('grp', 'rd')
Inputs may be any that keep to these rules, and one draw needn't show every extreme that they name: leaf_inverse[j] is lower triangular with a positive diagonal. `leaf_widths`: some leaf has width 256. `separator`: symmetric and positive definite.
All inputs are finite; a program needn't handle non-finite values. No bound on the sum of `block_pattern` on one device may be relied on, other than what follows from the above.
Results may differ from a plain program's by a relative error of at most 0.013.
Values may be sent and summed in bfloat16 or wider, within the bound.
No kernel may reach another device: no remote copies, remote signals or barrier semaphores. Data moves between devices by JAX's collectives and lax.ppermute only.
A program may use at most 64 MiB of HBM per device.

v0:
```python
import jax
import jax.numpy as jnp
from jax import lax
from jax.sharding import PartitionSpec as P


def spread(array, axis, root):
    mine = lax.axis_index(axis) == root
    return lax.psum(jnp.where(mine, array, jnp.zeros_like(array)), axis)


def body(leaf_rows, leaf_inverse, block_pattern, leaf_widths, separator):
    count, rows_rd, width = leaf_rows.shape
    blocks = block_pattern.shape[1]
    reader = lax.axis_index("rd")
    group = lax.axis_index("grp")
    product = jnp.einsum("jib,jcb->jic", leaf_rows, leaf_inverse, precision=lax.Precision.HIGHEST)
    global_rows = reader * rows_rd + jnp.arange(rows_rd, dtype=jnp.int32)
    onehot = (global_rows[:, None] // width == jnp.arange(blocks, dtype=jnp.int32)[None, :]).astype(
        jnp.float32
    )
    row_mask = jnp.dot(
        block_pattern.astype(jnp.float32), onehot.T, preferred_element_type=jnp.float32
    )
    col_mask = (jnp.arange(width, dtype=jnp.int32)[None, :] < leaf_widths[:, None]).astype(
        jnp.float32
    )
    panels = (product * row_mask[:, :, None] * col_mask[:, None, :]).astype(jnp.bfloat16)
    terms = jnp.einsum(
        "jkc,jic->ki",
        lax.all_gather(panels, "rd", axis=1, tiled=True),
        panels,
        preferred_element_type=jnp.float32,
    )
    update = lax.psum_scatter(
        terms.astype(jnp.bfloat16), "grp", scatter_dimension=0, tiled=True
    ).astype(jnp.float32)
    schur = separator - update
    own_rows = schur.shape[0]
    upper = lax.all_gather(schur, "rd", axis=1, tiled=True)
    factor = jnp.linalg.cholesky(upper[:, :width])
    solved = jax.scipy.linalg.solve_triangular(factor, upper, lower=True).astype(jnp.bfloat16)
    level_all = spread(solved, "grp", 0)
    level_own = lax.dynamic_slice_in_dim(level_all, reader * rows_rd, rows_rd, 1)
    rows_group = lax.dynamic_slice_in_dim(level_all, group * own_rows, own_rows, 1)
    outer = lax.dot_general(
        rows_group, level_own, (((0,), (0,)), ((), ())), preferred_element_type=jnp.float32
    )
    row_ids = group * own_rows + jnp.arange(own_rows, dtype=jnp.int32)
    col_ids = reader * rows_rd + jnp.arange(rows_rd, dtype=jnp.int32)
    keep = (row_ids[:, None] >= width) & (col_ids[None, :] >= width)
    schur_next = jnp.where(keep, schur - outer, jnp.float32(0.0))
    return (panels, level_own, schur_next)


def solution(mesh):
    return jax.shard_map(
        body,
        mesh=mesh,
        in_specs=(
            P("grp", "rd", None),
            P("grp", None, None),
            P("grp", None),
            P("grp"),
            P("grp", "rd"),
        ),
        out_specs=(P("grp", "rd", None), P(None, "rd"), P("grp", "rd")),
        check_vma=False,
    )
```

profile of v0, /device:TPU:1, one launch (start us, length us, event | category | flops | bytes accessed | tf_op | source)
XLA Modules:
  0.0 457.4 jit_solution(15016403055719489976)
XLA Ops:
  7.2 0.0 copy-start
  7.2 0.0 all-gather.3.cloned.1.call-start
  7.2 0.8 compare_convert_fusion
  8.0 0.9 convolution_bitcast_fusion.1
  8.9 0.0 copy-done
  8.9 2.3 fusion.4
  11.2 0.0 all-gather.3.cloned.1.call-update
  11.2 0.0 copy-start.4
  11.2 0.0 reduce-scatter.2.cloned.1.call-start
  11.3 90.2 %all-gather.3.cloned.1.call-done = bf16[2,4096,256]{2,1,0:T(8,128)(2,1)} async-done(((bf16[2,128,256]{2,1,0:T(8,128)(2,1)}), bf16[2,4096,256]{2,1,0:T(8,128)(2,1)}) %all-gather.3.cloned.1.call-update) | async-done | bytes 4194320 | tf_op jit(solution)/shard_map/all_gather | solution.py:31
  101.4 4.6 %fusion = bf16[4096,128]{0,1:T(8,128)(2,1)} fusion(bf16[2,4096,256]{2,1,0:T(8,128)(2,1)} %all-gather.3.cloned.1.call-done, bf16[2,128,256]{2,1,0:T(8,128)(2,1)} %fusion.4), kind=kOutput, calls=%fused_computation.4 | convolution fusion | flops 537395200 | bytes 5373952 | tf_op jit(solution)/shard_map/jkc,jic->ki/dot_general | solution.py:29
  106.1 0.0 reduce-scatter.2.cloned.1.call-update
  106.1 0.0 all-gather.5.cloned.1.call-start
  106.2 0.0 copy-done.4
  106.2 0.1 copy.9
  106.3 58.4 %reduce-scatter.2.cloned.1.call-done = bf16[256,128]{0,1:T(8,128)(2,1)} async-done(((bf16[4096,128]{0,1:T(8,128)(2,1)}), bf16[256,128]{0,1:T(8,128)(2,1)}) %reduce-scatter.2.cloned.1.call-update) | async-done | bytes 65552 | tf_op jit(solution)/shard_map/reduce_scatter | solution.py:35
  164.7 1.5 convert_subtract_fusion
  166.2 0.0 all-gather.5.cloned.1.call-update
  166.2 0.0 all-reduce.3.cloned.1.call-start
  166.3 88.0 %all-gather.5.cloned.1.call-done = f32[256,4096]{0,1:T(8,128)} async-done(((f32[256,128]{0,1:T(8,128)}), f32[256,4096]{0,1:T(8,128)}) %all-gather.5.cloned.1.call-update) | async-done | bytes 4194320 | tf_op jit(solution)/shard_map/all_gather | solution.py:40
  254.3 1.0 slice.62
  255.2 0.1 copy.10
  255.4 1.0 fusion.6
  256.4 11.7 %cholesky.50 = f32[128,128]{1,0:T(8,128)S(1)} custom-call(f32[128,128]{1,0:T(8,128)S(1)} %cholesky.118), custom_call_target="Cholesky" | custom-call | tf_op jit(solution)/shard_map/jit(cholesky)/cholesky | solution.py:41
  268.1 9.8 %custom-call.15 = f32[1,128,128]{1,2,0:T(8,128)S(1)} custom-call(f32[1,128,128]{2,1,0:T(8,128)S(1)} %get-tuple-element.27), custom_call_target="InvertDiagBlocksLowerTriangular" | custom-call | tf_op jit(solution)/shard_map/jit(cholesky)/cholesky | solution.py:41
  278.0 0.2 constant_dynamic-update-slice_fusion
  278.2 0.3 convolution_subtract_fusion.2
  278.4 11.7 %cholesky.105 = f32[128,128]{1,0:T(8,128)S(1)} custom-call(f32[128,128]{1,0:T(8,128)S(1)} %convolution_subtract_fusion.2), custom_call_target="Cholesky" | custom-call | tf_op jit(solution)/shard_map/jit(cholesky)/cholesky | solution.py:41
  290.2 0.7 compare_reduce_fusion
  292.1 0.1 triangular_solve.57
  292.2 4.0 while.1
  292.3 0.6 fusion.28
  292.9 1.3 bitcast_dynamic-update-slice_fusion.2
  294.3 0.6 fusion.28
  294.9 1.3 bitcast_dynamic-update-slice_fusion.2
  296.2 19.7 %custom-call.16 = f32[2,128,128]{1,2,0:T(8,128)S(1)} custom-call(f32[2,128,128]{2,1,0:T(8,128)S(1)} %get-tuple-element.10), custom_call_target="InvertDiagBlocksLowerTriangular" | custom-call | tf_op jit(solution)/shard_map/jit(_solve_triangular)/triangular_solve | solution.py:42
  315.9 0.0 copy-start.1
  315.9 3.7 fusion.17
  319.6 0.0 copy-done.1
  319.6 3.5 convolution_subtract_fusion
  323.1 2.0 convolution_convert_fusion
  325.1 1.7 maximum_select_fusion
  326.8 0.0 copy-start.2
  326.8 0.0 all-reduce.3.cloned.1.call-update
  326.9 121.3 %all-reduce.3.cloned.1.call-done = bf16[256,4096]{1,0:T(8,128)(2,1)} async-done(((bf16[256,4096]{1,0:T(8,128)(2,1)}), bf16[256,4096]{1,0:T(8,128)(2,1)}) %all-reduce.3.cloned.1.call-update) | async-done | bytes 2097168 | tf_op jit(solution)/shard_map/psum | solution.py:9
  448.1 0.8 constant_dynamic-slice_fusion.1
  449.0 0.0 copy-done.2
  449.0 0.0 copy-start.3
  449.0 1.2 fusion.5
  450.1 0.8 copy.12
  450.9 0.0 copy-done.3
  (12 shorter events, 0.2 us)
Async XLA Ops:
  7.2 1.7 copy-start
  7.2 94.3 %all-gather.3.cloned.1.call-start = ((), (), s32[]{:S(2)}) async-start(), calls=%async_computation.1 | async-start | bytes 4325376 | tf_op jit(solution)/shard_map/all_gather | solution.py:31
  11.2 95.0 %copy-start.4 = (f32[256,128]{1,0:T(8,128)S(1)}, f32[256,128]{1,0:T(8,128)}, u32[]{:S(2)}) copy-start(f32[256,128]{1,0:T(8,128)} %param.9) | copy-start | bytes 393220
  11.2 153.5 %reduce-scatter.2.cloned.1.call-start = ((), (), s32[]{:S(2)}) async-start(), calls=%async_computation.2 | async-start | bytes 1114112 | tf_op jit(solution)/shard_map/reduce_scatter | solution.py:35
  106.1 148.1 %all-gather.5.cloned.1.call-start = ((), (), s32[]{:S(2)}) async-start(), calls=%async_computation.3 | async-start | bytes 4325376 | tf_op jit(solution)/shard_map/all_gather | solution.py:40
  166.2 281.9 %all-reduce.3.cloned.1.call-start = ((), (), s32[]{:S(2)}) async-start(), calls=%async_computation.4 | async-start | bytes 4194304 | tf_op jit(solution)/shard_map/psum | solution.py:9
  315.9 3.7 copy-start.1
  326.8 122.2 %copy-start.2 = (f32[256,128]{0,1:T(8,128)S(1)}, f32[256,128]{0,1:T(8,128)}, u32[]{:S(2)}) copy-start(f32[256,128]{0,1:T(8,128)} %convert_subtract_fusion) | copy-start | bytes 393220
  449.0 1.9 copy-start.3
Sparse Core Ops, SparseCore 0:
  11.8 89.6 all-gather.2
  106.2 58.3 reduce-scatter.1
  168.9 85.2 all-gather.4
  327.0 121.1 all-reduce.2
where the time goes:
time: 458 us; the launch traced here: 457 us
  waiting for transfers between devices  358 us (78%)
  other arithmetic  58.7 us (13%)
  matrix products  18.6 us (4%)
  between operations  15.2 us (3%)
  local copies, waits for them, and re-layouts  6.73 us (1%)
    psum x1, waiting for transfers between devices, spread(): return lax.psum(jnp.where(mine, array, jnp.zeros_like(array)), axis)  121 us
    all_gather x1, waiting for transfers between devices, body(): lax.all_gather(panels, 'rd', axis=1, tiled=True)  90.2 us
    all_gather x1, waiting for transfers between devices, body(): upper = lax.all_gather(schur, 'rd', axis=1, tiled=True)  88 us
    reduce_scatter x1, waiting for transfers between devices, body(): lax.psum_scatter(terms.astype(jnp.bfloat16), 'grp', scatter_dimension=0,...  58.4 us
    another operation x6, other arithmetic, body(): factor = jnp.linalg.cholesky(upper[:, :width])  34 us
    another operation x3, other arithmetic, body(): jax.scipy.linalg.solve_triangular(factor, upper, lower=True)  19.7 us
  transfers between devices with their start and end apart: 4, of which 4 were waited for; matrix products, arithmetic and copies ran while one was open for 0% of the time, Pallas kernels for 0%

commit v1 on v0

v1 whole, which is shorter than its diff:
```python
import jax
import jax.numpy as jnp
from jax import lax
from jax.sharding import Mesh, PartitionSpec as P

Z, C, Y, X = 8, 2, 8, 4
HI = lax.Precision.HIGHEST
F32 = jnp.float32
BF16 = jnp.bfloat16


def dot_t(a, b, out=F32):
    return lax.dot_general(a, b, (((1,), (1,)), ((), ())), preferred_element_type=out)


def share(array, axis, size):
    copies = jnp.broadcast_to(array[None], (size,) + array.shape)
    return lax.all_to_all(copies, axis, 0, 0, tiled=True)


def body(leaf_rows, leaf_inverse, block_pattern, leaf_widths, separator):
    count, rows, width = leaf_rows.shape
    z, c, y, x = (lax.axis_index(a) for a in ("z", "c", "y", "x"))
    even = x % 2 == 0

    lead = lax.all_gather(separator, "y", axis=0)[0]

    product = jnp.einsum("jib,jcb->jic", leaf_rows, leaf_inverse, precision=HI)
    row_mask = lax.dynamic_slice_in_dim(block_pattern, 2 * y + x // 2, 1, 1).astype(F32)
    col_mask = (jnp.arange(width, dtype=jnp.int32)[None, :] < leaf_widths[:, None]).astype(F32)
    panels = (product * row_mask[:, :, None] * col_mask[:, None, :]).astype(BF16)
    own = jnp.concatenate([panels[j] for j in range(count)], axis=1)
    depth = own.shape[1]

    along_y = share(own, "y", Y)
    along_x = share(jnp.stack([own, along_y[0]]), "x", X)
    along_x = along_x.reshape(X, 2, rows, depth)
    first = along_x[:2, 1].reshape(2 * rows, depth)
    row_blocks = along_y.reshape(Y * rows, depth)
    col_blocks = along_x[:, 0].reshape(X * rows, depth)

    half = 2 * rows
    theirs = lax.dynamic_slice_in_dim(col_blocks, (1 - c) * half, half, 0)
    mine = lax.dynamic_slice_in_dim(col_blocks, c * half, half, 0)
    sent = lax.ppermute(dot_t(row_blocks, theirs).astype(BF16), "c", [(0, 1), (1, 0)])
    terms = (dot_t(row_blocks, mine) + sent.astype(F32)).astype(BF16)
    update = lax.psum_scatter(terms, "z", scatter_dimension=0, tiled=True)

    one = lax.ppermute(lead, "x", [(0, 1), (1, 0)])
    two = lax.ppermute(lead, "x", [(0, 2), (1, 3)])
    three = lax.ppermute(lead, "x", [(0, 3), (1, 2)])
    lead0 = jnp.where(x == 0, lead, jnp.where(x == 1, one, jnp.where(x == 2, two, three)))
    lead1 = jnp.where(x == 1, lead, jnp.where(x == 0, one, jnp.where(x == 3, two, three)))
    base = jnp.concatenate([lead0, lead1, separator], axis=1)
    base = jnp.where((z == 0) & (c == 0), base, jnp.zeros_like(base))
    part = base - dot_t(first, jnp.concatenate([first, own], axis=0))
    pieces = lax.all_to_all(part.reshape(Z * C, width // (Z * C), 3 * rows), ("z", "c"), 0, 0, tiled=True)
    top = lax.all_gather(jnp.sum(pieces, axis=0), ("z", "c"), axis=0, tiled=True)
    top_own = top[:, width:]

    def flip(t):
        pairs = []
        for zs in range(Z):
            for cs in range(C):
                for ys in range(Y):
                    for xs in range(X):
                        src = ((zs * C + cs) * Y + ys) * X + xs
                        dst = ((ys * C + xs // 2) * Y + zs) * X + 2 * cs + ((xs % 2) ^ t)
                        pairs.append((src, dst))
        return lax.ppermute(top_own, ("z", "c", "y", "x"), pairs)

    straight, crossed = flip(0), flip(1)
    top_rows = jnp.concatenate(
        [jnp.where(even, straight, crossed), jnp.where(even, crossed, straight)], axis=1
    )

    lead_block = top[:, :width]
    factor = jnp.linalg.cholesky((lead_block + lead_block.T) * 0.5)
    level = jax.scipy.linalg.solve_triangular(
        factor, jnp.concatenate([top_own, top_rows], axis=1), lower=True
    ).astype(BF16)
    level_own = level[:, :rows]
    level_rows = level[:, rows:]

    def place(t):
        pairs = []
        for cs in range(C):
            for xs in range(X):
                pairs.append((cs * X + xs, (xs // 2) * X + 2 * cs + ((xs % 2) ^ t)))
        which = (x % 2) ^ t
        block = lax.dynamic_slice_in_dim(update, which * rows, rows, 1)
        return lax.ppermute(block, ("c", "x"), pairs)

    near, far = place(0), place(1)
    update_own = jnp.concatenate(
        [jnp.where(even, near, far), jnp.where(even, far, near)], axis=0
    ).astype(F32)

    schur = separator - update_own
    outer = lax.dot_general(
        level_rows, level_own, (((0,), (0,)), ((), ())), preferred_element_type=F32
    )
    keep = ((z > 0) | (c > 0)) & ((y > 0) | (x > 1))
    schur_next = jnp.where(keep, schur - outer, jnp.float32(0.0))
    return (panels, level_own, schur_next)


def solution(mesh):
    fine = Mesh(mesh.devices.reshape(Z, C, Y, X), ("z", "c", "y", "x"))
    grp, rd = ("z", "c"), ("y", "x")
    return jax.shard_map(
        body,
        mesh=fine,
        in_specs=(
            P(grp, rd, None),
            P(grp, None, None),
            P(grp, None),
            P(grp),
            P(grp, rd),
        ),
        out_specs=(P(grp, rd, None), P(None, rd), P(grp, rd)),
        check_vma=False,
    )
```

time: 458 us -> 225 us (0.49)
  the two profiles are of different devices: /device:TPU:1 before, /device:TPU:33 now
where the time goes in v1:
time: 225 us; the launch traced here: 224 us
  starting transfers between devices  58.2 us (26%)
  waiting for transfers between devices  57.9 us (26%)
  other arithmetic  55.8 us (25%)
  between operations  17.2 us (8%)
  blocking collectives  15.6 us (7%)
  local copies, waits for them, and re-layouts  10.2 us (5%)
  matrix products  8.69 us (4%)
    another operation x6, other arithmetic, body(): factor = jnp.linalg.cholesky((lead_block + lead_block.T) * 0.5)  34 us
    all_to_all x2, waiting for transfers between devices, share(): return lax.all_to_all(copies, axis, 0, 0, tiled=True)  20.5 us
    another operation x3, other arithmetic, body(): jax.scipy.linalg.solve_triangular(factor, jnp.concatenate([top_own, top_r...  19.7 us
    all_gather x1, waiting for transfers between devices, body(): lead = lax.all_gather(separator, 'y', axis=0)[0]  17.9 us
    ppermute x2, starting transfers between devices, flip(): return lax.ppermute(top_own, ('z', 'c', 'y', 'x'), pairs)  16.3 us
    all_gather x1, blocking collectives, body(): lax.all_gather(jnp.sum(pieces, axis=0), ('z', 'c'), axis=0, tiled=True)  15.6 us
    all_to_all x1, waiting for transfers between devices, body(): lax.all_to_all(part.reshape(Z * C, width // (Z * C), 3 * rows), ('z', 'c'...  12.1 us
    all_to_all x2, starting transfers between devices, share(): return lax.all_to_all(copies, axis, 0, 0, tiled=True)  10.2 us
  transfers between devices with their start and end apart: 13, of which 5 were waited for; matrix products, arithmetic and copies ran while one was open for 30% of the time, Pallas kernels for 0%

profile of v1, /device:TPU:33, one launch (start us, length us, event | category | flops | bytes accessed | tf_op | source)
XLA Modules:
  0.0 223.8 jit_solution(11328110900024553742)
XLA Ops:
  8.0 0.0 copy-start
  8.0 0.7 copy-done.6
  8.7 0.1 compare_convert_fusion
  8.8 0.7 copy-done.5
  9.5 0.2 fusion.26
  9.7 1.6 fusion.1
  11.3 0.0 copy-start.1
  11.3 0.6 copy-done.1
  12.0 1.1 broadcast_in_dim.11
  13.0 6.6 %all-to-all-start = ((bf16[8,128,512]{2,1,0:T(8,128)(2,1)}), bf16[8,128,512]{2,1,0:T(8,128)(2,1)S(1)}, u32[]{:S(2)}, u32[]{:S(2)}) async-start(bf16[8,128,512]{2,1,0:T(8,128)(2,1)} %broadcast_in_dim.11), calls=%async_computation | async-start | bytes 2097152 | tf_op jit(solution)/shard_map/all_to_all | solution.py:18
  19.7 0.7 all-gather.3.cloned.1.call-update
  20.4 20.5 %all-to-all-done = bf16[8,128,512]{2,1,0:T(8,128)(2,1)S(1)} async-done(((bf16[8,128,512]{2,1,0:T(8,128)(2,1)}), bf16[8,128,512]{2,1,0:T(8,128)(2,1)S(1)}, u32[]{:S(2)}, u32[]{:S(2)}) %all-to-all-start) | async-done | bytes 1048608 | tf_op jit(solution)/shard_map/all_to_all | solution.py:18
  40.9 1.1 broadcast_in_dim.12
  42.0 3.5 %all-to-all-start.1 = ((bf16[4,2,128,512]{3,2,1,0:T(8,128)(2,1)}), bf16[4,2,128,512]{3,2,1,0:T(8,128)(2,1)S(1)}, u32[]{:S(2)}, u32[]{:S(2)}) async-start(bf16[4,2,128,512]{3,2,1,0:T(8,128)(2,1)} %broadcast_in_dim.12), calls=%async_computation.1 | async-start | bytes 2097152 | tf_op jit(solution)/shard_map/all_to_all | solution.py:18
  45.5 17.9 %all-gather.3.cloned.1.call-done = f32[2048,128]{1,0:T(8,128)} async-done(((f32[256,128]{1,0:T(8,128)}), f32[2048,128]{1,0:T(8,128)}) %all-gather.3.cloned.1.call-update) | async-done | bytes 1048592 | tf_op jit(solution)/shard_map/all_gather | solution.py:26
  63.5 0.9 slice.99
  64.4 4.7 %collective-permute-start.1 = (f32[256,128]{1,0:T(8,128)S(1)}, f32[256,128]{1,0:T(8,128)S(1)}, u32[]{:S(2)}, u32[]{:S(2)}) collective-permute-start(f32[256,128]{1,0:T(8,128)S(1)} %slice.99), channel_id=1, source_target_pairs={{0,2},{1,3},{4,6},{5,7},{8,10},{9,11},{12,14},{13,15},{16,18},{17,... | collective-permute-start | bytes 393224 | tf_op jit(solution)/shard_map/ppermute | solution.py:50
  69.1 2.2 collective-permute-start
  71.3 1.3 collective-permute-start.2
  72.7 0.0 collective-permute-done.1
  72.7 2.2 collective-permute-done
  74.8 0.0 collective-permute-done.2
  74.8 1.6 select_select_fusion.2
  76.4 0.0 all-to-all-done.1
  76.5 1.3 convolution_convert_fusion
  77.7 7.8 %collective-permute-start.5 = (bf16[1024,256]{1,0:T(8,128)(2,1)}, bf16[1024,256]{1,0:T(8,128)(2,1)}, u32[]{:S(2)}, u32[]{:S(2)}) collective-permute-start(bf16[1024,256]{1,0:T(8,128)(2,1)} %convolution_convert_fusion), channel_id=1, source_target_pairs={{0,32},{32,0},{1,33},{33,1},{2,34},{34,2},{3,35},{35,3},{4,36},{36... | collective-permute-start | bytes 1572872 | tf_op jit(solution)/shard_map/ppermute | solution.py:45
  85.6 1.1 convolution_subtract_fusion
  86.7 8.3 %all-to-all-start.2 = ((f32[16,16,384]{2,1,0:T(8,128)}), f32[16,16,384]{2,1,0:T(8,128)S(1)}, u32[]{:S(2)}, u32[]{:S(2)}) async-start(f32[16,16,384]{2,1,0:T(8,128)} %bitcast.4), calls=%async_computation.2 | async-start | bytes 786432 | tf_op jit(solution)/shard_map/all_to_all | solution.py:57
  95.1 0.0 reduce-scatter.2.cloned.1.call-start
  95.2 0.0 collective-permute-done.5
  95.2 2.3 %add_convert_fusion = bf16[1024,256]{1,0:T(8,128)(2,1)} fusion(bf16[1024,256]{1,0:T(8,128)(2,1)} %collective-permute-done.5, bf16[1024,512]{1,0:T(8,128)(2,1)S(1)} %bitcast.53, bf16[512,512]{1,0:T(8,128)(2,1)S(1)} %bitcast.55, s32[]{:T(128)S(6)} %select_n.127), kind=kOutput, calls=%fused_computation.9 | convolution fusion | flops 269221888 | bytes 2359300 | tf_op jit(solution)/shard_map/dot_general | solution.py:13
  97.5 0.0 reduce-scatter.2.cloned.1.call-update
  97.5 12.1 %all-to-all-done.2 = f32[16,16,384]{2,1,0:T(8,128)S(1)} async-done(((f32[16,16,384]{2,1,0:T(8,128)}), f32[16,16,384]{2,1,0:T(8,128)S(1)}, u32[]{:S(2)}, u32[]{:S(2)}) %all-to-all-start.2) | async-done | bytes 393248 | tf_op jit(solution)/shard_map/all_to_all | solution.py:57
  109.6 15.6 %all_gather.11 = f32[256,384]{1,0:T(8,128)S(1)} all-gather(f32[16,384]{1,0:T(8,128)S(1)} %reduce_sum.9), channel_id=1, replica_groups=mesh['z'=8,'c'=2,'y'=8,'x'=4] {'z','c'}, dimensions={0}, use_global_device_ids=true | all-gather | bytes 417792 | tf_op jit(solution)/shard_map/all_gather | solution.py:58
  125.3 10.5 %collective-permute-start.4 = (f32[256,128]{1,0:T(8,128)S(1)}, f32[256,128]{1,0:T(8,128)S(1)}, u32[]{:S(2)}, u32[]{:S(2)}) collective-permute-start(f32[256,128]{1,0:T(8,128)S(1)} %slice.105), channel_id=1, source_target_pairs={{0,1},{1,0},{2,33},{3,32},{4,65},{5,64},{6,97},{7,96},{8,129},{9,1... | collective-permute-start | bytes 393224 | tf_op jit(solution)/shard_map/ppermute | solution.py:70
  135.8 5.9 %collective-permute-start.3 = (f32[256,128]{1,0:T(8,128)S(1)}, f32[256,128]{1,0:T(8,128)S(1)}, u32[]{:S(2)}, u32[]{:S(2)}) collective-permute-start(f32[256,128]{1,0:T(8,128)S(1)} %slice.105), channel_id=1, source_target_pairs={{0,0},{1,1},{2,32},{3,33},{4,64},{5,65},{6,96},{7,97},{8,128},{9,1... | collective-permute-start | bytes 393224 | tf_op jit(solution)/shard_map/ppermute | solution.py:70
  141.7 0.1 copy.13
  141.8 0.1 copy.12
  142.0 11.7 %cholesky.50 = f32[128,128]{1,0:T(8,128)S(1)} custom-call(f32[128,128]{1,0:T(8,128)S(1)} %cholesky.118), custom_call_target="Cholesky" | custom-call | tf_op jit(solution)/shard_map/jit(cholesky)/cholesky | solution.py:78
  153.8 9.8 %custom-call.15 = f32[1,128,128]{1,2,0:T(8,128)S(1)} custom-call(f32[1,128,128]{2,1,0:T(8,128)S(1)} %get-tuple-element.36), custom_call_target="InvertDiagBlocksLowerTriangular" | custom-call | tf_op jit(solution)/shard_map/jit(cholesky)/cholesky | solution.py:78
  163.6 0.2 constant_dynamic-update-slice_fusion
  163.8 0.3 convolution_subtract_fusion.1
  164.1 11.7 %cholesky.105 = f32[128,128]{1,0:T(8,128)S(1)} custom-call(f32[128,128]{1,0:T(8,128)S(1)} %convolution_subtract_fusion.1), custom_call_target="Cholesky" | custom-call | tf_op jit(solution)/shard_map/jit(cholesky)/cholesky | solution.py:78
  175.9 0.7 compare_reduce_fusion
  177.8 0.1 triangular_solve.57
  177.9 4.1 %while.1 = (s32[]{:T(128)}, f32[256,256]{1,0:T(8,128)S(1)}, s32[2,2]{1,0:T(2,128)S(1)}, f32[2,128,128]{2,1,0:T(8,128)S(1)}, s32[]{:T(128)}) while((s32[]{:T(128)}, f32[256,256]{1,0:T(8,128)S(1)}, s32[2,2]{1,0:T(2,128)S(1)}, f32[2,128,128]{2,1,0:T(8,128)S(1)}, s32[]{:T(128)}) %tuple.34), condition=%wide.while_cond, body=%wide.while_body.sunk | while | flops 2 | bytes 131189 | solution.py:79
  178.1 0.6 fusion.42
  178.7 1.3 bitcast_dynamic-update-slice_fusion.2
  180.0 0.6 fusion.42
  180.6 1.3 bitcast_dynamic-update-slice_fusion.2
  182.0 19.7 %custom-call.16 = f32[2,128,128]{1,2,0:T(8,128)S(1)} custom-call(f32[2,128,128]{2,1,0:T(8,128)S(1)} %get-tuple-element.10), custom_call_target="InvertDiagBlocksLowerTriangular" | custom-call | tf_op jit(solution)/shard_map/jit(_solve_triangular)/triangular_solve | solution.py:79
  201.7 0.0 collective-permute-done.4
  201.7 0.0 collective-permute-done.3
  201.8 0.4 fusion.31
  202.1 0.3 fusion.18
  202.5 0.4 convolution_convert_fusion.1
  202.8 0.0 reduce-scatter.2.cloned.1.call-done
  202.9 0.8 constant_dynamic-slice_fusion.2
  203.7 5.3 %collective-permute-start.6 = (bf16[128,128]{1,0:T(8,128)(2,1)S(1)}, bf16[128,128]{1,0:T(8,128)(2,1)S(1)}, u32[]{:S(2)}, u32[]{:S(2)}) collective-permute-start(bf16[128,128]{1,0:T(8,128)(2,1)S(1)} %get-tuple-element.31), channel_id=1, source_target_pairs={{0,0},{1,1},{2,32},{3,33},{32,2},{33,3},{34,34},{35,35},{4,4},{5,5... | collective-permute-start | bytes 98312 | tf_op jit(solution)/shard_map/ppermute | solution.py:92
  209.0 2.0 collective-permute-start.7
  211.0 0.0 copy-start.3
  211.0 0.0 collective-permute-done.6
  211.0 4.4 %collective-permute-done.7 = bf16[128,128]{1,0:T(8,128)(2,1)S(1)} collective-permute-done((bf16[128,128]{1,0:T(8,128)(2,1)S(1)}, bf16[128,128]{1,0:T(8,128)(2,1)S(1)}, u32[]{:S(2)}, u32[]{:S(2)}) %collective-permute-start.7) | collective-permute-done | bytes 32800 | tf_op jit(solution)/shard_map/ppermute | solution.py:92
  215.5 0.9 subtract_select_fusion
  (33 shorter events, 0.5 us)
Async XLA Ops:
  8.0 1.7 copy-start
  8.0 0.7 copy-start.6
  8.8 0.7 copy-start.5
  11.3 0.7 copy-start.1
  13.0 27.8 %all-to-all-start = ((bf16[8,128,512]{2,1,0:T(8,128)(2,1)}), bf16[8,128,512]{2,1,0:T(8,128)(2,1)S(1)}, u32[]{:S(2)}, u32[]{:S(2)}) async-start(bf16[8,128,512]{2,1,0:T(8,128)(2,1)} %broadcast_in_dim.11), calls=%async_computation | async-start | bytes 2097152 | tf_op jit(solution)/shard_map/all_to_all | solution.py:18
  19.7 43.8 %all-gather.3.cloned.1.call-start = ((), (), s32[]{:S(2)}) async-start(), calls=%async_computation.5 | async-start | bytes 1179648 | tf_op jit(solution)/shard_map/all_gather | solution.py:26
  42.0 34.4 %all-to-all-start.1 = ((bf16[4,2,128,512]{3,2,1,0:T(8,128)(2,1)}), bf16[4,2,128,512]{3,2,1,0:T(8,128)(2,1)S(1)}, u32[]{:S(2)}, u32[]{:S(2)}) async-start(bf16[4,2,128,512]{3,2,1,0:T(8,128)(2,1)} %broadcast_in_dim.12), calls=%async_computation.1 | async-start | bytes 2097152 | tf_op jit(solution)/shard_map/all_to_all | solution.py:18
  64.4 8.3 %collective-permute-start.1 = (f32[256,128]{1,0:T(8,128)S(1)}, f32[256,128]{1,0:T(8,128)S(1)}, u32[]{:S(2)}, u32[]{:S(2)}) collective-permute-start(f32[256,128]{1,0:T(8,128)S(1)} %slice.99), channel_id=1, source_target_pairs={{0,2},{1,3},{4,6},{5,7},{8,10},{9,11},{12,14},{13,15},{16,18},{17,... | collective-permute-start | bytes 393224 | tf_op jit(solution)/shard_map/ppermute | solution.py:50
  69.1 5.7 %collective-permute-start = (f32[256,128]{1,0:T(8,128)S(1)}, f32[256,128]{1,0:T(8,128)S(1)}, u32[]{:S(2)}, u32[]{:S(2)}) collective-permute-start(f32[256,128]{1,0:T(8,128)S(1)} %slice.99), channel_id=1, source_target_pairs={{0,1},{1,0},{4,5},{5,4},{8,9},{9,8},{12,13},{13,12},{16,17},{17,16... | collective-permute-start | bytes 393224 | tf_op jit(solution)/shard_map/ppermute | solution.py:49
  71.3 3.5 %collective-permute-start.2 = (f32[256,128]{1,0:T(8,128)S(1)}, f32[256,128]{1,0:T(8,128)S(1)}, u32[]{:S(2)}, u32[]{:S(2)}) collective-permute-start(f32[256,128]{1,0:T(8,128)S(1)} %slice.99), channel_id=1, source_target_pairs={{0,3},{1,2},{4,7},{5,6},{8,11},{9,10},{12,15},{13,14},{16,19},{17,... | collective-permute-start | bytes 393224 | tf_op jit(solution)/shard_map/ppermute | solution.py:51
  77.7 7.9 %copy-start.2 = (f32[256,128]{1,0:T(8,128)S(1)}, f32[256,128]{1,0:T(8,128)}, u32[]{:S(2)}) copy-start(f32[256,128]{1,0:T(8,128)} %param.9) | copy-start | bytes 393220
  77.7 7.9 %copy-start.4 = (f32[256,128]{1,0:T(8,128)S(1)}, f32[256,128]{1,0:T(8,128)}, u32[]{:S(2)}) copy-start(f32[256,128]{1,0:T(8,128)} %get-tuple-element.22) | copy-start | bytes 393220
  77.7 17.4 %collective-permute-start.5 = (bf16[1024,256]{1,0:T(8,128)(2,1)}, bf16[1024,256]{1,0:T(8,128)(2,1)}, u32[]{:S(2)}, u32[]{:S(2)}) collective-permute-start(bf16[1024,256]{1,0:T(8,128)(2,1)} %convolution_convert_fusion), channel_id=1, source_target_pairs={{0,32},{32,0},{1,33},{33,1},{2,34},{34,2},{3,35},{35,3},{4,36},{36... | collective-permute-start | bytes 1572872 | tf_op jit(solution)/shard_map/ppermute | solution.py:45
  86.7 22.9 %all-to-all-start.2 = ((f32[16,16,384]{2,1,0:T(8,128)}), f32[16,16,384]{2,1,0:T(8,128)S(1)}, u32[]{:S(2)}, u32[]{:S(2)}) async-start(f32[16,16,384]{2,1,0:T(8,128)} %bitcast.4), calls=%async_computation.2 | async-start | bytes 786432 | tf_op jit(solution)/shard_map/all_to_all | solution.py:57
  95.1 107.8 %reduce-scatter.2.cloned.1.call-start = ((), (), s32[]{:S(2)}) async-start(), calls=%async_computation.4 | async-start | bytes 589824 | tf_op jit(solution)/shard_map/reduce_scatter | solution.py:47
  125.3 76.4 %collective-permute-start.4 = (f32[256,128]{1,0:T(8,128)S(1)}, f32[256,128]{1,0:T(8,128)S(1)}, u32[]{:S(2)}, u32[]{:S(2)}) collective-permute-start(f32[256,128]{1,0:T(8,128)S(1)} %slice.105), channel_id=1, source_target_pairs={{0,1},{1,0},{2,33},{3,32},{4,65},{5,64},{6,97},{7,96},{8,129},{9,1... | collective-permute-start | bytes 393224 | tf_op jit(solution)/shard_map/ppermute | solution.py:70
  135.8 65.9 %collective-permute-start.3 = (f32[256,128]{1,0:T(8,128)S(1)}, f32[256,128]{1,0:T(8,128)S(1)}, u32[]{:S(2)}, u32[]{:S(2)}) collective-permute-start(f32[256,128]{1,0:T(8,128)S(1)} %slice.105), channel_id=1, source_target_pairs={{0,0},{1,1},{2,32},{3,33},{4,64},{5,65},{6,96},{7,97},{8,128},{9,1... | collective-permute-start | bytes 393224 | tf_op jit(solution)/shard_map/ppermute | solution.py:70
  203.7 7.3 %collective-permute-start.6 = (bf16[128,128]{1,0:T(8,128)(2,1)S(1)}, bf16[128,128]{1,0:T(8,128)(2,1)S(1)}, u32[]{:S(2)}, u32[]{:S(2)}) collective-permute-start(bf16[128,128]{1,0:T(8,128)(2,1)S(1)} %get-tuple-element.31), channel_id=1, source_target_pairs={{0,0},{1,1},{2,32},{3,33},{32,2},{33,3},{34,34},{35,35},{4,4},{5,5... | collective-permute-start | bytes 98312 | tf_op jit(solution)/shard_map/ppermute | solution.py:92
  209.0 6.4 %collective-permute-start.7 = (bf16[128,128]{1,0:T(8,128)(2,1)S(1)}, bf16[128,128]{1,0:T(8,128)(2,1)S(1)}, u32[]{:S(2)}, u32[]{:S(2)}) collective-permute-start(bf16[128,128]{1,0:T(8,128)(2,1)S(1)} %get-tuple-element.32), channel_id=1, source_target_pairs={{0,1},{1,0},{2,33},{3,32},{32,3},{33,2},{34,35},{35,34},{4,5},{5,4... | collective-permute-start | bytes 98312 | tf_op jit(solution)/shard_map/ppermute | solution.py:92
  211.0 4.5 %copy-start.3 = (bf16[256,128]{1,0:T(8,128)(2,1)}, bf16[256,128]{1,0:T(8,128)(2,1)S(1)}, u32[]{:S(2)}) copy-start(bf16[256,128]{1,0:T(8,128)(2,1)S(1)} %pad_maximum_fusion.5) | copy-start | bytes 196612
Sparse Core Ops, SparseCore 0:
  22.6 40.8 all-gather.2
Sparse Core Ops, SparseCore 1:
  98.3 36.8 reduce-scatter.1

commit v2 on v1

--- a/solution.py
+++ b/solution.py
@@ -1,12 +1,15 @@
 import jax
 import jax.numpy as jnp
 from jax import lax
+from jax.experimental import pallas as pl
+from jax.experimental.pallas import tpu as pltpu
 from jax.sharding import Mesh, PartitionSpec as P
 
 Z, C, Y, X = 8, 2, 8, 4
 HI = lax.Precision.HIGHEST
 F32 = jnp.float32
 BF16 = jnp.bfloat16
+BLOCK, LANES, SUB = 64, 128, 8
 
 
 def dot_t(a, b, out=F32):
@@ -18,12 +21,80 @@
     return lax.all_to_all(copies, axis, 0, 0, tiled=True)
 
 
+def lane(tile, k):
+    return jnp.broadcast_to(tile[:, k:k + 1], tile.shape)
+
+def sub(tile, s):
+    return jnp.broadcast_to(tile[s:s + 1, :], tile.shape)
+
+def block_inverse(block):
+    n = BLOCK
+    rowid = lax.broadcasted_iota(jnp.int32, (SUB, LANES), 0)
+    laneid = lax.broadcasted_iota(jnp.int32, (SUB, LANES), 1)
+    wide = jnp.concatenate([block, jnp.zeros((n, LANES - n), F32)], axis=1)
+    tiles = []
+    for t in range(n // SUB):
+        unit = jnp.where(laneid == rowid + (n + t * SUB), 1.0, 0.0).astype(F32)
+        tiles.append(wide[t * SUB:(t + 1) * SUB, :] + unit)
+    out = [None] * len(tiles)
+    for t in range(len(tiles)):
+        acc = jnp.zeros((SUB, LANES), F32)
+        for s in range(0, SUB, 2):
+            k = t * SUB + s
+            r1, r2 = sub(tiles[t], s), sub(tiles[t], s + 1)
+            a, b, d = lane(r1, k), lane(r1, k + 1), lane(r2, k + 1)
+            inv = 1.0 / (a * d - b * b)
+            q1 = (d * r1 - b * r2) * inv
+            q2 = (a * r2 - b * r1) * inv
+            for u in range(t, len(tiles)):
+                c1, c2 = lane(tiles[u], k), lane(tiles[u], k + 1)
+                new = tiles[u] - (c1 * q1 + c2 * q2)
+                tiles[u] = jnp.where(rowid > s + 1, new, tiles[u]) if u == t else new
+            ratio = b / a
+            acc = jnp.where(rowid == s, r1 * lax.rsqrt(a), acc)
+            acc = jnp.where(rowid == s + 1, (r2 - ratio * r1) * lax.rsqrt(d - ratio * b), acc)
+        out[t] = acc
+    return jnp.concatenate(out, axis=0)[:, n:]
+
+def kernel(a_ref, w_ref, aug):
+    n = a_ref.shape[0]
+    a = a_ref[...]
+    a = a * 0.5 + a.T * 0.5
+    ri = lax.broadcasted_iota(jnp.int32, (n, n), 0)
+    ci = lax.broadcasted_iota(jnp.int32, (n, n), 1)
+    diag = jnp.where(ri == ci, a, 0.0)
+    s_row = lax.rsqrt(jnp.sum(diag, axis=0, keepdims=True))
+    s_col = lax.rsqrt(jnp.sum(diag, axis=1, keepdims=True))
+    aug[:, :n] = a * s_col * s_row
+    aug[:, n:] = jnp.where(ri == ci, 1.0, 0.0)
+    for k in range(0, n, BLOCK):
+        rows = aug[k:k + BLOCK, :]
+        inv = block_inverse(rows[:, k:k + BLOCK])
+        u = jnp.dot(inv, rows, precision=HI, preferred_element_type=F32)
+        w_ref[k:k + BLOCK, :] = u[:, n:] * s_row
+        for m in range(k + BLOCK, n, BLOCK):
+            aug[m:m + BLOCK, :] = aug[m:m + BLOCK, :] - lax.dot_general(
+                u[:, m:m + BLOCK], u, (((0,), (0,)), ((), ())), precision=HI, preferred_element_type=F32)
+
+def inverse_factor(a):
+    n=a.shape[0]
+    return pl.pallas_call(kernel, out_shape=jax.ShapeDtypeStruct((n,n),F32),
+        in_specs=[pl.BlockSpec(memory_space=pltpu.VMEM)], out_specs=pl.BlockSpec(memory_space=pltpu.VMEM),
+        scratch_shapes=[pltpu.VMEM((n,2*n),F32)],
+        compiler_params=pltpu.CompilerParams(vmem_limit_bytes=32 * 1024 * 1024),
+        name="inverse_factor",
+    )(a)
+
+
 def body(leaf_rows, leaf_inverse, block_pattern, leaf_widths, separator):
     count, rows, width = leaf_rows.shape
     z, c, y, x = (lax.axis_index(a) for a in ("z", "c", "y", "x"))
     even = x % 2 == 0
 
-    lead = lax.all_gather(separator, "y", axis=0)[0]
+    slab = width // (Z * C)
+    base_own = lax.all_to_all(separator, ("z", "c"), 0, 0, tiled=True)[:slab]
+    lead = share(base_own, ("y", "x"), Y * X)
+    base = jnp.concatenate([lead[0], lead[1], base_own], axis=1)
 
     product = jnp.einsum("jib,jcb->jic", leaf_rows, leaf_inverse, precision=HI)
     row_mask = lax.dynamic_slice_in_dim(block_pattern, 2 * y + x // 2, 1, 1).astype(F32)
@@ -44,18 +115,13 @@
     mine = lax.dynamic_slice_in_dim(col_blocks, c * half, half, 0)
     sent = lax.ppermute(dot_t(row_blocks, theirs).astype(BF16), "c", [(0, 1), (1, 0)])
     terms = (dot_t(row_blocks, mine) + sent.astype(F32)).astype(BF16)
-    update = lax.psum_scatter(terms, "z", scatter_dimension=0, tiled=True)
 
-    one = lax.ppermute(lead, "x", [(0, 1), (1, 0)])
-    two = lax.ppermute(lead, "x", [(0, 2), (1, 3)])
-    three = lax.ppermute(lead, "x", [(0, 3), (1, 2)])
-    lead0 = jnp.where(x == 0, lead, jnp.where(x == 1, one, jnp.where(x == 2, two, three)))
-    lead1 = jnp.where(x == 1, lead, jnp.where(x == 0, one, jnp.where(x == 3, two, three)))
-    base = jnp.concatenate([lead0, lead1, separator], axis=1)
-    base = jnp.where((z == 0) & (c == 0), base, jnp.zeros_like(base))
-    part = base - dot_t(first, jnp.concatenate([first, own], axis=0))
-    pieces = lax.all_to_all(part.reshape(Z * C, width // (Z * C), 3 * rows), ("z", "c"), 0, 0, tiled=True)
-    top = lax.all_gather(jnp.sum(pieces, axis=0), ("z", "c"), axis=0, tiled=True)
+    part = dot_t(first, jnp.concatenate([first, own], axis=0))
+    pieces = lax.all_to_all(part.reshape(Z * C, slab, 3 * rows), ("z", "c"), 0, 0, tiled=True)
+    top, terms = lax.optimization_barrier((base - jnp.sum(pieces, axis=0), terms))
+    terms = lax.all_to_all(terms.reshape(Z, rows, half), "z", 0, 0, tiled=True)
+    update = jnp.sum(terms.astype(F32), axis=0)
+    top = lax.all_gather(top, ("z", "c"), axis=0, tiled=True)
     top_own = top[:, width:]
 
     def flip(t):
@@ -74,11 +140,8 @@
         [jnp.where(even, straight, crossed), jnp.where(even, crossed, straight)], axis=1
     )
 
-    lead_block = top[:, :width]
-    factor = jnp.linalg.cholesky((lead_block + lead_block.T) * 0.5)
-    level = jax.scipy.linalg.solve_triangular(
-        factor, jnp.concatenate([top_own, top_rows], axis=1), lower=True
-    ).astype(BF16)
+    inverse = inverse_factor(top[:, :width])
+    level = jnp.dot(inverse, jnp.concatenate([top_own, top_rows], axis=1), precision=HI).astype(BF16)
     level_own = level[:, :rows]
     level_rows = level[:, rows:]
 
@@ -94,7 +157,7 @@
     near, far = place(0), place(1)
     update_own = jnp.concatenate(
         [jnp.where(even, near, far), jnp.where(even, far, near)], axis=0
-    ).astype(F32)
+    )
 
     schur = separator - update_own
     outer = lax.dot_general(

time: 225 us -> 192 us (0.85)
  the two profiles are of different devices: /device:TPU:33 before, /device:TPU:257 now
where the time goes in v2:
time: 192 us; the launch traced here: 191 us
  starting transfers between devices  63.9 us (33%)
  blocking collectives  59.6 us (31%)
  waiting for transfers between devices  33.4 us (17%)
  Pallas kernels  20 us (10%)
  matrix products  8.68 us (5%)
  local copies, waits for them, and re-layouts  4.03 us (2%)
    all_to_all x1, blocking collectives, share(): return lax.all_to_all(copies, axis, 0, 0, tiled=True)  33.9 us
    all_gather x1, blocking collectives, body(): top = lax.all_gather(top, ('z', 'c'), axis=0, tiled=True)  25.8 us
    pallas_call x1, Pallas kernels, inverse_factor(): pl.pallas_call(kernel, out_shape=jax.ShapeDtypeStruct((n, n), F32), in_sp...  20 us
    all_to_all x2, waiting for transfers between devices, share(): return lax.all_to_all(copies, axis, 0, 0, tiled=True)  19 us
    ppermute x2, starting transfers between devices, flip(): return lax.ppermute(top_own, ('z', 'c', 'y', 'x'), pairs)  15.7 us
    all_to_all x1, starting transfers between devices, body(): lax.all_to_all(part.reshape(Z * C, slab, 3 * rows), ('z', 'c'), 0, 0, til...  12.5 us
    all_to_all x1, starting transfers between devices, body(): base_own = lax.all_to_all(separator, ('z', 'c'), 0, 0, tiled=True)[:slab]  9.34 us
    all_to_all x1, starting transfers between devices, body(): terms = lax.all_to_all(terms.reshape(Z, rows, half), 'z', 0, 0, tiled=True)  7.88 us
  transfers between devices with their start and end apart: 10, of which 5 were waited for; matrix products, arithmetic and copies ran while one was open for 3% of the time, Pallas kernels for 10%

profile of v2, /device:TPU:257, one launch (start us, length us, event | category | flops | bytes accessed | tf_op | source)
XLA Modules:
  0.0 191.1 jit_solution(10409061914400143063)
XLA Ops:
  0.6 0.0 copy-start
  0.7 0.0 copy-start.4
  0.7 0.7 copy-done.4
  1.4 0.1 compare_convert_fusion
  1.4 0.0 copy-start.3
  1.4 0.7 copy-done.3
  2.1 0.2 fusion.24
  2.3 0.0 copy-done
  2.3 1.6 fusion.1
  3.9 0.0 copy-start.1
  3.9 0.6 copy-done.1
  4.6 0.1 broadcast_in_dim.13
  4.7 33.9 %all_to_all.34 = bf16[8,128,512]{2,1,0:T(8,128)(2,1)S(1)} all-to-all(bf16[8,128,512]{2,1,0:T(8,128)(2,1)S(1)} %broadcast_in_dim.13), channel_id=1, replica_groups=mesh['z'=8,'c'=2,'y'=8,'x'=4] {'y'}, dimensions={0} | all-to-all | bytes 2097152 | tf_op jit(solution)/shard_map/all_to_all | solution.py:21
  38.5 9.3 %all-to-all-start = ((f32[16,16,128]{2,1,0:T(8,128)}), f32[16,16,128]{2,1,0:T(8,128)S(1)}, u32[]{:S(2)}, u32[]{:S(2)}) async-start(f32[16,16,128]{2,1,0:T(8,128)} %bitcast), calls=%async_computation | async-start | bytes 262144 | tf_op jit(solution)/shard_map/all_to_all | solution.py:95
  47.9 4.5 %all-to-all-done = f32[16,16,128]{2,1,0:T(8,128)S(1)} async-done(((f32[16,16,128]{2,1,0:T(8,128)}), f32[16,16,128]{2,1,0:T(8,128)S(1)}, u32[]{:S(2)}, u32[]{:S(2)}) %all-to-all-start) | async-done | bytes 131104 | tf_op jit(solution)/shard_map/all_to_all | solution.py:95
  52.4 1.1 broadcast_in_dim.14
  53.5 4.0 %all-to-all-start.3 = ((bf16[4,2,128,512]{3,2,1,0:T(8,128)(2,1)}), bf16[4,2,128,512]{3,2,1,0:T(8,128)(2,1)S(1)}, u32[]{:S(2)}, u32[]{:S(2)}) async-start(bf16[4,2,128,512]{3,2,1,0:T(8,128)(2,1)} %broadcast_in_dim.14), calls=%async_computation.3 | async-start | bytes 2097152 | tf_op jit(solution)/shard_map/all_to_all | solution.py:21
  57.5 14.5 %all-to-all-done.3 = bf16[4,2,128,512]{3,2,1,0:T(8,128)(2,1)S(1)} async-done(((bf16[4,2,128,512]{3,2,1,0:T(8,128)(2,1)}), bf16[4,2,128,512]{3,2,1,0:T(8,128)(2,1)S(1)}, u32[]{:S(2)}, u32[]{:S(2)}) %all-to-all-start.3) | async-done | bytes 1048608 | tf_op jit(solution)/shard_map/all_to_all | solution.py:21
  72.0 0.7 broadcast_in_dim.12
  72.7 3.9 %all-to-all-start.1 = ((f32[32,16,128]{2,1,0:T(8,128)}), f32[32,16,128]{2,1,0:T(8,128)S(1)}, u32[]{:S(2)}, u32[]{:S(2)}) async-start(f32[32,16,128]{2,1,0:T(8,128)} %broadcast_in_dim.12), calls=%async_computation.1 | async-start | bytes 524288 | tf_op jit(solution)/shard_map/all_to_all | solution.py:21
  76.6 1.3 convolution_convert_fusion
  77.9 3.4 %collective-permute-start = (bf16[1024,256]{1,0:T(8,128)(2,1)}, bf16[1024,256]{1,0:T(8,128)(2,1)}, u32[]{:S(2)}, u32[]{:S(2)}) collective-permute-start(bf16[1024,256]{1,0:T(8,128)(2,1)} %convolution_convert_fusion), channel_id=1, source_target_pairs={{0,32},{32,0},{1,33},{33,1},{2,34},{34,2},{3,35},{35,3},{4,36},{36... | collective-permute-start | bytes 1572872 | tf_op jit(solution)/shard_map/ppermute | solution.py:116
  81.4 1.1 fusion.2
  82.5 4.5 %all-to-all-done.1 = f32[32,16,128]{2,1,0:T(8,128)S(1)} async-done(((f32[32,16,128]{2,1,0:T(8,128)}), f32[32,16,128]{2,1,0:T(8,128)S(1)}, u32[]{:S(2)}, u32[]{:S(2)}) %all-to-all-start.1) | async-done | bytes 262176 | tf_op jit(solution)/shard_map/all_to_all | solution.py:21
  87.0 12.5 %all-to-all-start.4 = ((f32[16,16,384]{2,1,0:T(8,128)}), f32[16,16,384]{2,1,0:T(8,128)S(1)}, u32[]{:S(2)}, u32[]{:S(2)}) async-start(f32[16,16,384]{2,1,0:T(8,128)} %fusion.2), calls=%async_computation.4 | async-start | bytes 786432 | tf_op jit(solution)/shard_map/all_to_all | solution.py:120
  99.5 0.0 collective-permute-done
  99.5 2.3 %add_convert_fusion = bf16[1024,256]{1,0:T(8,128)(2,1)} fusion(bf16[1024,256]{1,0:T(8,128)(2,1)} %collective-permute-done, bf16[1024,512]{1,0:T(8,128)(2,1)S(1)} %bitcast.29, bf16[512,512]{1,0:T(8,128)(2,1)S(1)} %bitcast.31, s32[]{:T(128)S(6)} %select_n.64), kind=kOutput, calls=%fused_computation.6 | convolution fusion | flops 269221888 | bytes 2359300 | tf_op jit(solution)/shard_map/dot_general | solution.py:16
  101.8 7.8 %all-to-all-done.4 = f32[16,16,384]{2,1,0:T(8,128)S(1)} async-done(((f32[16,16,384]{2,1,0:T(8,128)}), f32[16,16,384]{2,1,0:T(8,128)S(1)}, u32[]{:S(2)}, u32[]{:S(2)}) %all-to-all-start.4) | async-done | bytes 393248 | tf_op jit(solution)/shard_map/all_to_all | solution.py:120
  109.7 7.9 %all-to-all-start.5 = ((bf16[8,128,256]{2,1,0:T(8,128)(2,1)}), bf16[8,128,256]{2,1,0:T(8,128)(2,1)S(1)}, u32[]{:S(2)}, u32[]{:S(2)}) async-start(bf16[8,128,256]{2,1,0:T(8,128)(2,1)} %bitcast.12), calls=%async_computation.5 | async-start | bytes 1048576 | tf_op jit(solution)/shard_map/all_to_all | solution.py:122
  117.6 25.8 %all_gather.3 = f32[256,384]{1,0:T(8,128)S(1)} all-gather(f32[16,384]{1,0:T(8,128)S(1)} %maximum_subtract_fusion.1), channel_id=1, replica_groups=mesh['z'=8,'c'=2,'y'=8,'x'=4] {'z','c'}, dimensions={0}, use_global_device_ids=true | all-gather | bytes 417792 | tf_op jit(solution)/shard_map/all_gather | solution.py:124
  143.3 4.3 %collective-permute-start.1 = (f32[256,128]{1,0:T(8,128)S(1)}, f32[256,128]{1,0:T(8,128)S(1)}, u32[]{:S(2)}, u32[]{:S(2)}) collective-permute-start(f32[256,128]{1,0:T(8,128)S(1)} %slice.58), channel_id=1, source_target_pairs={{0,0},{1,1},{2,32},{3,33},{4,64},{5,65},{6,96},{7,97},{8,128},{9,1... | collective-permute-start | bytes 393224 | tf_op jit(solution)/shard_map/ppermute | solution.py:136
  147.7 11.3 %collective-permute-start.2 = (f32[256,128]{1,0:T(8,128)S(1)}, f32[256,128]{1,0:T(8,128)S(1)}, u32[]{:S(2)}, u32[]{:S(2)}) collective-permute-start(f32[256,128]{1,0:T(8,128)S(1)} %slice.58), channel_id=1, source_target_pairs={{0,1},{1,0},{2,33},{3,32},{4,65},{5,64},{6,97},{7,96},{8,129},{9,1... | collective-permute-start | bytes 393224 | tf_op jit(solution)/shard_map/ppermute | solution.py:136
  159.1 20.0 %inverse_factor.1 = f32[256,256]{1,0:T(8,128)S(1)} custom-call(f32[256,256]{1,0:T(8,128)S(1)} %slice.57.a_ref), custom_call_target="tpu_custom_call" | custom-call | tf_op jit(solution)/shard_map/inverse_factor/pallas_call | solution.py:81
  179.2 0.0 collective-permute-done.1
  179.2 0.0 collective-permute-done.2
  179.2 0.0 all-to-all-done.5
  179.2 0.1 convert_reduce_fusion
  179.3 3.1 %collective-permute-start.3 = (f32[128,128]{1,0:T(8,128)S(1)}, f32[128,128]{1,0:T(8,128)S(1)}, u32[]{:S(2)}, u32[]{:S(2)}) collective-permute-start(f32[128,128]{1,0:T(8,128)S(1)} %get-tuple-element.13), channel_id=1, source_target_pairs={{0,0},{1,1},{2,32},{3,33},{32,2},{33,3},{34,34},{35,35},{4,4},{5,5... | collective-permute-start | bytes 196616 | tf_op jit(solution)/shard_map/ppermute | solution.py:155
  182.5 4.0 %collective-permute-start.4 = (f32[128,128]{1,0:T(8,128)S(1)}, f32[128,128]{1,0:T(8,128)S(1)}, u32[]{:S(2)}, u32[]{:S(2)}) collective-permute-start(f32[128,128]{1,0:T(8,128)S(1)} %get-tuple-element.14), channel_id=1, source_target_pairs={{0,1},{1,0},{2,33},{3,32},{32,3},{33,2},{34,35},{35,34},{4,5},{5,4... | collective-permute-start | bytes 196616 | tf_op jit(solution)/shard_map/ppermute | solution.py:155
  186.5 0.6 convolution_convert_fusion.1
  187.1 0.0 copy-start.2
  187.1 0.0 collective-permute-done.3
  187.1 2.1 %collective-permute-done.4 = f32[128,128]{1,0:T(8,128)S(1)} collective-permute-done((f32[128,128]{1,0:T(8,128)S(1)}, f32[128,128]{1,0:T(8,128)S(1)}, u32[]{:S(2)}, u32[]{:S(2)}) %collective-permute-start.4) | collective-permute-done | bytes 65568 | tf_op jit(solution)/shard_map/ppermute | solution.py:155
  189.3 0.0 copy-done.2
  189.3 1.8 fusion.20
  (16 shorter events, 0.2 us)
Async XLA Ops:
  0.6 1.7 copy-start
  0.7 0.7 copy-start.4
  1.4 0.7 copy-start.3
  3.9 0.7 copy-start.1
  38.5 13.9 %all-to-all-start = ((f32[16,16,128]{2,1,0:T(8,128)}), f32[16,16,128]{2,1,0:T(8,128)S(1)}, u32[]{:S(2)}, u32[]{:S(2)}) async-start(f32[16,16,128]{2,1,0:T(8,128)} %bitcast), calls=%async_computation | async-start | bytes 262144 | tf_op jit(solution)/shard_map/all_to_all | solution.py:95
  53.5 18.5 %all-to-all-start.3 = ((bf16[4,2,128,512]{3,2,1,0:T(8,128)(2,1)}), bf16[4,2,128,512]{3,2,1,0:T(8,128)(2,1)S(1)}, u32[]{:S(2)}, u32[]{:S(2)}) async-start(bf16[4,2,128,512]{3,2,1,0:T(8,128)(2,1)} %broadcast_in_dim.14), calls=%async_computation.3 | async-start | bytes 2097152 | tf_op jit(solution)/shard_map/all_to_all | solution.py:21
  72.7 14.3 %all-to-all-start.1 = ((f32[32,16,128]{2,1,0:T(8,128)}), f32[32,16,128]{2,1,0:T(8,128)S(1)}, u32[]{:S(2)}, u32[]{:S(2)}) async-start(f32[32,16,128]{2,1,0:T(8,128)} %broadcast_in_dim.12), calls=%async_computation.1 | async-start | bytes 524288 | tf_op jit(solution)/shard_map/all_to_all | solution.py:21
  77.9 21.6 %collective-permute-start = (bf16[1024,256]{1,0:T(8,128)(2,1)}, bf16[1024,256]{1,0:T(8,128)(2,1)}, u32[]{:S(2)}, u32[]{:S(2)}) collective-permute-start(bf16[1024,256]{1,0:T(8,128)(2,1)} %convolution_convert_fusion), channel_id=1, source_target_pairs={{0,32},{32,0},{1,33},{33,1},{2,34},{34,2},{3,35},{35,3},{4,36},{36... | collective-permute-start | bytes 1572872 | tf_op jit(solution)/shard_map/ppermute | solution.py:116
  87.0 22.7 %all-to-all-start.4 = ((f32[16,16,384]{2,1,0:T(8,128)}), f32[16,16,384]{2,1,0:T(8,128)S(1)}, u32[]{:S(2)}, u32[]{:S(2)}) async-start(f32[16,16,384]{2,1,0:T(8,128)} %fusion.2), calls=%async_computation.4 | async-start | bytes 786432 | tf_op jit(solution)/shard_map/all_to_all | solution.py:120
  109.7 69.5 %all-to-all-start.5 = ((bf16[8,128,256]{2,1,0:T(8,128)(2,1)}), bf16[8,128,256]{2,1,0:T(8,128)(2,1)S(1)}, u32[]{:S(2)}, u32[]{:S(2)}) async-start(bf16[8,128,256]{2,1,0:T(8,128)(2,1)} %bitcast.12), calls=%async_computation.5 | async-start | bytes 1048576 | tf_op jit(solution)/shard_map/all_to_all | solution.py:122
  143.3 35.8 %collective-permute-start.1 = (f32[256,128]{1,0:T(8,128)S(1)}, f32[256,128]{1,0:T(8,128)S(1)}, u32[]{:S(2)}, u32[]{:S(2)}) collective-permute-start(f32[256,128]{1,0:T(8,128)S(1)} %slice.58), channel_id=1, source_target_pairs={{0,0},{1,1},{2,32},{3,33},{4,64},{5,65},{6,96},{7,97},{8,128},{9,1... | collective-permute-start | bytes 393224 | tf_op jit(solution)/shard_map/ppermute | solution.py:136
  147.7 31.5 %collective-permute-start.2 = (f32[256,128]{1,0:T(8,128)S(1)}, f32[256,128]{1,0:T(8,128)S(1)}, u32[]{:S(2)}, u32[]{:S(2)}) collective-permute-start(f32[256,128]{1,0:T(8,128)S(1)} %slice.58), channel_id=1, source_target_pairs={{0,1},{1,0},{2,33},{3,32},{4,65},{5,64},{6,97},{7,96},{8,129},{9,1... | collective-permute-start | bytes 393224 | tf_op jit(solution)/shard_map/ppermute | solution.py:136
  179.3 7.8 %collective-permute-start.3 = (f32[128,128]{1,0:T(8,128)S(1)}, f32[128,128]{1,0:T(8,128)S(1)}, u32[]{:S(2)}, u32[]{:S(2)}) collective-permute-start(f32[128,128]{1,0:T(8,128)S(1)} %get-tuple-element.13), channel_id=1, source_target_pairs={{0,0},{1,1},{2,32},{3,33},{32,2},{33,3},{34,34},{35,35},{4,4},{5,5... | collective-permute-start | bytes 196616 | tf_op jit(solution)/shard_map/ppermute | solution.py:155
  182.5 6.8 %collective-permute-start.4 = (f32[128,128]{1,0:T(8,128)S(1)}, f32[128,128]{1,0:T(8,128)S(1)}, u32[]{:S(2)}, u32[]{:S(2)}) collective-permute-start(f32[128,128]{1,0:T(8,128)S(1)} %get-tuple-element.14), channel_id=1, source_target_pairs={{0,1},{1,0},{2,33},{3,32},{32,3},{33,2},{34,35},{35,34},{4,5},{5,4... | collective-permute-start | bytes 196616 | tf_op jit(solution)/shard_map/ppermute | solution.py:155
  187.1 2.2 %copy-start.2 = (bf16[256,128]{1,0:T(8,128)(2,1)}, bf16[256,128]{1,0:T(8,128)(2,1)S(1)}, u32[]{:S(2)}) copy-start(bf16[256,128]{1,0:T(8,128)(2,1)S(1)} %slice.59) | copy-start | bytes 196612

commit v3 on v2

--- a/solution.py
+++ b/solution.py
@@ -56,7 +56,22 @@
         out[t] = acc
     return jnp.concatenate(out, axis=0)[:, n:]
 
-def kernel(a_ref, w_ref, aug):
+def eliminate(aug, w_ref, s_row, start):
+    n = aug.shape[1] // 2
+    count = aug.shape[0]
+    for k in range(0, w_ref.shape[0], BLOCK):
+        rows = aug[k:k + BLOCK, :]
+        inv = block_inverse(rows[:, start + k:start + k + BLOCK])
+        u = jnp.dot(inv, rows, precision=HI, preferred_element_type=F32)
+        w_ref[k:k + BLOCK, :] = u[:, n:] * s_row
+        for m in range(k + BLOCK, count, BLOCK):
+            left = u[:, start + m:start + m + BLOCK]
+            aug[m:m + BLOCK, :] = aug[m:m + BLOCK, :] - lax.dot_general(
+                left, u, (((0,), (0,)), ((), ())), precision=HI, preferred_element_type=F32
+            )
+
+
+def first_half(a_ref, w_ref, rest_ref, scale_ref, aug):
     n = a_ref.shape[0]
     a = a_ref[...]
     a = a * 0.5 + a.T * 0.5
@@ -67,23 +82,28 @@
     s_col = lax.rsqrt(jnp.sum(diag, axis=1, keepdims=True))
     aug[:, :n] = a * s_col * s_row
     aug[:, n:] = jnp.where(ri == ci, 1.0, 0.0)
-    for k in range(0, n, BLOCK):
-        rows = aug[k:k + BLOCK, :]
-        inv = block_inverse(rows[:, k:k + BLOCK])
-        u = jnp.dot(inv, rows, precision=HI, preferred_element_type=F32)
-        w_ref[k:k + BLOCK, :] = u[:, n:] * s_row
-        for m in range(k + BLOCK, n, BLOCK):
-            aug[m:m + BLOCK, :] = aug[m:m + BLOCK, :] - lax.dot_general(
-                u[:, m:m + BLOCK], u, (((0,), (0,)), ((), ())), precision=HI, preferred_element_type=F32)
-
-def inverse_factor(a):
-    n=a.shape[0]
-    return pl.pallas_call(kernel, out_shape=jax.ShapeDtypeStruct((n,n),F32),
-        in_specs=[pl.BlockSpec(memory_space=pltpu.VMEM)], out_specs=pl.BlockSpec(memory_space=pltpu.VMEM),
-        scratch_shapes=[pltpu.VMEM((n,2*n),F32)],
+    eliminate(aug, w_ref, s_row, 0)
+    rest_ref[...] = aug[n // 2:, :]
+    scale_ref[...] = jnp.broadcast_to(s_row, scale_ref.shape)
+
+
+def second_half(rest_ref, scale_ref, w_ref, aug):
+    aug[...] = rest_ref[...]
+    eliminate(aug, w_ref, scale_ref[:1, :], rest_ref.shape[0])
+
+
+def in_vmem(body, outs, scratch, name, *args):
+    spec = pl.BlockSpec(memory_space=pltpu.VMEM)
+    return pl.pallas_call(
+        body,
+        out_shape=[jax.ShapeDtypeStruct(shape, F32) for shape in outs],
+        in_specs=[spec] * len(args),
+        out_specs=[spec] * len(outs),
+        scratch_shapes=[pltpu.VMEM(scratch, F32)],
         compiler_params=pltpu.CompilerParams(vmem_limit_bytes=32 * 1024 * 1024),
-        name="inverse_factor",
-    )(a)
+        cost_estimate=pl.CostEstimate(flops=10**10, bytes_accessed=10**6, transcendentals=0),
+        name=name,
+    )(*args)
 
 
 def body(leaf_rows, leaf_inverse, block_pattern, leaf_widths, separator):
@@ -91,10 +111,20 @@
     z, c, y, x = (lax.axis_index(a) for a in ("z", "c", "y", "x"))
     even = x % 2 == 0
 
-    slab = width // (Z * C)
-    base_own = lax.all_to_all(separator, ("z", "c"), 0, 0, tiled=True)[:slab]
-    lead = share(base_own, ("y", "x"), Y * X)
-    base = jnp.concatenate([lead[0], lead[1], base_own], axis=1)
+    def move(array, steps):
+        pairs = [(X * ys + xs, X * yd + xd) for (ys, xs), (yd, xd) in steps]
+        return lax.ppermute(array, ("z", "c", "y", "x"), pairs)
+
+    lead = separator
+    for span in (4, 2, 1):
+        steps = [((ys, xs), (ys + span, xs)) for ys in range(0, Y, 2 * span) for xs in range(2)]
+        lead = jnp.where(y % (2 * span) == span, move(lead, steps), lead)
+    steps = [((ys, xs), (ys, xs + 2)) for ys in range(Y) for xs in range(2)]
+    lead = jnp.where(x >= 2, move(lead, steps), lead)
+    steps = [((ys, xs), (ys, xs ^ 1)) for ys in range(Y) for xs in range(X)]
+    beside = move(lead, steps)
+    base = jnp.concatenate([jnp.where(even, lead, beside), jnp.where(even, beside, lead), separator], axis=1)
+    base = jnp.where((z == 0) & (c == 0), base, jnp.zeros_like(base))
 
     product = jnp.einsum("jib,jcb->jic", leaf_rows, leaf_inverse, precision=HI)
     row_mask = lax.dynamic_slice_in_dim(block_pattern, 2 * y + x // 2, 1, 1).astype(F32)
@@ -116,13 +146,24 @@
     sent = lax.ppermute(dot_t(row_blocks, theirs).astype(BF16), "c", [(0, 1), (1, 0)])
     terms = (dot_t(row_blocks, mine) + sent.astype(F32)).astype(BF16)
 
-    part = dot_t(first, jnp.concatenate([first, own], axis=0))
+    update = lax.psum_scatter(terms, "z", scatter_dimension=0, tiled=True)
+
+    slab = width // (Z * C)
+    part = base - dot_t(first, jnp.concatenate([first, own], axis=0))
     pieces = lax.all_to_all(part.reshape(Z * C, slab, 3 * rows), ("z", "c"), 0, 0, tiled=True)
-    top, terms = lax.optimization_barrier((base - jnp.sum(pieces, axis=0), terms))
-    terms = lax.all_to_all(terms.reshape(Z, rows, half), "z", 0, 0, tiled=True)
-    update = jnp.sum(terms.astype(F32), axis=0)
-    top = lax.all_gather(top, ("z", "c"), axis=0, tiled=True)
+    top = lax.all_gather(jnp.sum(pieces, axis=0), ("z", "c"), axis=0, tiled=True)
     top_own = top[:, width:]
+
+    half_rows = width // 2
+    upper, rest, scale = in_vmem(
+        first_half, [(half_rows, width), (half_rows, 2 * width), (SUB, width)], (width, 2 * width),
+        "first_half", top[:, :width],
+    )
+    rest, top_own, update = lax.optimization_barrier((rest, top_own, update))
+    (lower,) = in_vmem(
+        second_half, [(half_rows, width)], (half_rows, 2 * width), "second_half", rest, scale
+    )
+    inverse = jnp.concatenate([upper, lower], axis=0)
 
     def flip(t):
         pairs = []
@@ -140,7 +181,6 @@
         [jnp.where(even, straight, crossed), jnp.where(even, crossed, straight)], axis=1
     )
 
-    inverse = inverse_factor(top[:, :width])
     level = jnp.dot(inverse, jnp.concatenate([top_own, top_rows], axis=1), precision=HI).astype(BF16)
     level_own = level[:, :rows]
     level_rows = level[:, rows:]
@@ -157,7 +197,7 @@
     near, far = place(0), place(1)
     update_own = jnp.concatenate(
         [jnp.where(even, near, far), jnp.where(even, far, near)], axis=0
-    )
+    ).astype(F32)
 
     schur = separator - update_own
     outer = lax.dot_general(

time: 192 us -> 170 us (0.89)
  the two profiles are of different devices: /device:TPU:257 before, /device:TPU:33 now
where the time goes in v3:
time: 170 us; the launch traced here: 169 us
  starting transfers between devices  62.7 us (37%)
  waiting for transfers between devices  42.1 us (25%)
  Pallas kernels  19.9 us (12%)
  blocking collectives  15.6 us (9%)
  between operations  14.5 us (9%)
  matrix products  7.76 us (5%)
  local copies, waits for them, and re-layouts  5.13 us (3%)
    all_to_all x2, waiting for transfers between devices, share(): return lax.all_to_all(copies, axis, 0, 0, tiled=True)  26.6 us
    pallas_call x2, Pallas kernels, in_vmem(): pl.pallas_call(body, out_shape=[jax.ShapeDtypeStruct(shape, F32) for shap...  19.9 us
    ppermute x1, starting transfers between devices, body(): lax.ppermute(dot_t(row_blocks, theirs).astype(BF16), 'c', [(0, 1), (1, 0)])  18.1 us
    ppermute x2, starting transfers between devices, flip(): return lax.ppermute(top_own, ('z', 'c', 'y', 'x'), pairs)  16.6 us
    all_gather x1, blocking collectives, body(): lax.all_gather(jnp.sum(pieces, axis=0), ('z', 'c'), axis=0, tiled=True)  15.6 us
    all_to_all x1, waiting for transfers between devices, body(): lax.all_to_all(part.reshape(Z * C, slab, 3 * rows), ('z', 'c'), 0, 0, til...  12 us
    ppermute x2, starting transfers between devices, place(): return lax.ppermute(block, ('c', 'x'), pairs)  10.9 us
    all_to_all x2, starting transfers between devices, share(): return lax.all_to_all(copies, axis, 0, 0, tiled=True)  10.3 us
  transfers between devices with their start and end apart: 14, of which 4 were waited for; matrix products, arithmetic and copies ran while one was open for 4% of the time, Pallas kernels for 12%

profile of v3, /device:TPU:33, one launch (start us, length us, event | category | flops | bytes accessed | tf_op | source)
XLA Modules:
  0.0 168.8 jit_solution(16796207066980250718)
XLA Ops:
  7.2 0.0 copy-start
  7.2 0.0 copy-start.7
  7.2 0.7 copy-done.7
  7.9 0.1 compare_convert_fusion
  8.0 0.0 copy-start.6
  8.0 0.7 copy-done.6
  8.7 0.2 fusion.29
  8.8 0.0 copy-done
  8.8 1.6 fusion.1
  10.4 0.0 copy-start.2
  10.5 0.6 copy-done.2
  11.1 1.1 broadcast_in_dim.10
  12.2 0.0 copy-start.1
  12.2 6.8 %all-to-all-start = ((bf16[8,128,512]{2,1,0:T(8,128)(2,1)}), bf16[8,128,512]{2,1,0:T(8,128)(2,1)S(1)}, u32[]{:S(2)}, u32[]{:S(2)}) async-start(bf16[8,128,512]{2,1,0:T(8,128)(2,1)} %broadcast_in_dim.10), calls=%async_computation | async-start | bytes 2097152 | tf_op jit(solution)/shard_map/all_to_all | solution.py:21
  19.0 0.0 copy-done.1
  19.0 0.7 collective-permute-start
  19.7 0.0 collective-permute-done
  19.7 0.7 collective-permute-start.1
  20.4 0.0 collective-permute-done.1
  20.4 0.7 collective-permute-start.2
  21.1 19.1 %all-to-all-done = bf16[8,128,512]{2,1,0:T(8,128)(2,1)S(1)} async-done(((bf16[8,128,512]{2,1,0:T(8,128)(2,1)}), bf16[8,128,512]{2,1,0:T(8,128)(2,1)S(1)}, u32[]{:S(2)}, u32[]{:S(2)}) %all-to-all-start) | async-done | bytes 1048608 | tf_op jit(solution)/shard_map/all_to_all | solution.py:21
  40.2 1.1 broadcast_in_dim.11
  41.3 3.5 %all-to-all-start.1 = ((bf16[4,2,128,512]{3,2,1,0:T(8,128)(2,1)}), bf16[4,2,128,512]{3,2,1,0:T(8,128)(2,1)S(1)}, u32[]{:S(2)}, u32[]{:S(2)}) async-start(bf16[4,2,128,512]{3,2,1,0:T(8,128)(2,1)} %broadcast_in_dim.11), calls=%async_computation.1 | async-start | bytes 2097152 | tf_op jit(solution)/shard_map/all_to_all | solution.py:21
  44.8 0.0 collective-permute-done.2
  44.9 0.7 collective-permute-start.3
  45.6 0.0 collective-permute-done.3
  45.6 0.7 collective-permute-start.4
  46.3 0.0 collective-permute-done.4
  46.3 0.7 broadcast_select_fusion.7
  47.0 7.5 %all-to-all-done.1 = bf16[4,2,128,512]{3,2,1,0:T(8,128)(2,1)S(1)} async-done(((bf16[4,2,128,512]{3,2,1,0:T(8,128)(2,1)}), bf16[4,2,128,512]{3,2,1,0:T(8,128)(2,1)S(1)}, u32[]{:S(2)}, u32[]{:S(2)}) %all-to-all-start.1) | async-done | bytes 1048608 | tf_op jit(solution)/shard_map/all_to_all | solution.py:21
  54.6 1.3 convolution_convert_fusion
  55.9 0.0 copy-start.4
  55.9 0.0 copy-start.5
  55.9 18.1 %collective-permute-start.5 = (bf16[1024,256]{1,0:T(8,128)(2,1)}, bf16[1024,256]{1,0:T(8,128)(2,1)}, u32[]{:S(2)}, u32[]{:S(2)}) collective-permute-start(bf16[1024,256]{1,0:T(8,128)(2,1)} %convolution_convert_fusion), channel_id=1, source_target_pairs={{0,32},{32,0},{1,33},{33,1},{2,34},{34,2},{3,35},{35,3},{4,36},{36... | collective-permute-start | bytes 1572872 | tf_op jit(solution)/shard_map/ppermute | solution.py:146
  74.0 0.0 copy-done.4
  74.0 0.0 copy-done.5
  74.0 1.1 fusion.2
  75.1 3.4 %all-to-all-start.2 = ((f32[16,16,384]{2,1,0:T(8,128)}), f32[16,16,384]{2,1,0:T(8,128)S(1)}, u32[]{:S(2)}, u32[]{:S(2)}) async-start(f32[16,16,384]{2,1,0:T(8,128)} %bitcast.4), calls=%async_computation.2 | async-start | bytes 786432 | tf_op jit(solution)/shard_map/all_to_all | solution.py:153
  78.5 0.0 reduce-scatter.2.cloned.1.call-start
  78.6 0.0 collective-permute-done.5
  78.6 2.3 %add_convert_fusion = bf16[1024,256]{1,0:T(8,128)(2,1)} fusion(bf16[1024,256]{1,0:T(8,128)(2,1)} %collective-permute-done.5, bf16[1024,512]{1,0:T(8,128)(2,1)S(1)} %bitcast.17, bf16[512,512]{1,0:T(8,128)(2,1)S(1)} %bitcast.19, s32[]{:T(128)S(6)} %select_n.133), kind=kOutput, calls=%fused_computation.5 | convolution fusion | flops 269221888 | bytes 2359300 | tf_op jit(solution)/shard_map/dot_general | solution.py:16
  80.9 0.0 reduce-scatter.2.cloned.1.call-update
  81.0 12.0 %all-to-all-done.2 = f32[16,16,384]{2,1,0:T(8,128)S(1)} async-done(((f32[16,16,384]{2,1,0:T(8,128)}), f32[16,16,384]{2,1,0:T(8,128)S(1)}, u32[]{:S(2)}, u32[]{:S(2)}) %all-to-all-start.2) | async-done | bytes 393248 | tf_op jit(solution)/shard_map/all_to_all | solution.py:153
  93.0 15.6 %all_gather.3 = f32[256,384]{1,0:T(8,128)S(1)} all-gather(f32[16,384]{1,0:T(8,128)S(1)} %reduce_sum.9), channel_id=1, replica_groups=mesh['z'=8,'c'=2,'y'=8,'x'=4] {'z','c'}, dimensions={0}, use_global_device_ids=true | all-gather | bytes 417792 | tf_op jit(solution)/shard_map/all_gather | solution.py:154
  108.6 10.4 %first_half.1 = (f32[128,256]{1,0:T(8,128)S(1)}, f32[128,512]{1,0:T(8,128)S(1)}, f32[8,256]{1,0:T(8,128)S(1)}) custom-call(f32[256,256]{1,0:T(8,128)S(1)} %slice.40.a_ref), custom_call_target="tpu_custom_call" | custom-call | flops 10000000000 | bytes 1000000 | tf_op jit(solution)/shard_map/first_half/pallas_call | solution.py:97
  119.0 3.4 %reduce-scatter.2.cloned.1.call-done = bf16[128,256]{1,0:T(8,128)(2,1)} async-done(((bf16[1024,256]{1,0:T(8,128)(2,1)}), bf16[128,256]{1,0:T(8,128)(2,1)}) %reduce-scatter.2.cloned.1.call-update) | async-done | bytes 65552 | tf_op jit(solution)/shard_map/reduce_scatter | solution.py:149
  122.4 11.5 %collective-permute-start.6 = (f32[256,128]{1,0:T(8,128)S(1)}, f32[256,128]{1,0:T(8,128)S(1)}, u32[]{:S(2)}, u32[]{:S(2)}) collective-permute-start(f32[256,128]{1,0:T(8,128)S(1)} %slice.41), channel_id=1, source_target_pairs={{0,0},{1,1},{2,32},{3,33},{4,64},{5,65},{6,96},{7,97},{8,128},{9,1... | collective-permute-start | bytes 393224 | tf_op jit(solution)/shard_map/ppermute | solution.py:177
  133.9 5.1 %collective-permute-start.7 = (f32[256,128]{1,0:T(8,128)S(1)}, f32[256,128]{1,0:T(8,128)S(1)}, u32[]{:S(2)}, u32[]{:S(2)}) collective-permute-start(f32[256,128]{1,0:T(8,128)S(1)} %slice.41), channel_id=1, source_target_pairs={{0,1},{1,0},{2,33},{3,32},{4,65},{5,64},{6,97},{7,96},{8,129},{9,1... | collective-permute-start | bytes 393224 | tf_op jit(solution)/shard_map/ppermute | solution.py:177
  139.0 0.8 constant_dynamic-slice_fusion.1
  139.8 8.4 %collective-permute-start.8 = (bf16[128,128]{1,0:T(8,128)(2,1)S(1)}, bf16[128,128]{1,0:T(8,128)(2,1)S(1)}, u32[]{:S(2)}, u32[]{:S(2)}) collective-permute-start(bf16[128,128]{1,0:T(8,128)(2,1)S(1)} %get-tuple-element.25), channel_id=1, source_target_pairs={{0,0},{1,1},{2,32},{3,33},{32,2},{33,3},{34,34},{35,35},{4,4},{5,5... | collective-permute-start | bytes 98312 | tf_op jit(solution)/shard_map/ppermute | solution.py:195
  148.3 2.5 %collective-permute-start.9 = (bf16[128,128]{1,0:T(8,128)(2,1)S(1)}, bf16[128,128]{1,0:T(8,128)(2,1)S(1)}, u32[]{:S(2)}, u32[]{:S(2)}) collective-permute-start(bf16[128,128]{1,0:T(8,128)(2,1)S(1)} %get-tuple-element.26), channel_id=1, source_target_pairs={{0,1},{1,0},{2,33},{3,32},{32,3},{33,2},{34,35},{35,34},{4,5},{5,4... | collective-permute-start | bytes 98312 | tf_op jit(solution)/shard_map/ppermute | solution.py:195
  150.8 9.6 %second_half.1 = f32[128,256]{1,0:T(8,128)S(1)} custom-call(f32[128,512]{1,0:T(8,128)S(1)} %get-tuple-element.11.rest_ref, f32[8,256]{1,0:T(8,128)S(1)} %get-tuple-element.12.scale_ref), custom_call_target="tpu_custom_call" | custom-call | flops 10000000000 | bytes 1000000 | tf_op jit(solution)/shard_map/second_half/pallas_call | solution.py:97
  160.3 0.0 collective-permute-done.8
  160.4 0.0 collective-permute-done.9
  160.4 0.0 collective-permute-done.6
  160.4 0.0 collective-permute-done.7
  160.4 0.6 convolution_convert_fusion.1
  161.1 0.0 copy-start.3
  161.1 0.9 subtract_select_fusion
  162.0 0.0 copy-done.3
  (16 shorter events, 0.3 us)
Async XLA Ops:
  7.2 1.7 copy-start
  7.2 0.7 copy-start.7
  8.0 0.7 copy-start.6
  10.4 0.7 copy-start.2
  12.2 6.8 %copy-start.1 = (f32[256,128]{1,0:T(8,128)S(1)}, f32[256,128]{1,0:T(8,128)}, u32[]{:S(2)}) copy-start(f32[256,128]{1,0:T(8,128)} %param.9) | copy-start | bytes 393220
  12.2 28.0 %all-to-all-start = ((bf16[8,128,512]{2,1,0:T(8,128)(2,1)}), bf16[8,128,512]{2,1,0:T(8,128)(2,1)S(1)}, u32[]{:S(2)}, u32[]{:S(2)}) async-start(bf16[8,128,512]{2,1,0:T(8,128)(2,1)} %broadcast_in_dim.10), calls=%async_computation | async-start | bytes 2097152 | tf_op jit(solution)/shard_map/all_to_all | solution.py:21
  19.0 0.7 collective-permute-start
  19.7 0.7 collective-permute-start.1
  20.4 24.4 %collective-permute-start.2 = (f32[256,128]{1,0:T(8,128)S(1)}, f32[256,128]{1,0:T(8,128)S(1)}, u32[]{:S(2)}, u32[]{:S(2)}) collective-permute-start(f32[256,128]{1,0:T(8,128)S(1)} %broadcast_select_fusion.1), channel_id=1, source_target_pairs={{0,4},{1,5},{8,12},{9,13},{16,20},{17,21},{24,28},{25,29}} | collective-permute-start | bytes 393224 | tf_op jit(solution)/shard_map/ppermute | solution.py:116
  41.3 13.2 %all-to-all-start.1 = ((bf16[4,2,128,512]{3,2,1,0:T(8,128)(2,1)}), bf16[4,2,128,512]{3,2,1,0:T(8,128)(2,1)S(1)}, u32[]{:S(2)}, u32[]{:S(2)}) async-start(bf16[4,2,128,512]{3,2,1,0:T(8,128)(2,1)} %broadcast_in_dim.11), calls=%async_computation.1 | async-start | bytes 2097152 | tf_op jit(solution)/shard_map/all_to_all | solution.py:21
  44.9 0.7 collective-permute-start.3
  45.6 0.7 collective-permute-start.4
  55.9 18.1 %copy-start.4 = (f32[256,128]{1,0:T(8,128)S(1)}, f32[256,128]{1,0:T(8,128)}, u32[]{:S(2)}) copy-start(f32[256,128]{1,0:T(8,128)} %get-tuple-element.17) | copy-start | bytes 393220
  55.9 18.1 %copy-start.5 = (f32[256,128]{1,0:T(8,128)S(1)}, f32[256,128]{1,0:T(8,128)}, u32[]{:S(2)}) copy-start(f32[256,128]{1,0:T(8,128)} %get-tuple-element.18) | copy-start | bytes 393220
  55.9 22.7 %collective-permute-start.5 = (bf16[1024,256]{1,0:T(8,128)(2,1)}, bf16[1024,256]{1,0:T(8,128)(2,1)}, u32[]{:S(2)}, u32[]{:S(2)}) collective-permute-start(bf16[1024,256]{1,0:T(8,128)(2,1)} %convolution_convert_fusion), channel_id=1, source_target_pairs={{0,32},{32,0},{1,33},{33,1},{2,34},{34,2},{3,35},{35,3},{4,36},{36... | collective-permute-start | bytes 1572872 | tf_op jit(solution)/shard_map/ppermute | solution.py:146
  75.1 17.9 %all-to-all-start.2 = ((f32[16,16,384]{2,1,0:T(8,128)}), f32[16,16,384]{2,1,0:T(8,128)S(1)}, u32[]{:S(2)}, u32[]{:S(2)}) async-start(f32[16,16,384]{2,1,0:T(8,128)} %bitcast.4), calls=%async_computation.2 | async-start | bytes 786432 | tf_op jit(solution)/shard_map/all_to_all | solution.py:153
  78.5 43.9 %reduce-scatter.2.cloned.1.call-start = ((), (), s32[]{:S(2)}) async-start(), calls=%async_computation.4 | async-start | bytes 589824 | tf_op jit(solution)/shard_map/reduce_scatter | solution.py:149
  122.4 38.0 %collective-permute-start.6 = (f32[256,128]{1,0:T(8,128)S(1)}, f32[256,128]{1,0:T(8,128)S(1)}, u32[]{:S(2)}, u32[]{:S(2)}) collective-permute-start(f32[256,128]{1,0:T(8,128)S(1)} %slice.41), channel_id=1, source_target_pairs={{0,0},{1,1},{2,32},{3,33},{4,64},{5,65},{6,96},{7,97},{8,128},{9,1... | collective-permute-start | bytes 393224 | tf_op jit(solution)/shard_map/ppermute | solution.py:177
  133.9 26.5 %collective-permute-start.7 = (f32[256,128]{1,0:T(8,128)S(1)}, f32[256,128]{1,0:T(8,128)S(1)}, u32[]{:S(2)}, u32[]{:S(2)}) collective-permute-start(f32[256,128]{1,0:T(8,128)S(1)} %slice.41), channel_id=1, source_target_pairs={{0,1},{1,0},{2,33},{3,32},{4,65},{5,64},{6,97},{7,96},{8,129},{9,1... | collective-permute-start | bytes 393224 | tf_op jit(solution)/shard_map/ppermute | solution.py:177
  139.8 20.5 %collective-permute-start.8 = (bf16[128,128]{1,0:T(8,128)(2,1)S(1)}, bf16[128,128]{1,0:T(8,128)(2,1)S(1)}, u32[]{:S(2)}, u32[]{:S(2)}) collective-permute-start(bf16[128,128]{1,0:T(8,128)(2,1)S(1)} %get-tuple-element.25), channel_id=1, source_target_pairs={{0,0},{1,1},{2,32},{3,33},{32,2},{33,3},{34,34},{35,35},{4,4},{5,5... | collective-permute-start | bytes 98312 | tf_op jit(solution)/shard_map/ppermute | solution.py:195
  148.3 12.1 %collective-permute-start.9 = (bf16[128,128]{1,0:T(8,128)(2,1)S(1)}, bf16[128,128]{1,0:T(8,128)(2,1)S(1)}, u32[]{:S(2)}, u32[]{:S(2)}) collective-permute-start(bf16[128,128]{1,0:T(8,128)(2,1)S(1)} %get-tuple-element.26), channel_id=1, source_target_pairs={{0,1},{1,0},{2,33},{3,32},{32,3},{33,2},{34,35},{35,34},{4,5},{5,4... | collective-permute-start | bytes 98312 | tf_op jit(solution)/shard_map/ppermute | solution.py:195
  161.1 0.9 copy-start.3
Sparse Core Ops, SparseCore 0:
  82.2 40.2 reduce-scatter.1

commit v4 on v3

--- a/solution.py
+++ b/solution.py
@@ -26,6 +26,40 @@
 
 def sub(tile, s):
     return jnp.broadcast_to(tile[s:s + 1, :], tile.shape)
+
+def group_rows(tile, start):
+    r = [sub(tile, s) for s in range(SUB)]
+    d = [[lane(r[i], start + j) if j >= i else None for j in range(SUB)] for i in range(SUB)]
+    pairs = []
+    for p in range(0, SUB, 2):
+        a, b, e = d[p][p], d[p][p + 1], d[p + 1][p + 1]
+        inv = 1.0 / (a * e - b * b)
+        ia, ib, ie = a * inv, b * inv, e * inv
+        raw, low = {}, {}
+        for i in range(p + 2, SUB):
+            raw[i] = (e * d[p][i] - b * d[p + 1][i], a * d[p + 1][i] - b * d[p][i])
+        for i in range(p + 2, SUB):
+            for j in range(i, SUB):
+                d[i][j] = d[i][j] - inv * (raw[i][0] * d[p][j] + raw[i][1] * d[p + 1][j])
+            low[i] = (raw[i][0] * inv, raw[i][1] * inv)
+            r[i] = r[i] - (low[i][0] * r[p] + low[i][1] * r[p + 1])
+        pairs.append((a, b, e, ia, ib, ie, low))
+    solved = [None] * SUB
+    for p in range(SUB - 2, -1, -2):
+        a, b, e, ia, ib, ie, low = pairs[p // 2]
+        s0 = ie * r[p] - ib * r[p + 1]
+        s1 = ia * r[p + 1] - ib * r[p]
+        for i in range(p + 2, SUB):
+            s0 = s0 - low[i][0] * solved[i]
+            s1 = s1 - low[i][1] * solved[i]
+        solved[p], solved[p + 1] = s0, s1
+    norm = [None] * SUB
+    for p in range(0, SUB, 2):
+        a, b, e = pairs[p // 2][:3]
+        ratio = b / a
+        norm[p] = r[p] * lax.rsqrt(a)
+        norm[p + 1] = (r[p + 1] - ratio * r[p]) * lax.rsqrt(e - ratio * b)
+    return norm, solved
 
 def block_inverse(block):
     n = BLOCK
@@ -36,25 +70,19 @@
     for t in range(n // SUB):
         unit = jnp.where(laneid == rowid + (n + t * SUB), 1.0, 0.0).astype(F32)
         tiles.append(wide[t * SUB:(t + 1) * SUB, :] + unit)
-    out = [None] * len(tiles)
     for t in range(len(tiles)):
-        acc = jnp.zeros((SUB, LANES), F32)
-        for s in range(0, SUB, 2):
-            k = t * SUB + s
-            r1, r2 = sub(tiles[t], s), sub(tiles[t], s + 1)
-            a, b, d = lane(r1, k), lane(r1, k + 1), lane(r2, k + 1)
-            inv = 1.0 / (a * d - b * b)
-            q1 = (d * r1 - b * r2) * inv
-            q2 = (a * r2 - b * r1) * inv
-            for u in range(t, len(tiles)):
-                c1, c2 = lane(tiles[u], k), lane(tiles[u], k + 1)
-                new = tiles[u] - (c1 * q1 + c2 * q2)
-                tiles[u] = jnp.where(rowid > s + 1, new, tiles[u]) if u == t else new
-            ratio = b / a
-            acc = jnp.where(rowid == s, r1 * lax.rsqrt(a), acc)
-            acc = jnp.where(rowid == s + 1, (r2 - ratio * r1) * lax.rsqrt(d - ratio * b), acc)
-        out[t] = acc
-    return jnp.concatenate(out, axis=0)[:, n:]
+        norm, solved = group_rows(tiles[t], t * SUB)
+        for u in range(t + 1, len(tiles)):
+            terms = [lane(tiles[u], t * SUB + s) * solved[s] for s in range(SUB)]
+            while len(terms) > 1:
+                terms = [x + y for x, y in zip(terms[::2], terms[1::2])]
+            tiles[u] = tiles[u] - terms[0]
+        out = norm[0]
+        for s in range(1, SUB):
+            out = jnp.where(rowid == s, norm[s], out)
+        tiles[t] = out
+    return jnp.concatenate(tiles, axis=0)[:, n:]
+
 
 def eliminate(aug, w_ref, s_row, start):
     n = aug.shape[1] // 2
@@ -111,21 +139,6 @@
     z, c, y, x = (lax.axis_index(a) for a in ("z", "c", "y", "x"))
     even = x % 2 == 0
 
-    def move(array, steps):
-        pairs = [(X * ys + xs, X * yd + xd) for (ys, xs), (yd, xd) in steps]
-        return lax.ppermute(array, ("z", "c", "y", "x"), pairs)
-
-    lead = separator
-    for span in (4, 2, 1):
-        steps = [((ys, xs), (ys + span, xs)) for ys in range(0, Y, 2 * span) for xs in range(2)]
-        lead = jnp.where(y % (2 * span) == span, move(lead, steps), lead)
-    steps = [((ys, xs), (ys, xs + 2)) for ys in range(Y) for xs in range(2)]
-    lead = jnp.where(x >= 2, move(lead, steps), lead)
-    steps = [((ys, xs), (ys, xs ^ 1)) for ys in range(Y) for xs in range(X)]
-    beside = move(lead, steps)
-    base = jnp.concatenate([jnp.where(even, lead, beside), jnp.where(even, beside, lead), separator], axis=1)
-    base = jnp.where((z == 0) & (c == 0), base, jnp.zeros_like(base))
-
     product = jnp.einsum("jib,jcb->jic", leaf_rows, leaf_inverse, precision=HI)
     row_mask = lax.dynamic_slice_in_dim(block_pattern, 2 * y + x // 2, 1, 1).astype(F32)
     col_mask = (jnp.arange(width, dtype=jnp.int32)[None, :] < leaf_widths[:, None]).astype(F32)
@@ -133,16 +146,38 @@
     own = jnp.concatenate([panels[j] for j in range(count)], axis=1)
     depth = own.shape[1]
 
+    shifted = [own] + [lax.ppermute(own, "x", [(i, (i + k) % X) for i in range(X)]) for k in range(1, X)]
+
+    def move(array, steps):
+        pairs = [(X * ys + xs, X * yd + xd) for (ys, xs), (yd, xd) in steps]
+        return lax.ppermute(array, ("z", "c", "y", "x"), pairs)
+
+    lead, *shifted = lax.optimization_barrier((separator, *shifted))
+    for span in (4, 2, 1):
+        steps = [((ys, xs), (ys + span, xs)) for ys in range(0, Y, 2 * span) for xs in range(2)]
+        lead = jnp.where(y % (2 * span) == span, move(lead, steps), lead)
+
+    def across(*moves):
+        return move(lead, [((ys, src), (ys, dst)) for ys in range(Y) for src, dst in moves])
+
+    one, two, three = across((0, 1), (1, 0)), across((0, 2), (1, 3)), across((0, 3), (1, 2))
+    lead0 = jnp.where(x == 0, lead, jnp.where(x == 1, one, jnp.where(x == 2, two, three)))
+    lead1 = jnp.where(x == 1, lead, jnp.where(x == 0, one, jnp.where(x == 3, two, three)))
+    base = jnp.concatenate([lead0, lead1, separator], axis=1)
+    base = jnp.where((z == 0) & (c == 0), base, jnp.zeros_like(base))
+
     along_y = share(own, "y", Y)
-    along_x = share(jnp.stack([own, along_y[0]]), "x", X)
-    along_x = along_x.reshape(X, 2, rows, depth)
-    first = along_x[:2, 1].reshape(2 * rows, depth)
     row_blocks = along_y.reshape(Y * rows, depth)
-    col_blocks = along_x[:, 0].reshape(X * rows, depth)
+    first = share(along_y[0], "x", X)[:2].reshape(2 * rows, depth)
+    def column(place):
+        block = shifted[0]
+        for k in range(1, X):
+            block = jnp.where((x - place) % X == k, shifted[k], block)
+        return block
 
     half = 2 * rows
-    theirs = lax.dynamic_slice_in_dim(col_blocks, (1 - c) * half, half, 0)
-    mine = lax.dynamic_slice_in_dim(col_blocks, c * half, half, 0)
+    theirs = jnp.concatenate([column(2 - 2 * c), column(3 - 2 * c)], axis=0)
+    mine = jnp.concatenate([column(2 * c), column(2 * c + 1)], axis=0)
     sent = lax.ppermute(dot_t(row_blocks, theirs).astype(BF16), "c", [(0, 1), (1, 0)])
     terms = (dot_t(row_blocks, mine) + sent.astype(F32)).astype(BF16)
 

time: 170 us -> 164 us (0.965)
  the two profiles are of different devices: /device:TPU:33 before, /device:TPU:16 now
where the time goes in v4:
time: 164 us
  waiting for transfers between devices  56.4 us (34%)
  starting transfers between devices  50.2 us (31%)
  blocking collectives  16.7 us (10%)
  between operations  14.6 us (9%)
  Pallas kernels  11.1 us (7%)
  matrix products  7.75 us (5%)
  local copies, waits for them, and re-layouts  5.69 us (3%)
    all_gather x1, blocking collectives, body(): lax.all_gather(jnp.sum(pieces, axis=0), ('z', 'c'), axis=0, tiled=True)  16.7 us
    ppermute x6, waiting for transfers between devices, move(): return lax.ppermute(array, ('z', 'c', 'y', 'x'), pairs)  14.2 us
    ppermute x2, waiting for transfers between devices, flip(): return lax.ppermute(top_own, ('z', 'c', 'y', 'x'), pairs)  14.1 us
    all_to_all x2, starting transfers between devices, share(): return lax.all_to_all(copies, axis, 0, 0, tiled=True)  12.8 us
    all_to_all x1, waiting for transfers between devices, body(): lax.all_to_all(part.reshape(Z * C, slab, 3 * rows), ('z', 'c'), 0, 0, til...  11.1 us
    pallas_call x2, Pallas kernels, in_vmem(): pl.pallas_call(body, out_shape=[jax.ShapeDtypeStruct(shape, F32) for shap...  11.1 us
    ppermute x6, starting transfers between devices, move(): return lax.ppermute(array, ('z', 'c', 'y', 'x'), pairs)  9.79 us
    ppermute x3, starting transfers between devices, body(): lax.ppermute(own, 'x', [(i, (i + k) % X) for i in range(X)])  9.63 us
  transfers between devices with their start and end apart: 18, of which 8 were waited for; matrix products, arithmetic and copies ran while one was open for 4% of the time, Pallas kernels for 7%

profile of v4, /device:TPU:16, one launch (start us, length us, event | category | flops | bytes accessed | tf_op | source)
XLA Modules:
  0.0 163.6 jit_solution(5981197571908061769)
XLA Ops:
  7.2 0.0 copy-start
  7.2 0.0 copy-start.7
  7.2 0.7 copy-done.7
  7.9 0.1 compare_convert_fusion
  8.0 0.7 copy-done.6
  8.7 0.2 convert_reduce_fusion
  8.8 0.0 copy-done
  8.8 1.6 fusion.1
  10.4 0.0 copy-start.2
  10.5 0.6 copy-done.2
  11.1 1.1 broadcast_in_dim.12
  12.2 9.3 %all-to-all-start = ((bf16[8,128,512]{2,1,0:T(8,128)(2,1)}), bf16[8,128,512]{2,1,0:T(8,128)(2,1)S(1)}, u32[]{:S(2)}, u32[]{:S(2)}) async-start(bf16[8,128,512]{2,1,0:T(8,128)(2,1)} %broadcast_in_dim.12), calls=%async_computation | async-start | bytes 2097152 | tf_op jit(solution)/shard_map/all_to_all | solution.py:21
  21.5 1.9 %collective-permute-start = (bf16[128,512]{1,0:T(8,128)(2,1)S(1)}, bf16[128,512]{1,0:T(8,128)(2,1)S(1)}, u32[]{:S(2)}, u32[]{:S(2)}) collective-permute-start(bf16[128,512]{1,0:T(8,128)(2,1)S(1)} %pad_maximum_fusion), channel_id=1, source_target_pairs={{0,1},{1,2},{2,3},{3,0},{4,5},{5,6},{6,7},{7,4},{8,9},{9,10},{10,1... | collective-permute-start | bytes 393224 | tf_op jit(solution)/shard_map/ppermute | solution.py:149
  23.4 4.4 %collective-permute-start.1 = (bf16[128,512]{1,0:T(8,128)(2,1)S(1)}, bf16[128,512]{1,0:T(8,128)(2,1)S(1)}, u32[]{:S(2)}, u32[]{:S(2)}) collective-permute-start(bf16[128,512]{1,0:T(8,128)(2,1)S(1)} %pad_maximum_fusion), channel_id=1, source_target_pairs={{0,2},{1,3},{2,0},{3,1},{4,6},{5,7},{6,4},{7,5},{8,10},{9,11},{10,... | collective-permute-start | bytes 393224 | tf_op jit(solution)/shard_map/ppermute | solution.py:149
  27.8 3.3 %collective-permute-start.2 = (bf16[128,512]{1,0:T(8,128)(2,1)S(1)}, bf16[128,512]{1,0:T(8,128)(2,1)S(1)}, u32[]{:S(2)}, u32[]{:S(2)}) collective-permute-start(bf16[128,512]{1,0:T(8,128)(2,1)S(1)} %pad_maximum_fusion), channel_id=1, source_target_pairs={{0,3},{1,0},{2,1},{3,2},{4,7},{5,4},{6,5},{7,6},{8,11},{9,8},{10,9... | collective-permute-start | bytes 393224 | tf_op jit(solution)/shard_map/ppermute | solution.py:149
  31.1 1.2 collective-permute-done
  32.4 0.0 collective-permute-done.1
  32.4 2.8 %collective-permute-done.2 = bf16[128,512]{1,0:T(8,128)(2,1)S(1)} collective-permute-done((bf16[128,512]{1,0:T(8,128)(2,1)S(1)}, bf16[128,512]{1,0:T(8,128)(2,1)S(1)}, u32[]{:S(2)}, u32[]{:S(2)}) %collective-permute-start.2) | collective-permute-done | bytes 131104 | tf_op jit(solution)/shard_map/ppermute | solution.py:149
  35.1 0.7 collective-permute-start.3
  35.8 0.0 collective-permute-done.3
  35.8 1.3 collective-permute-start.4
  37.3 12.4 %collective-permute-done.4 = f32[256,128]{1,0:T(8,128)S(1)} collective-permute-done((f32[256,128]{1,0:T(8,128)S(1)}, f32[256,128]{1,0:T(8,128)S(1)}, u32[]{:S(2)}, u32[]{:S(2)}) %collective-permute-start.4) | collective-permute-done | bytes 131104 | tf_op jit(solution)/shard_map/ppermute | solution.py:153
  49.7 1.3 collective-permute-start.5
  51.1 0.8 select_select_fusion.3
  51.8 1.7 %collective-permute-done.5 = f32[256,128]{1,0:T(8,128)S(1)} collective-permute-done((f32[256,128]{1,0:T(8,128)S(1)}, f32[256,128]{1,0:T(8,128)S(1)}, u32[]{:S(2)}, u32[]{:S(2)}) %collective-permute-start.5) | collective-permute-done | bytes 131104 | tf_op jit(solution)/shard_map/ppermute | solution.py:153
  53.6 4.0 %collective-permute-start.6 = (f32[256,128]{1,0:T(8,128)S(1)}, f32[256,128]{1,0:T(8,128)S(1)}, u32[]{:S(2)}, u32[]{:S(2)}) collective-permute-start(f32[256,128]{1,0:T(8,128)S(1)} %broadcast_select_fusion.4), channel_id=1, source_target_pairs={{0,1},{1,0},{4,5},{5,4},{8,9},{9,8},{12,13},{13,12},{16,17},{17,16... | collective-permute-start | bytes 393224 | tf_op jit(solution)/shard_map/ppermute | solution.py:153
  57.5 1.3 collective-permute-start.7
  58.8 1.3 collective-permute-start.8
  60.1 0.0 all-to-all-done
  60.2 0.9 broadcast_in_dim.27
  61.0 3.5 %all-to-all-start.1 = ((bf16[4,128,512]{2,1,0:T(8,128)(2,1)}), bf16[4,128,512]{2,1,0:T(8,128)(2,1)S(1)}, u32[]{:S(2)}, u32[]{:S(2)}) async-start(bf16[4,128,512]{2,1,0:T(8,128)(2,1)} %broadcast_in_dim.27), calls=%async_computation.1 | async-start | bytes 1048576 | tf_op jit(solution)/shard_map/all_to_all | solution.py:21
  64.5 0.0 copy-start.4
  64.5 0.0 copy-start.5
  64.5 0.0 collective-permute-done.6
  64.5 0.0 collective-permute-done.7
  64.5 0.0 collective-permute-done.8
  64.6 0.8 copy-done.4
  65.4 0.1 copy-done.5
  65.5 1.3 convolution_convert_fusion
  66.7 1.9 %collective-permute-start.9 = (bf16[1024,256]{1,0:T(8,128)(2,1)}, bf16[1024,256]{1,0:T(8,128)(2,1)}, u32[]{:S(2)}, u32[]{:S(2)}) collective-permute-start(bf16[1024,256]{1,0:T(8,128)(2,1)} %convolution_convert_fusion), channel_id=1, source_target_pairs={{0,32},{32,0},{1,33},{33,1},{2,34},{34,2},{3,35},{35,3},{4,36},{36... | collective-permute-start | bytes 1572872 | tf_op jit(solution)/shard_map/ppermute | solution.py:181
  68.7 3.9 %all-to-all-done.1 = bf16[4,128,512]{2,1,0:T(8,128)(2,1)S(1)} async-done(((bf16[4,128,512]{2,1,0:T(8,128)(2,1)}), bf16[4,128,512]{2,1,0:T(8,128)(2,1)S(1)}, u32[]{:S(2)}, u32[]{:S(2)}) %all-to-all-start.1) | async-done | bytes 524320 | tf_op jit(solution)/shard_map/all_to_all | solution.py:21
  72.6 1.1 convolution_subtract_fusion
  73.6 3.6 %all-to-all-start.2 = ((f32[16,16,384]{2,1,0:T(8,128)}), f32[16,16,384]{2,1,0:T(8,128)S(1)}, u32[]{:S(2)}, u32[]{:S(2)}) async-start(f32[16,16,384]{2,1,0:T(8,128)} %bitcast.4), calls=%async_computation.2 | async-start | bytes 786432 | tf_op jit(solution)/shard_map/all_to_all | solution.py:188
  77.2 0.0 reduce-scatter.2.cloned.1.call-start
  77.3 0.0 collective-permute-done.9
  77.3 2.3 %add_convert_fusion = bf16[1024,256]{1,0:T(8,128)(2,1)} fusion(bf16[1024,256]{1,0:T(8,128)(2,1)} %collective-permute-done.9, bf16[1024,512]{1,0:T(8,128)(2,1)S(1)} %bitcast.16, bf16[128,512]{1,0:T(8,128)(2,1)S(1)} %get-tuple-element.28, bf16[128,512]{1,0:T(8,128)(2,1)S(1)} %get-tuple-element.25), kind=kOutput, calls=%fused_computation.6 | convolution fusion | flops 269746176 | bytes 2359296 | tf_op jit(solution)/shard_map/dot_general | solution.py:16
  79.6 0.0 reduce-scatter.2.cloned.1.call-update
  79.6 11.1 %all-to-all-done.2 = f32[16,16,384]{2,1,0:T(8,128)S(1)} async-done(((f32[16,16,384]{2,1,0:T(8,128)}), f32[16,16,384]{2,1,0:T(8,128)S(1)}, u32[]{:S(2)}, u32[]{:S(2)}) %all-to-all-start.2) | async-done | bytes 393248 | tf_op jit(solution)/shard_map/all_to_all | solution.py:188
  90.8 16.7 %all_gather.3 = f32[256,384]{1,0:T(8,128)S(1)} all-gather(f32[16,384]{1,0:T(8,128)S(1)} %reduce_sum.9), channel_id=1, replica_groups=mesh['z'=8,'c'=2,'y'=8,'x'=4] {'z','c'}, dimensions={0}, use_global_device_ids=true | all-gather | bytes 417792 | tf_op jit(solution)/shard_map/all_gather | solution.py:189
  107.5 6.1 %first_half.1 = (f32[128,256]{1,0:T(8,128)S(1)}, f32[128,512]{1,0:T(8,128)S(1)}, f32[8,256]{1,0:T(8,128)S(1)}) custom-call(f32[256,256]{1,0:T(8,128)S(1)} %slice.36.a_ref), custom_call_target="tpu_custom_call" | custom-call | flops 10000000000 | bytes 1000000 | tf_op jit(solution)/shard_map/first_half/pallas_call | solution.py:125
  113.6 9.1 %reduce-scatter.2.cloned.1.call-done = bf16[128,256]{1,0:T(8,128)(2,1)} async-done(((bf16[1024,256]{1,0:T(8,128)(2,1)}), bf16[128,256]{1,0:T(8,128)(2,1)}) %reduce-scatter.2.cloned.1.call-update) | async-done | bytes 65552 | tf_op jit(solution)/shard_map/reduce_scatter | solution.py:184
  122.7 2.6 %collective-permute-start.10 = (f32[256,128]{1,0:T(8,128)S(1)}, f32[256,128]{1,0:T(8,128)S(1)}, u32[]{:S(2)}, u32[]{:S(2)}) collective-permute-start(f32[256,128]{1,0:T(8,128)S(1)} %slice.37), channel_id=1, source_target_pairs={{0,0},{1,1},{2,32},{3,33},{4,64},{5,65},{6,96},{7,97},{8,128},{9,1... | collective-permute-start | bytes 393224 | tf_op jit(solution)/shard_map/ppermute | solution.py:212
  125.3 6.8 %collective-permute-start.11 = (f32[256,128]{1,0:T(8,128)S(1)}, f32[256,128]{1,0:T(8,128)S(1)}, u32[]{:S(2)}, u32[]{:S(2)}) collective-permute-start(f32[256,128]{1,0:T(8,128)S(1)} %slice.37), channel_id=1, source_target_pairs={{0,1},{1,0},{2,33},{3,32},{4,65},{5,64},{6,97},{7,96},{8,129},{9,1... | collective-permute-start | bytes 393224 | tf_op jit(solution)/shard_map/ppermute | solution.py:212
  132.1 0.8 constant_dynamic-slice_fusion.1
  132.9 0.7 collective-permute-start.12
  133.5 2.5 %collective-permute-start.13 = (bf16[128,128]{1,0:T(8,128)(2,1)S(1)}, bf16[128,128]{1,0:T(8,128)(2,1)S(1)}, u32[]{:S(2)}, u32[]{:S(2)}) collective-permute-start(bf16[128,128]{1,0:T(8,128)(2,1)S(1)} %get-tuple-element.38), channel_id=1, source_target_pairs={{0,1},{1,0},{2,33},{3,32},{32,3},{33,2},{34,35},{35,34},{4,5},{5,4... | collective-permute-start | bytes 98312 | tf_op jit(solution)/shard_map/ppermute | solution.py:230
  136.0 5.0 %second_half.1 = f32[128,256]{1,0:T(8,128)S(1)} custom-call(f32[128,512]{1,0:T(8,128)S(1)} %get-tuple-element.21.rest_ref, f32[8,256]{1,0:T(8,128)S(1)} %get-tuple-element.22.scale_ref), custom_call_target="tpu_custom_call" | custom-call | flops 10000000000 | bytes 1000000 | tf_op jit(solution)/shard_map/second_half/pallas_call | solution.py:125
  141.1 0.0 collective-permute-done.12
  141.1 0.0 collective-permute-done.13
  141.1 0.0 collective-permute-done.10
  141.1 14.1 %collective-permute-done.11 = f32[256,128]{1,0:T(8,128)S(1)} collective-permute-done((f32[256,128]{1,0:T(8,128)S(1)}, f32[256,128]{1,0:T(8,128)S(1)}, u32[]{:S(2)}, u32[]{:S(2)}) %collective-permute-start.11) | collective-permute-done | bytes 131104 | tf_op jit(solution)/shard_map/ppermute | solution.py:212
  155.3 0.6 convolution_convert_fusion.1
  155.9 0.0 copy-start.3
  155.9 0.9 subtract_select_fusion
  (18 shorter events, 0.2 us)
Async XLA Ops:
  7.2 1.7 %copy-start = (f32[2,256,256]{2,1,0:T(8,128)S(1)}, f32[2,256,256]{2,1,0:T(8,128)}, u32[]{:S(2)}) copy-start(f32[2,256,256]{2,1,0:T(8,128)} %param.6) | copy-start | bytes 1572868
  7.2 0.7 copy-start.7
  8.0 0.7 copy-start.6
  10.4 0.7 copy-start.2
  12.2 23.0 %copy-start.1 = (f32[256,128]{1,0:T(8,128)S(1)}, f32[256,128]{1,0:T(8,128)}, u32[]{:S(2)}) copy-start(f32[256,128]{1,0:T(8,128)} %param.9) | copy-start | bytes 393220
  12.2 48.0 %all-to-all-start = ((bf16[8,128,512]{2,1,0:T(8,128)(2,1)}), bf16[8,128,512]{2,1,0:T(8,128)(2,1)S(1)}, u32[]{:S(2)}, u32[]{:S(2)}) async-start(bf16[8,128,512]{2,1,0:T(8,128)(2,1)} %broadcast_in_dim.12), calls=%async_computation | async-start | bytes 2097152 | tf_op jit(solution)/shard_map/all_to_all | solution.py:21
  21.5 10.9 %collective-permute-start = (bf16[128,512]{1,0:T(8,128)(2,1)S(1)}, bf16[128,512]{1,0:T(8,128)(2,1)S(1)}, u32[]{:S(2)}, u32[]{:S(2)}) collective-permute-start(bf16[128,512]{1,0:T(8,128)(2,1)S(1)} %pad_maximum_fusion), channel_id=1, source_target_pairs={{0,1},{1,2},{2,3},{3,0},{4,5},{5,6},{6,7},{7,4},{8,9},{9,10},{10,1... | collective-permute-start | bytes 393224 | tf_op jit(solution)/shard_map/ppermute | solution.py:149
  23.4 8.9 %collective-permute-start.1 = (bf16[128,512]{1,0:T(8,128)(2,1)S(1)}, bf16[128,512]{1,0:T(8,128)(2,1)S(1)}, u32[]{:S(2)}, u32[]{:S(2)}) collective-permute-start(bf16[128,512]{1,0:T(8,128)(2,1)S(1)} %pad_maximum_fusion), channel_id=1, source_target_pairs={{0,2},{1,3},{2,0},{3,1},{4,6},{5,7},{6,4},{7,5},{8,10},{9,11},{10,... | collective-permute-start | bytes 393224 | tf_op jit(solution)/shard_map/ppermute | solution.py:149
  27.8 7.3 %collective-permute-start.2 = (bf16[128,512]{1,0:T(8,128)(2,1)S(1)}, bf16[128,512]{1,0:T(8,128)(2,1)S(1)}, u32[]{:S(2)}, u32[]{:S(2)}) collective-permute-start(bf16[128,512]{1,0:T(8,128)(2,1)S(1)} %pad_maximum_fusion), channel_id=1, source_target_pairs={{0,3},{1,0},{2,1},{3,2},{4,7},{5,4},{6,5},{7,6},{8,11},{9,8},{10,9... | collective-permute-start | bytes 393224 | tf_op jit(solution)/shard_map/ppermute | solution.py:149
  35.1 0.7 collective-permute-start.3
  35.8 13.9 %collective-permute-start.4 = (f32[256,128]{1,0:T(8,128)S(1)}, f32[256,128]{1,0:T(8,128)S(1)}, u32[]{:S(2)}, u32[]{:S(2)}) collective-permute-start(f32[256,128]{1,0:T(8,128)S(1)} %broadcast_select_fusion.2), channel_id=1, source_target_pairs={{0,8},{1,9},{16,24},{17,25}} | collective-permute-start | bytes 393224 | tf_op jit(solution)/shard_map/ppermute | solution.py:153
  49.7 3.8 %collective-permute-start.5 = (f32[256,128]{1,0:T(8,128)S(1)}, f32[256,128]{1,0:T(8,128)S(1)}, u32[]{:S(2)}, u32[]{:S(2)}) collective-permute-start(f32[256,128]{1,0:T(8,128)S(1)} %broadcast_select_fusion.3), channel_id=1, source_target_pairs={{0,4},{1,5},{8,12},{9,13},{16,20},{17,21},{24,28},{25,29}} | collective-permute-start | bytes 393224 | tf_op jit(solution)/shard_map/ppermute | solution.py:153
  53.6 11.0 %collective-permute-start.6 = (f32[256,128]{1,0:T(8,128)S(1)}, f32[256,128]{1,0:T(8,128)S(1)}, u32[]{:S(2)}, u32[]{:S(2)}) collective-permute-start(f32[256,128]{1,0:T(8,128)S(1)} %broadcast_select_fusion.4), channel_id=1, source_target_pairs={{0,1},{1,0},{4,5},{5,4},{8,9},{9,8},{12,13},{13,12},{16,17},{17,16... | collective-permute-start | bytes 393224 | tf_op jit(solution)/shard_map/ppermute | solution.py:153
  57.5 7.0 %collective-permute-start.7 = (f32[256,128]{1,0:T(8,128)S(1)}, f32[256,128]{1,0:T(8,128)S(1)}, u32[]{:S(2)}, u32[]{:S(2)}) collective-permute-start(f32[256,128]{1,0:T(8,128)S(1)} %broadcast_select_fusion.4), channel_id=1, source_target_pairs={{0,2},{1,3},{4,6},{5,7},{8,10},{9,11},{12,14},{13,15},{16,18},{17,... | collective-permute-start | bytes 393224 | tf_op jit(solution)/shard_map/ppermute | solution.py:153
  58.8 5.7 %collective-permute-start.8 = (f32[256,128]{1,0:T(8,128)S(1)}, f32[256,128]{1,0:T(8,128)S(1)}, u32[]{:S(2)}, u32[]{:S(2)}) collective-permute-start(f32[256,128]{1,0:T(8,128)S(1)} %broadcast_select_fusion.4), channel_id=1, source_target_pairs={{0,3},{1,2},{4,7},{5,6},{8,11},{9,10},{12,15},{13,14},{16,19},{17,... | collective-permute-start | bytes 393224 | tf_op jit(solution)/shard_map/ppermute | solution.py:153
  61.0 11.5 %all-to-all-start.1 = ((bf16[4,128,512]{2,1,0:T(8,128)(2,1)}), bf16[4,128,512]{2,1,0:T(8,128)(2,1)S(1)}, u32[]{:S(2)}, u32[]{:S(2)}) async-start(bf16[4,128,512]{2,1,0:T(8,128)(2,1)} %broadcast_in_dim.27), calls=%async_computation.1 | async-start | bytes 1048576 | tf_op jit(solution)/shard_map/all_to_all | solution.py:21
  64.5 0.9 copy-start.4
  64.5 1.0 copy-start.5
  66.7 10.6 %collective-permute-start.9 = (bf16[1024,256]{1,0:T(8,128)(2,1)}, bf16[1024,256]{1,0:T(8,128)(2,1)}, u32[]{:S(2)}, u32[]{:S(2)}) collective-permute-start(bf16[1024,256]{1,0:T(8,128)(2,1)} %convolution_convert_fusion), channel_id=1, source_target_pairs={{0,32},{32,0},{1,33},{33,1},{2,34},{34,2},{3,35},{35,3},{4,36},{36... | collective-permute-start | bytes 1572872 | tf_op jit(solution)/shard_map/ppermute | solution.py:181
  73.6 17.1 %all-to-all-start.2 = ((f32[16,16,384]{2,1,0:T(8,128)}), f32[16,16,384]{2,1,0:T(8,128)S(1)}, u32[]{:S(2)}, u32[]{:S(2)}) async-start(f32[16,16,384]{2,1,0:T(8,128)} %bitcast.4), calls=%async_computation.2 | async-start | bytes 786432 | tf_op jit(solution)/shard_map/all_to_all | solution.py:188
  77.2 45.5 %reduce-scatter.2.cloned.1.call-start = ((), (), s32[]{:S(2)}) async-start(), calls=%async_computation.4 | async-start | bytes 589824 | tf_op jit(solution)/shard_map/reduce_scatter | solution.py:184
  122.7 18.4 %collective-permute-start.10 = (f32[256,128]{1,0:T(8,128)S(1)}, f32[256,128]{1,0:T(8,128)S(1)}, u32[]{:S(2)}, u32[]{:S(2)}) collective-permute-start(f32[256,128]{1,0:T(8,128)S(1)} %slice.37), channel_id=1, source_target_pairs={{0,0},{1,1},{2,32},{3,33},{4,64},{5,65},{6,96},{7,97},{8,128},{9,1... | collective-permute-start | bytes 393224 | tf_op jit(solution)/shard_map/ppermute | solution.py:212
  125.3 29.9 %collective-permute-start.11 = (f32[256,128]{1,0:T(8,128)S(1)}, f32[256,128]{1,0:T(8,128)S(1)}, u32[]{:S(2)}, u32[]{:S(2)}) collective-permute-start(f32[256,128]{1,0:T(8,128)S(1)} %slice.37), channel_id=1, source_target_pairs={{0,1},{1,0},{2,33},{3,32},{4,65},{5,64},{6,97},{7,96},{8,129},{9,1... | collective-permute-start | bytes 393224 | tf_op jit(solution)/shard_map/ppermute | solution.py:212
  132.9 8.2 %collective-permute-start.12 = (bf16[128,128]{1,0:T(8,128)(2,1)S(1)}, bf16[128,128]{1,0:T(8,128)(2,1)S(1)}, u32[]{:S(2)}, u32[]{:S(2)}) collective-permute-start(bf16[128,128]{1,0:T(8,128)(2,1)S(1)} %get-tuple-element.37), channel_id=1, source_target_pairs={{0,0},{1,1},{2,32},{3,33},{32,2},{33,3},{34,34},{35,35},{4,4},{5,5... | collective-permute-start | bytes 98312 | tf_op jit(solution)/shard_map/ppermute | solution.py:230
  133.5 7.5 %collective-permute-start.13 = (bf16[128,128]{1,0:T(8,128)(2,1)S(1)}, bf16[128,128]{1,0:T(8,128)(2,1)S(1)}, u32[]{:S(2)}, u32[]{:S(2)}) collective-permute-start(bf16[128,128]{1,0:T(8,128)(2,1)S(1)} %get-tuple-element.38), channel_id=1, source_target_pairs={{0,1},{1,0},{2,33},{3,32},{32,3},{33,2},{34,35},{35,34},{4,5},{5,4... | collective-permute-start | bytes 98312 | tf_op jit(solution)/shard_map/ppermute | solution.py:230
  155.9 0.9 copy-start.3
Sparse Core Ops, SparseCore 0:
  80.8 41.7 reduce-scatter.1

commit v5 on v4

--- a/solution.py
+++ b/solution.py
@@ -99,9 +99,9 @@
             )
 
 
-def first_half(a_ref, w_ref, rest_ref, scale_ref, aug):
+def inverse_factor(a_ref, w_ref, aug):
     n = a_ref.shape[0]
-    a = a_ref[...]
+    a = a_ref[:, :n]
     a = a * 0.5 + a.T * 0.5
     ri = lax.broadcasted_iota(jnp.int32, (n, n), 0)
     ci = lax.broadcasted_iota(jnp.int32, (n, n), 1)
@@ -111,13 +111,6 @@
     aug[:, :n] = a * s_col * s_row
     aug[:, n:] = jnp.where(ri == ci, 1.0, 0.0)
     eliminate(aug, w_ref, s_row, 0)
-    rest_ref[...] = aug[n // 2:, :]
-    scale_ref[...] = jnp.broadcast_to(s_row, scale_ref.shape)
-
-
-def second_half(rest_ref, scale_ref, w_ref, aug):
-    aug[...] = rest_ref[...]
-    eliminate(aug, w_ref, scale_ref[:1, :], rest_ref.shape[0])
 
 
 def in_vmem(body, outs, scratch, name, *args):
@@ -146,95 +139,68 @@
     own = jnp.concatenate([panels[j] for j in range(count)], axis=1)
     depth = own.shape[1]
 
-    shifted = [own] + [lax.ppermute(own, "x", [(i, (i + k) % X) for i in range(X)]) for k in range(1, X)]
-
-    def move(array, steps):
-        pairs = [(X * ys + xs, X * yd + xd) for (ys, xs), (yd, xd) in steps]
-        return lax.ppermute(array, ("z", "c", "y", "x"), pairs)
-
-    lead, *shifted = lax.optimization_barrier((separator, *shifted))
-    for span in (4, 2, 1):
-        steps = [((ys, xs), (ys + span, xs)) for ys in range(0, Y, 2 * span) for xs in range(2)]
-        lead = jnp.where(y % (2 * span) == span, move(lead, steps), lead)
-
-    def across(*moves):
-        return move(lead, [((ys, src), (ys, dst)) for ys in range(Y) for src, dst in moves])
-
-    one, two, three = across((0, 1), (1, 0)), across((0, 2), (1, 3)), across((0, 3), (1, 2))
-    lead0 = jnp.where(x == 0, lead, jnp.where(x == 1, one, jnp.where(x == 2, two, three)))
-    lead1 = jnp.where(x == 1, lead, jnp.where(x == 0, one, jnp.where(x == 3, two, three)))
-    base = jnp.concatenate([lead0, lead1, separator], axis=1)
-    base = jnp.where((z == 0) & (c == 0), base, jnp.zeros_like(base))
-
+    def send(array, pairs):
+        return lax.ppermute(array, ("y", "x"), [(X * ys + xs, X * yd + xd) for (ys, xs), (yd, xd) in pairs])
+
+    block = own
+    for k in range(1, Y):
+        got = send(own, [((0, xs), (k, xs)) for xs in range(2)])
+        block = jnp.where(y == k, got, block)
+    own, block = lax.optimization_barrier((own, block))
+    one, two, three = (
+        send(block, [((ys, src), (ys, dst)) for ys in range(Y) for src, dst in moves])
+        for moves in (((0, 1), (1, 0)), ((0, 2), (1, 3)), ((0, 3), (1, 2)))
+    )
+    first = jnp.concatenate(
+        [
+            jnp.where(x == 0, block, jnp.where(x == 1, one, jnp.where(x == 2, two, three))),
+            jnp.where(x == 1, block, jnp.where(x == 0, one, jnp.where(x == 3, two, three))),
+        ],
+        axis=0,
+    )
     along_y = share(own, "y", Y)
-    row_blocks = along_y.reshape(Y * rows, depth)
-    first = share(along_y[0], "x", X)[:2].reshape(2 * rows, depth)
-    def column(place):
-        block = shifted[0]
-        for k in range(1, X):
-            block = jnp.where((x - place) % X == k, shifted[k], block)
-        return block
-
-    half = 2 * rows
-    theirs = jnp.concatenate([column(2 - 2 * c), column(3 - 2 * c)], axis=0)
-    mine = jnp.concatenate([column(2 * c), column(2 * c + 1)], axis=0)
-    sent = lax.ppermute(dot_t(row_blocks, theirs).astype(BF16), "c", [(0, 1), (1, 0)])
-    terms = (dot_t(row_blocks, mine) + sent.astype(F32)).astype(BF16)
-
-    update = lax.psum_scatter(terms, "z", scatter_dimension=0, tiled=True)
+    shifted = [lax.ppermute(own, "x", [(i, (i + k) % X) for i in range(X)]) for k in range(1, X)]
 
     slab = width // (Z * C)
-    part = base - dot_t(first, jnp.concatenate([first, own], axis=0))
-    pieces = lax.all_to_all(part.reshape(Z * C, slab, 3 * rows), ("z", "c"), 0, 0, tiled=True)
-    top = lax.all_gather(jnp.sum(pieces, axis=0), ("z", "c"), axis=0, tiled=True)
-    top_own = top[:, width:]
-
-    half_rows = width // 2
-    upper, rest, scale = in_vmem(
-        first_half, [(half_rows, width), (half_rows, 2 * width), (SUB, width)], (width, 2 * width),
-        "first_half", top[:, :width],
-    )
-    rest, top_own, update = lax.optimization_barrier((rest, top_own, update))
-    (lower,) = in_vmem(
-        second_half, [(half_rows, width)], (half_rows, 2 * width), "second_half", rest, scale
-    )
-    inverse = jnp.concatenate([upper, lower], axis=0)
-
-    def flip(t):
-        pairs = []
-        for zs in range(Z):
-            for cs in range(C):
-                for ys in range(Y):
-                    for xs in range(X):
-                        src = ((zs * C + cs) * Y + ys) * X + xs
-                        dst = ((ys * C + xs // 2) * Y + zs) * X + 2 * cs + ((xs % 2) ^ t)
-                        pairs.append((src, dst))
-        return lax.ppermute(top_own, ("z", "c", "y", "x"), pairs)
-
-    straight, crossed = flip(0), flip(1)
-    top_rows = jnp.concatenate(
-        [jnp.where(even, straight, crossed), jnp.where(even, crossed, straight)], axis=1
-    )
-
+    base = jnp.where((z == 0) & (c == 0), separator, jnp.zeros_like(separator))
+    part = base - dot_t(first, own)
+    part, along_y, *shifted = lax.optimization_barrier((part, along_y, *shifted))
+    pieces = lax.all_to_all(part.reshape(Z * C, slab, rows), ("z", "c"), 0, 0, tiled=True)
+    strip = jnp.sum(pieces, axis=0)
+
+    shifted = [own] + shifted
+    cols = []
+    for k in range(X):
+        place = (2 * c + x % 2) ^ k
+        found = shifted[0]
+        for m in range(1, X):
+            found = jnp.where((x - place) % X == m, shifted[m], found)
+        cols.append(found)
+    terms = dot_t(along_y.reshape(Y * rows, depth), jnp.concatenate(cols, axis=0)).astype(BF16)
+    moved = []
+    for k in range(X):
+        pairs = [(cs * X + xs, (xs // 2) * X + ((2 * cs + xs % 2) ^ k)) for cs in range(C) for xs in range(X)]
+        moved.append(lax.ppermute(terms[:, k * rows:(k + 1) * rows], ("c", "x"), pairs).astype(F32))
+    upper, lower = (moved[0] + moved[2]).astype(BF16), (moved[1] + moved[3]).astype(BF16)
+    terms = jnp.stack([jnp.where(even, upper, lower), jnp.where(even, lower, upper)])
+    terms = terms.reshape(2, Z, rows, rows).transpose(1, 0, 2, 3).reshape(Z, width, rows)
+
+    strips = share(strip, ("y", "x"), Y * X)
+    lead = jnp.concatenate([strips[0], strips[1], strip], axis=1)
+    groups = strips.reshape(Z * C, 2, slab, rows).transpose(0, 2, 1, 3).reshape(Z * C, slab, width)
+    top = jnp.concatenate([jnp.broadcast_to(lead[None], (Z * C,) + lead.shape), groups], axis=2)
+    top, terms = lax.optimization_barrier((top, terms))
+    top = lax.all_to_all(top, ("z", "c"), 0, 0, tiled=True).reshape(width, 5 * rows)
+    top, terms = lax.optimization_barrier((top, terms))
+    top_own, top_rows = top[:, width:width + rows], top[:, width + rows:]
+    update = jnp.sum(lax.all_to_all(terms, "z", 0, 0, tiled=True).astype(F32), axis=0)
+
+    (inverse,) = in_vmem(inverse_factor, [(width, width)], (width, 2 * width), "inverse_factor", top[:, :width])
     level = jnp.dot(inverse, jnp.concatenate([top_own, top_rows], axis=1), precision=HI).astype(BF16)
     level_own = level[:, :rows]
     level_rows = level[:, rows:]
 
-    def place(t):
-        pairs = []
-        for cs in range(C):
-            for xs in range(X):
-                pairs.append((cs * X + xs, (xs // 2) * X + 2 * cs + ((xs % 2) ^ t)))
-        which = (x % 2) ^ t
-        block = lax.dynamic_slice_in_dim(update, which * rows, rows, 1)
-        return lax.ppermute(block, ("c", "x"), pairs)
-
-    near, far = place(0), place(1)
-    update_own = jnp.concatenate(
-        [jnp.where(even, near, far), jnp.where(even, far, near)], axis=0
-    ).astype(F32)
-
-    schur = separator - update_own
+    schur = separator - update
     outer = lax.dot_general(
         level_rows, level_own, (((0,), (0,)), ((), ())), preferred_element_type=F32
     )

time: 164 us -> 153 us (0.933)
  the two profiles are of different devices: /device:TPU:16 before, /device:TPU:1 now
where the time goes in v5:
time: 153 us
  starting transfers between devices  75.5 us (49%)
  waiting for transfers between devices  53.7 us (35%)
  Pallas kernels  11.4 us (7%)
  matrix products  4.7 us (3%)
  other arithmetic  3.91 us (3%)
  local copies, waits for them, and re-layouts  2.13 us (1%)
    ppermute x10, starting transfers between devices, send(): lax.ppermute(array, ('y', 'x'), [(X * ys + xs, X * yd + xd) for (ys, xs),...  20.8 us
    all_to_all x1, waiting for transfers between devices, body(): lax.all_to_all(top, ('z', 'c'), 0, 0, tiled=True).reshape(width, 5 * rows)  20 us
    all_to_all x2, waiting for transfers between devices, share(): return lax.all_to_all(copies, axis, 0, 0, tiled=True)  18.9 us
    all_to_all x1, starting transfers between devices, body(): lax.all_to_all(part.reshape(Z * C, slab, rows), ('z', 'c'), 0, 0, tiled=T...  13.7 us
    ppermute x4, starting transfers between devices, body(): lax.ppermute(terms[:, k * rows:(k + 1) * rows], ('c', 'x'), pairs)  12.9 us
    pallas_call x1, Pallas kernels, in_vmem(): pl.pallas_call(body, out_shape=[jax.ShapeDtypeStruct(shape, F32) for shap...  11.4 us
    all_to_all x1, starting transfers between devices, body(): lax.all_to_all(top, ('z', 'c'), 0, 0, tiled=True).reshape(width, 5 * rows)  8.49 us
    ppermute x3, starting transfers between devices, body(): lax.ppermute(own, 'x', [(i, (i + k) % X) for i in range(X)])  8.41 us
  transfers between devices with their start and end apart: 22, of which 9 were waited for; matrix products, arithmetic and copies ran while one was open for 3% of the time, Pallas kernels for 7%

profile of v5, /device:TPU:1, one launch (start us, length us, event | category | flops | bytes accessed | tf_op | source)
XLA Modules:
  0.0 152.5 jit_solution(10319686847526405455)
XLA Ops:
  0.6 0.0 copy-start
  0.7 0.8 compare_convert_fusion
  1.4 0.9 convert_reduce_fusion.1
  2.3 1.6 %fusion.1 = bf16[2,128,256]{2,1,0:T(8,128)(2,1)S(1)} fusion(f32[2,128,256]{2,1,0:T(8,128)} %param.5, f32[2,256,256]{2,1,0:T(8,128)S(1)} %copy-done, f32[2,256]{1,0:T(2,128)S(1)} %compare_convert_fusion, f32[2]{0:T(128)S(1)} %convert_reduce_fusion.1), kind=kOutput, calls=%fused_computation.4 | convolution fusion | flops 201523200 | bytes 919560 | tf_op jit(solution)/shard_map/jib,jcb->jic/dot_general | solution.py:135
  3.9 0.0 copy-start.1
  4.0 5.9 %collective-permute-start = (bf16[128,512]{1,0:T(8,128)(2,1)S(1)}, bf16[128,512]{1,0:T(8,128)(2,1)S(1)}, u32[]{:S(2)}, u32[]{:S(2)}) collective-permute-start(bf16[128,512]{1,0:T(8,128)(2,1)S(1)} %pad_maximum_fusion.2), channel_id=1, source_target_pairs={{0,28},{1,29},{32,60},{33,61},{64,92},{65,93},{96,124},{97,125},{1... | collective-permute-start | bytes 393224 | tf_op jit(solution)/shard_map/ppermute | solution.py:143
  9.9 1.5 collective-permute-start.1
  11.4 1.5 collective-permute-start.2
  12.8 1.5 collective-permute-start.3
  14.3 1.3 collective-permute-start.4
  15.6 0.0 collective-permute-done
  15.6 1.3 collective-permute-start.5
  16.9 0.0 collective-permute-done.1
  16.9 1.3 collective-permute-start.6
  18.2 0.0 collective-permute-done.2
  18.2 0.0 collective-permute-done.3
  18.3 0.1 collective-permute-done.4
  18.4 2.8 %collective-permute-done.5 = bf16[128,512]{1,0:T(8,128)(2,1)S(1)} collective-permute-done((bf16[128,512]{1,0:T(8,128)(2,1)S(1)}, bf16[128,512]{1,0:T(8,128)(2,1)S(1)}, u32[]{:S(2)}, u32[]{:S(2)}) %collective-permute-start.5) | collective-permute-done | bytes 131104 | tf_op jit(solution)/shard_map/ppermute | solution.py:143
  21.2 2.8 %collective-permute-done.6 = bf16[128,512]{1,0:T(8,128)(2,1)S(1)} collective-permute-done((bf16[128,512]{1,0:T(8,128)(2,1)S(1)}, bf16[128,512]{1,0:T(8,128)(2,1)S(1)}, u32[]{:S(2)}, u32[]{:S(2)}) %collective-permute-start.6) | collective-permute-done | bytes 131104 | tf_op jit(solution)/shard_map/ppermute | solution.py:143
  24.0 0.1 select_select_fusion.6
  24.1 1.1 broadcast_in_dim.10
  25.2 3.7 %all-to-all-start = ((bf16[8,128,512]{2,1,0:T(8,128)(2,1)}), bf16[8,128,512]{2,1,0:T(8,128)(2,1)S(1)}, u32[]{:S(2)}, u32[]{:S(2)}) async-start(bf16[8,128,512]{2,1,0:T(8,128)(2,1)} %broadcast_in_dim.10), calls=%async_computation | async-start | bytes 2097152 | tf_op jit(solution)/shard_map/all_to_all | solution.py:21
  28.9 4.0 %collective-permute-start.7 = (bf16[128,512]{1,0:T(8,128)(2,1)S(1)}, bf16[128,512]{1,0:T(8,128)(2,1)S(1)}, u32[]{:S(2)}, u32[]{:S(2)}) collective-permute-start(bf16[128,512]{1,0:T(8,128)(2,1)S(1)} %select_select_fusion.6), channel_id=1, source_target_pairs={{0,1},{1,0},{4,5},{5,4},{8,9},{9,8},{12,13},{13,12},{16,17},{17,16... | collective-permute-start | bytes 393224 | tf_op jit(solution)/shard_map/ppermute | solution.py:143
  32.9 1.3 collective-permute-start.8
  34.2 1.3 collective-permute-start.9
  35.6 1.9 %collective-permute-start.10 = (bf16[128,512]{1,0:T(8,128)(2,1)S(1)}, bf16[128,512]{1,0:T(8,128)(2,1)S(1)}, u32[]{:S(2)}, u32[]{:S(2)}) collective-permute-start(bf16[128,512]{1,0:T(8,128)(2,1)S(1)} %pad_maximum_fusion.2), channel_id=1, source_target_pairs={{0,1},{1,2},{2,3},{3,0},{4,5},{5,6},{6,7},{7,4},{8,9},{9,10},{10,1... | collective-permute-start | bytes 393224 | tf_op jit(solution)/shard_map/ppermute | solution.py:162
  37.6 1.9 %collective-permute-start.11 = (bf16[128,512]{1,0:T(8,128)(2,1)S(1)}, bf16[128,512]{1,0:T(8,128)(2,1)S(1)}, u32[]{:S(2)}, u32[]{:S(2)}) collective-permute-start(bf16[128,512]{1,0:T(8,128)(2,1)S(1)} %pad_maximum_fusion.2), channel_id=1, source_target_pairs={{0,2},{1,3},{2,0},{3,1},{4,6},{5,7},{6,4},{7,5},{8,10},{9,11},{10,... | collective-permute-start | bytes 393224 | tf_op jit(solution)/shard_map/ppermute | solution.py:162
  39.5 0.0 collective-permute-done.7
  39.5 4.6 %collective-permute-start.12 = (bf16[128,512]{1,0:T(8,128)(2,1)S(1)}, bf16[128,512]{1,0:T(8,128)(2,1)S(1)}, u32[]{:S(2)}, u32[]{:S(2)}) collective-permute-start(bf16[128,512]{1,0:T(8,128)(2,1)S(1)} %pad_maximum_fusion.2), channel_id=1, source_target_pairs={{0,3},{1,0},{2,1},{3,2},{4,7},{5,4},{6,5},{7,6},{8,11},{9,8},{10,9... | collective-permute-start | bytes 393224 | tf_op jit(solution)/shard_map/ppermute | solution.py:162
  44.1 0.0 collective-permute-done.8
  44.1 0.0 collective-permute-done.9
  44.2 0.9 convolution_subtract_fusion
  45.1 0.0 collective-permute-done.10
  45.1 0.0 collective-permute-done.11
  45.1 2.8 %collective-permute-done.12 = bf16[128,512]{1,0:T(8,128)(2,1)S(1)} collective-permute-done((bf16[128,512]{1,0:T(8,128)(2,1)S(1)}, bf16[128,512]{1,0:T(8,128)(2,1)S(1)}, u32[]{:S(2)}, u32[]{:S(2)}) %collective-permute-start.12) | collective-permute-done | bytes 131104 | tf_op jit(solution)/shard_map/ppermute | solution.py:162
  47.9 8.2 %all-to-all-done = bf16[8,128,512]{2,1,0:T(8,128)(2,1)S(1)} async-done(((bf16[8,128,512]{2,1,0:T(8,128)(2,1)}), bf16[8,128,512]{2,1,0:T(8,128)(2,1)S(1)}, u32[]{:S(2)}, u32[]{:S(2)}) %all-to-all-start) | async-done | bytes 1048608 | tf_op jit(solution)/shard_map/all_to_all | solution.py:21
  56.1 13.7 %all-to-all-start.1 = ((f32[16,16,128]{2,1,0:T(8,128)}), f32[16,16,128]{2,1,0:T(8,128)S(1)}, u32[]{:S(2)}, u32[]{:S(2)}) async-start(f32[16,16,128]{2,1,0:T(8,128)} %bitcast.2), calls=%async_computation.1 | async-start | bytes 262144 | tf_op jit(solution)/shard_map/all_to_all | solution.py:168
  69.7 0.1 select_select_fusion.3
  69.8 0.7 convolution_convert_fusion
  70.5 0.2 fusion.17
  70.7 1.9 %collective-permute-start.13 = (bf16[1024,128]{1,0:T(8,128)(2,1)S(1)}, bf16[1024,128]{1,0:T(8,128)(2,1)S(1)}, u32[]{:S(2)}, u32[]{:S(2)}) collective-permute-start(bf16[1024,128]{1,0:T(8,128)(2,1)S(1)} %get-tuple-element.30), channel_id=1, source_target_pairs={{0,0},{1,1},{2,32},{3,33},{32,2},{33,3},{34,34},{35,35},{4,4},{5,5... | collective-permute-start | bytes 786440 | tf_op jit(solution)/shard_map/ppermute | solution.py:183
  72.6 1.9 %collective-permute-start.14 = (bf16[1024,128]{1,0:T(8,128)(2,1)S(1)}, bf16[1024,128]{1,0:T(8,128)(2,1)S(1)}, u32[]{:S(2)}, u32[]{:S(2)}) collective-permute-start(bf16[1024,128]{1,0:T(8,128)(2,1)S(1)} %get-tuple-element.29), channel_id=1, source_target_pairs={{0,2},{1,3},{2,34},{3,35},{32,0},{33,1},{34,32},{35,33},{4,6},{5,7... | collective-permute-start | bytes 786440 | tf_op jit(solution)/shard_map/ppermute | solution.py:183
  74.6 5.8 %collective-permute-start.15 = (bf16[1024,128]{1,0:T(8,128)(2,1)S(1)}, bf16[1024,128]{1,0:T(8,128)(2,1)S(1)}, u32[]{:S(2)}, u32[]{:S(2)}) collective-permute-start(bf16[1024,128]{1,0:T(8,128)(2,1)S(1)} %get-tuple-element.27), channel_id=1, source_target_pairs={{0,1},{1,0},{2,33},{3,32},{32,3},{33,2},{34,35},{35,34},{4,5},{5,4... | collective-permute-start | bytes 786440 | tf_op jit(solution)/shard_map/ppermute | solution.py:183
  80.4 3.3 %collective-permute-start.16 = (bf16[1024,128]{1,0:T(8,128)(2,1)S(1)}, bf16[1024,128]{1,0:T(8,128)(2,1)S(1)}, u32[]{:S(2)}, u32[]{:S(2)}) collective-permute-start(bf16[1024,128]{1,0:T(8,128)(2,1)S(1)} %get-tuple-element.28), channel_id=1, source_target_pairs={{0,3},{1,2},{2,35},{3,34},{32,1},{33,0},{34,33},{35,32},{4,7},{5,6... | collective-permute-start | bytes 786440 | tf_op jit(solution)/shard_map/ppermute | solution.py:183
  83.7 0.0 all-to-all-done.1
  83.7 0.7 broadcast_in_dim.11
  84.4 3.9 %all-to-all-start.2 = ((f32[32,16,128]{2,1,0:T(8,128)}), f32[32,16,128]{2,1,0:T(8,128)S(1)}, u32[]{:S(2)}, u32[]{:S(2)}) async-start(f32[32,16,128]{2,1,0:T(8,128)} %broadcast_in_dim.11), calls=%async_computation.2 | async-start | bytes 524288 | tf_op jit(solution)/shard_map/all_to_all | solution.py:21
  88.3 0.0 collective-permute-done.13
  88.3 0.0 collective-permute-done.14
  88.3 0.0 collective-permute-done.15
  88.3 0.4 collective-permute-done.16
  88.7 0.2 broadcast_select_fusion.1
  88.9 0.9 pad_maximum_fusion.1
  89.7 10.8 %all-to-all-done.2 = f32[32,16,128]{2,1,0:T(8,128)S(1)} async-done(((f32[32,16,128]{2,1,0:T(8,128)}), f32[32,16,128]{2,1,0:T(8,128)S(1)}, u32[]{:S(2)}, u32[]{:S(2)}) %all-to-all-start.2) | async-done | bytes 262176 | tf_op jit(solution)/shard_map/all_to_all | solution.py:21
  100.6 0.9 pad_maximum_fusion
  101.5 8.5 %all-to-all-start.3 = ((f32[16,16,640]{2,1,0:T(8,128)}), f32[16,16,640]{2,1,0:T(8,128)S(1)}, u32[]{:S(2)}, u32[]{:S(2)}) async-start(f32[16,16,640]{2,1,0:T(8,128)} %pad_maximum_fusion), calls=%async_computation.3 | async-start | bytes 1310720 | tf_op jit(solution)/shard_map/all_to_all | solution.py:193
  110.0 20.0 %all-to-all-done.3 = f32[16,16,640]{2,1,0:T(8,128)S(1)} async-done(((f32[16,16,640]{2,1,0:T(8,128)}), f32[16,16,640]{2,1,0:T(8,128)S(1)}, u32[]{:S(2)}, u32[]{:S(2)}) %all-to-all-start.3) | async-done | bytes 655392 | tf_op jit(solution)/shard_map/all_to_all | solution.py:193
  130.0 3.7 %all-to-all-start.4 = ((bf16[8,256,128]{2,1,0:T(8,128)(2,1)}), bf16[8,256,128]{2,1,0:T(8,128)(2,1)S(1)}, u32[]{:S(2)}, u32[]{:S(2)}) async-start(bf16[8,256,128]{2,1,0:T(8,128)(2,1)} %bitcast.13), calls=%async_computation.4 | async-start | bytes 1048576 | tf_op jit(solution)/shard_map/all_to_all | solution.py:196
  133.7 11.4 %inverse_factor.1 = f32[256,256]{1,0:T(8,128)S(1)} custom-call(f32[256,256]{1,0:T(8,128)S(1)} %slice.44.a_ref), custom_call_target="tpu_custom_call" | custom-call | flops 10000000000 | bytes 1000000 | tf_op jit(solution)/shard_map/inverse_factor/pallas_call | solution.py:118
  145.2 0.6 convolution_convert_fusion.1
  145.8 0.0 copy-start.2
  145.8 5.8 %all-to-all-done.4 = bf16[8,256,128]{2,1,0:T(8,128)(2,1)S(1)} async-done(((bf16[8,256,128]{2,1,0:T(8,128)(2,1)}), bf16[8,256,128]{2,1,0:T(8,128)(2,1)S(1)}, u32[]{:S(2)}, u32[]{:S(2)}) %all-to-all-start.4) | async-done | bytes 524320 | tf_op jit(solution)/shard_map/all_to_all | solution.py:196
  151.6 0.1 convert_reduce_fusion
  151.6 0.9 fusion.2
  (15 shorter events, 0.2 us)
Async XLA Ops:
  0.6 1.7 %copy-start = (f32[2,256,256]{2,1,0:T(8,128)S(1)}, f32[2,256,256]{2,1,0:T(8,128)}, u32[]{:S(2)}) copy-start(f32[2,256,256]{2,1,0:T(8,128)} %param.6) | copy-start | bytes 1572868
  3.9 21.3 %copy-start.1 = (bf16[2,128,256]{2,1,0:T(8,128)(2,1)}, bf16[2,128,256]{2,1,0:T(8,128)(2,1)S(1)}, u32[]{:S(2)}) copy-start(bf16[2,128,256]{2,1,0:T(8,128)(2,1)S(1)} %fusion.1) | copy-start | bytes 393220
  4.0 11.6 %collective-permute-start = (bf16[128,512]{1,0:T(8,128)(2,1)S(1)}, bf16[128,512]{1,0:T(8,128)(2,1)S(1)}, u32[]{:S(2)}, u32[]{:S(2)}) collective-permute-start(bf16[128,512]{1,0:T(8,128)(2,1)S(1)} %pad_maximum_fusion.2), channel_id=1, source_target_pairs={{0,28},{1,29},{32,60},{33,61},{64,92},{65,93},{96,124},{97,125},{1... | collective-permute-start | bytes 393224 | tf_op jit(solution)/shard_map/ppermute | solution.py:143
  9.9 7.0 %collective-permute-start.1 = (bf16[128,512]{1,0:T(8,128)(2,1)S(1)}, bf16[128,512]{1,0:T(8,128)(2,1)S(1)}, u32[]{:S(2)}, u32[]{:S(2)}) collective-permute-start(bf16[128,512]{1,0:T(8,128)(2,1)S(1)} %pad_maximum_fusion.2), channel_id=1, source_target_pairs={{0,24},{1,25},{32,56},{33,57},{64,88},{65,89},{96,120},{97,121},{1... | collective-permute-start | bytes 393224 | tf_op jit(solution)/shard_map/ppermute | solution.py:143
  11.4 6.9 %collective-permute-start.2 = (bf16[128,512]{1,0:T(8,128)(2,1)S(1)}, bf16[128,512]{1,0:T(8,128)(2,1)S(1)}, u32[]{:S(2)}, u32[]{:S(2)}) collective-permute-start(bf16[128,512]{1,0:T(8,128)(2,1)S(1)} %pad_maximum_fusion.2), channel_id=1, source_target_pairs={{0,20},{1,21},{32,52},{33,53},{64,84},{65,85},{96,116},{97,117},{1... | collective-permute-start | bytes 393224 | tf_op jit(solution)/shard_map/ppermute | solution.py:143
  12.8 5.4 %collective-permute-start.3 = (bf16[128,512]{1,0:T(8,128)(2,1)S(1)}, bf16[128,512]{1,0:T(8,128)(2,1)S(1)}, u32[]{:S(2)}, u32[]{:S(2)}) collective-permute-start(bf16[128,512]{1,0:T(8,128)(2,1)S(1)} %pad_maximum_fusion.2), channel_id=1, source_target_pairs={{0,16},{1,17},{32,48},{33,49},{64,80},{65,81},{96,112},{97,113},{1... | collective-permute-start | bytes 393224 | tf_op jit(solution)/shard_map/ppermute | solution.py:143
  14.3 4.1 %collective-permute-start.4 = (bf16[128,512]{1,0:T(8,128)(2,1)S(1)}, bf16[128,512]{1,0:T(8,128)(2,1)S(1)}, u32[]{:S(2)}, u32[]{:S(2)}) collective-permute-start(bf16[128,512]{1,0:T(8,128)(2,1)S(1)} %pad_maximum_fusion.2), channel_id=1, source_target_pairs={{0,12},{1,13},{32,44},{33,45},{64,76},{65,77},{96,108},{97,109},{1... | collective-permute-start | bytes 393224 | tf_op jit(solution)/shard_map/ppermute | solution.py:143
  15.6 5.6 %collective-permute-start.5 = (bf16[128,512]{1,0:T(8,128)(2,1)S(1)}, bf16[128,512]{1,0:T(8,128)(2,1)S(1)}, u32[]{:S(2)}, u32[]{:S(2)}) collective-permute-start(bf16[128,512]{1,0:T(8,128)(2,1)S(1)} %pad_maximum_fusion.2), channel_id=1, source_target_pairs={{0,8},{1,9},{32,40},{33,41},{64,72},{65,73},{96,104},{97,105},{128... | collective-permute-start | bytes 393224 | tf_op jit(solution)/shard_map/ppermute | solution.py:143
  16.9 7.1 %collective-permute-start.6 = (bf16[128,512]{1,0:T(8,128)(2,1)S(1)}, bf16[128,512]{1,0:T(8,128)(2,1)S(1)}, u32[]{:S(2)}, u32[]{:S(2)}) collective-permute-start(bf16[128,512]{1,0:T(8,128)(2,1)S(1)} %pad_maximum_fusion.2), channel_id=1, source_target_pairs={{0,4},{1,5},{32,36},{33,37},{64,68},{65,69},{96,100},{97,101},{128... | collective-permute-start | bytes 393224 | tf_op jit(solution)/shard_map/ppermute | solution.py:143
  25.2 18.9 %copy-start.3 = (f32[256,128]{1,0:T(8,128)S(1)}, f32[256,128]{1,0:T(8,128)}, u32[]{:S(2)}) copy-start(f32[256,128]{1,0:T(8,128)} %param.9) | copy-start | bytes 393220
  25.2 30.8 %all-to-all-start = ((bf16[8,128,512]{2,1,0:T(8,128)(2,1)}), bf16[8,128,512]{2,1,0:T(8,128)(2,1)S(1)}, u32[]{:S(2)}, u32[]{:S(2)}) async-start(bf16[8,128,512]{2,1,0:T(8,128)(2,1)} %broadcast_in_dim.10), calls=%async_computation | async-start | bytes 2097152 | tf_op jit(solution)/shard_map/all_to_all | solution.py:21
  28.9 10.6 %collective-permute-start.7 = (bf16[128,512]{1,0:T(8,128)(2,1)S(1)}, bf16[128,512]{1,0:T(8,128)(2,1)S(1)}, u32[]{:S(2)}, u32[]{:S(2)}) collective-permute-start(bf16[128,512]{1,0:T(8,128)(2,1)S(1)} %select_select_fusion.6), channel_id=1, source_target_pairs={{0,1},{1,0},{4,5},{5,4},{8,9},{9,8},{12,13},{13,12},{16,17},{17,16... | collective-permute-start | bytes 393224 | tf_op jit(solution)/shard_map/ppermute | solution.py:143
  32.9 11.2 %collective-permute-start.8 = (bf16[128,512]{1,0:T(8,128)(2,1)S(1)}, bf16[128,512]{1,0:T(8,128)(2,1)S(1)}, u32[]{:S(2)}, u32[]{:S(2)}) collective-permute-start(bf16[128,512]{1,0:T(8,128)(2,1)S(1)} %select_select_fusion.6), channel_id=1, source_target_pairs={{0,2},{1,3},{4,6},{5,7},{8,10},{9,11},{12,14},{13,15},{16,18},{17,... | collective-permute-start | bytes 393224 | tf_op jit(solution)/shard_map/ppermute | solution.py:143
  34.2 9.9 %collective-permute-start.9 = (bf16[128,512]{1,0:T(8,128)(2,1)S(1)}, bf16[128,512]{1,0:T(8,128)(2,1)S(1)}, u32[]{:S(2)}, u32[]{:S(2)}) collective-permute-start(bf16[128,512]{1,0:T(8,128)(2,1)S(1)} %select_select_fusion.6), channel_id=1, source_target_pairs={{0,3},{1,2},{4,7},{5,6},{8,11},{9,10},{12,15},{13,14},{16,19},{17,... | collective-permute-start | bytes 393224 | tf_op jit(solution)/shard_map/ppermute | solution.py:143
  35.6 9.4 %collective-permute-start.10 = (bf16[128,512]{1,0:T(8,128)(2,1)S(1)}, bf16[128,512]{1,0:T(8,128)(2,1)S(1)}, u32[]{:S(2)}, u32[]{:S(2)}) collective-permute-start(bf16[128,512]{1,0:T(8,128)(2,1)S(1)} %pad_maximum_fusion.2), channel_id=1, source_target_pairs={{0,1},{1,2},{2,3},{3,0},{4,5},{5,6},{6,7},{7,4},{8,9},{9,10},{10,1... | collective-permute-start | bytes 393224 | tf_op jit(solution)/shard_map/ppermute | solution.py:162
  37.6 7.5 %collective-permute-start.11 = (bf16[128,512]{1,0:T(8,128)(2,1)S(1)}, bf16[128,512]{1,0:T(8,128)(2,1)S(1)}, u32[]{:S(2)}, u32[]{:S(2)}) collective-permute-start(bf16[128,512]{1,0:T(8,128)(2,1)S(1)} %pad_maximum_fusion.2), channel_id=1, source_target_pairs={{0,2},{1,3},{2,0},{3,1},{4,6},{5,7},{6,4},{7,5},{8,10},{9,11},{10,... | collective-permute-start | bytes 393224 | tf_op jit(solution)/shard_map/ppermute | solution.py:162
  39.5 8.4 %collective-permute-start.12 = (bf16[128,512]{1,0:T(8,128)(2,1)S(1)}, bf16[128,512]{1,0:T(8,128)(2,1)S(1)}, u32[]{:S(2)}, u32[]{:S(2)}) collective-permute-start(bf16[128,512]{1,0:T(8,128)(2,1)S(1)} %pad_maximum_fusion.2), channel_id=1, source_target_pairs={{0,3},{1,0},{2,1},{3,2},{4,7},{5,4},{6,5},{7,6},{8,11},{9,8},{10,9... | collective-permute-start | bytes 393224 | tf_op jit(solution)/shard_map/ppermute | solution.py:162
  56.1 27.6 %all-to-all-start.1 = ((f32[16,16,128]{2,1,0:T(8,128)}), f32[16,16,128]{2,1,0:T(8,128)S(1)}, u32[]{:S(2)}, u32[]{:S(2)}) async-start(f32[16,16,128]{2,1,0:T(8,128)} %bitcast.2), calls=%async_computation.1 | async-start | bytes 262144 | tf_op jit(solution)/shard_map/all_to_all | solution.py:168
  70.7 17.6 %collective-permute-start.13 = (bf16[1024,128]{1,0:T(8,128)(2,1)S(1)}, bf16[1024,128]{1,0:T(8,128)(2,1)S(1)}, u32[]{:S(2)}, u32[]{:S(2)}) collective-permute-start(bf16[1024,128]{1,0:T(8,128)(2,1)S(1)} %get-tuple-element.30), channel_id=1, source_target_pairs={{0,0},{1,1},{2,32},{3,33},{32,2},{33,3},{34,34},{35,35},{4,4},{5,5... | collective-permute-start | bytes 786440 | tf_op jit(solution)/shard_map/ppermute | solution.py:183
  72.6 15.7 %collective-permute-start.14 = (bf16[1024,128]{1,0:T(8,128)(2,1)S(1)}, bf16[1024,128]{1,0:T(8,128)(2,1)S(1)}, u32[]{:S(2)}, u32[]{:S(2)}) collective-permute-start(bf16[1024,128]{1,0:T(8,128)(2,1)S(1)} %get-tuple-element.29), channel_id=1, source_target_pairs={{0,2},{1,3},{2,34},{3,35},{32,0},{33,1},{34,32},{35,33},{4,6},{5,7... | collective-permute-start | bytes 786440 | tf_op jit(solution)/shard_map/ppermute | solution.py:183
  74.6 13.8 %collective-permute-start.15 = (bf16[1024,128]{1,0:T(8,128)(2,1)S(1)}, bf16[1024,128]{1,0:T(8,128)(2,1)S(1)}, u32[]{:S(2)}, u32[]{:S(2)}) collective-permute-start(bf16[1024,128]{1,0:T(8,128)(2,1)S(1)} %get-tuple-element.27), channel_id=1, source_target_pairs={{0,1},{1,0},{2,33},{3,32},{32,3},{33,2},{34,35},{35,34},{4,5},{5,4... | collective-permute-start | bytes 786440 | tf_op jit(solution)/shard_map/ppermute | solution.py:183
  80.4 8.3 %collective-permute-start.16 = (bf16[1024,128]{1,0:T(8,128)(2,1)S(1)}, bf16[1024,128]{1,0:T(8,128)(2,1)S(1)}, u32[]{:S(2)}, u32[]{:S(2)}) collective-permute-start(bf16[1024,128]{1,0:T(8,128)(2,1)S(1)} %get-tuple-element.28), channel_id=1, source_target_pairs={{0,3},{1,2},{2,35},{3,34},{32,1},{33,0},{34,33},{35,32},{4,7},{5,6... | collective-permute-start | bytes 786440 | tf_op jit(solution)/shard_map/ppermute | solution.py:183
  84.4 16.1 %all-to-all-start.2 = ((f32[32,16,128]{2,1,0:T(8,128)}), f32[32,16,128]{2,1,0:T(8,128)S(1)}, u32[]{:S(2)}, u32[]{:S(2)}) async-start(f32[32,16,128]{2,1,0:T(8,128)} %broadcast_in_dim.11), calls=%async_computation.2 | async-start | bytes 524288 | tf_op jit(solution)/shard_map/all_to_all | solution.py:21
  101.5 28.5 %all-to-all-start.3 = ((f32[16,16,640]{2,1,0:T(8,128)}), f32[16,16,640]{2,1,0:T(8,128)S(1)}, u32[]{:S(2)}, u32[]{:S(2)}) async-start(f32[16,16,640]{2,1,0:T(8,128)} %pad_maximum_fusion), calls=%async_computation.3 | async-start | bytes 1310720 | tf_op jit(solution)/shard_map/all_to_all | solution.py:193
  130.0 21.5 %all-to-all-start.4 = ((bf16[8,256,128]{2,1,0:T(8,128)(2,1)}), bf16[8,256,128]{2,1,0:T(8,128)(2,1)S(1)}, u32[]{:S(2)}, u32[]{:S(2)}) async-start(bf16[8,256,128]{2,1,0:T(8,128)(2,1)} %bitcast.13), calls=%async_computation.4 | async-start | bytes 1048576 | tf_op jit(solution)/shard_map/all_to_all | solution.py:196
  145.8 6.7 %copy-start.2 = (bf16[256,128]{1,0:T(8,128)(2,1)}, bf16[256,128]{1,0:T(8,128)(2,1)S(1)}, u32[]{:S(2)}) copy-start(bf16[256,128]{1,0:T(8,128)(2,1)S(1)} %slice.55) | copy-start | bytes 196612

commit v6 on v5

--- a/solution.py
+++ b/solution.py
@@ -142,11 +142,10 @@
     def send(array, pairs):
         return lax.ppermute(array, ("y", "x"), [(X * ys + xs, X * yd + xd) for (ys, xs), (yd, xd) in pairs])
 
-    block = own
-    for k in range(1, Y):
-        got = send(own, [((0, xs), (k, xs)) for xs in range(2)])
-        block = jnp.where(y == k, got, block)
-    own, block = lax.optimization_barrier((own, block))
+    along_y = share(own, "y", Y)
+    block = along_y[0]
+    shifted = [lax.ppermute(own, "x", [(i, (i + k) % X) for i in range(X)]) for k in range(1, X)]
+    block, *shifted = lax.optimization_barrier((block, *shifted))
     one, two, three = (
         send(block, [((ys, src), (ys, dst)) for ys in range(Y) for src, dst in moves])
         for moves in (((0, 1), (1, 0)), ((0, 2), (1, 3)), ((0, 3), (1, 2)))
@@ -158,15 +157,13 @@
         ],
         axis=0,
     )
-    along_y = share(own, "y", Y)
-    shifted = [lax.ppermute(own, "x", [(i, (i + k) % X) for i in range(X)]) for k in range(1, X)]
-
     slab = width // (Z * C)
     base = jnp.where((z == 0) & (c == 0), separator, jnp.zeros_like(separator))
     part = base - dot_t(first, own)
-    part, along_y, *shifted = lax.optimization_barrier((part, along_y, *shifted))
     pieces = lax.all_to_all(part.reshape(Z * C, slab, rows), ("z", "c"), 0, 0, tiled=True)
     strip = jnp.sum(pieces, axis=0)
+
+    strips = share(strip, ("y", "x"), Y * X)
 
     shifted = [own] + shifted
     cols = []
@@ -177,6 +174,7 @@
             found = jnp.where((x - place) % X == m, shifted[m], found)
         cols.append(found)
     terms = dot_t(along_y.reshape(Y * rows, depth), jnp.concatenate(cols, axis=0)).astype(BF16)
+    strips, terms = lax.optimization_barrier((strips, terms))
     moved = []
     for k in range(X):
         pairs = [(cs * X + xs, (xs // 2) * X + ((2 * cs + xs % 2) ^ k)) for cs in range(C) for xs in range(X)]
@@ -185,11 +183,9 @@
     terms = jnp.stack([jnp.where(even, upper, lower), jnp.where(even, lower, upper)])
     terms = terms.reshape(2, Z, rows, rows).transpose(1, 0, 2, 3).reshape(Z, width, rows)
 
-    strips = share(strip, ("y", "x"), Y * X)
     lead = jnp.concatenate([strips[0], strips[1], strip], axis=1)
     groups = strips.reshape(Z * C, 2, slab, rows).transpose(0, 2, 1, 3).reshape(Z * C, slab, width)
     top = jnp.concatenate([jnp.broadcast_to(lead[None], (Z * C,) + lead.shape), groups], axis=2)
-    top, terms = lax.optimization_barrier((top, terms))
     top = lax.all_to_all(top, ("z", "c"), 0, 0, tiled=True).reshape(width, 5 * rows)
     top, terms = lax.optimization_barrier((top, terms))
     top_own, top_rows = top[:, width:width + rows], top[:, width + rows:]

time: 153 us -> 145 us (0.948)
  starting transfers between devices: 75.5 us -> 67.3 us
    all_to_all x1, waiting for transfers between devices: 20 us -> 0.29 us  [body(): lax.all_to_all(top, ('z', 'c'), 0, 0, tiled=True).reshape(width, 5 * rows)]
    ppermute x10 -> x3, starting transfers between devices: 20.8 us -> 8.63 us  [send(): lax.ppermute(array, ('y', 'x'), [(X * ys + xs, X * yd + xd) for (ys, xs),...]
    all_to_all x1, waiting for transfers between devices: 0.01 us -> 9.04 us  [body(): lax.all_to_all(part.reshape(Z * C, slab, rows), ('z', 'c'), 0, 0, tiled=T...]
    all_to_all x2, waiting for transfers between devices: 18.9 us -> 27.9 us  [share(): return lax.all_to_all(copies, axis, 0, 0, tiled=True)]
    all_to_all x2, starting transfers between devices: 7.56 us -> 12.7 us  [share(): return lax.all_to_all(copies, axis, 0, 0, tiled=True)]
    ppermute x4, waiting for transfers between devices: 0.36 us -> 4.85 us  [body(): lax.ppermute(terms[:, k * rows:(k + 1) * rows], ('c', 'x'), pairs)]
    all_to_all x1, starting transfers between devices: 8.49 us -> 4.94 us  [body(): lax.all_to_all(top, ('z', 'c'), 0, 0, tiled=True).reshape(width, 5 * rows)]
    ppermute x3, waiting for transfers between devices: 2.85 us -> 0.01 us  [body(): lax.ppermute(own, 'x', [(i, (i + k) % X) for i in range(X)])]
  transfers between devices with their start and end apart: 22 -> 15, of which waited for: 9 -> 9; matrix products, arithmetic and copies ran while one was open for 3% -> 2% of each run, Pallas kernels for 7% -> 8%
where the time goes in v6:
time: 145 us; the launch traced here: 144 us
  starting transfers between devices  67.3 us (46%)
  waiting for transfers between devices  53 us (37%)
  Pallas kernels  11.4 us (8%)
  matrix products  4.71 us (3%)
  other arithmetic  3.91 us (3%)
  local copies, waits for them, and re-layouts  2.8 us (2%)
    all_to_all x2, waiting for transfers between devices, share(): return lax.all_to_all(copies, axis, 0, 0, tiled=True)  27.9 us
    ppermute x4, starting transfers between devices, body(): lax.ppermute(terms[:, k * rows:(k + 1) * rows], ('c', 'x'), pairs)  12.9 us
    all_to_all x2, starting transfers between devices, share(): return lax.all_to_all(copies, axis, 0, 0, tiled=True)  12.7 us
    pallas_call x1, Pallas kernels, in_vmem(): pl.pallas_call(body, out_shape=[jax.ShapeDtypeStruct(shape, F32) for shap...  11.4 us
    all_to_all x1, starting transfers between devices, body(): lax.all_to_all(part.reshape(Z * C, slab, rows), ('z', 'c'), 0, 0, tiled=T...  11.1 us
    ppermute x3, starting transfers between devices, body(): lax.ppermute(own, 'x', [(i, (i + k) % X) for i in range(X)])  10.7 us
    all_to_all x1, waiting for transfers between devices, body(): lax.all_to_all(part.reshape(Z * C, slab, rows), ('z', 'c'), 0, 0, tiled=T...  9.04 us
    ppermute x3, starting transfers between devices, send(): lax.ppermute(array, ('y', 'x'), [(X * ys + xs, X * yd + xd) for (ys, xs),...  8.63 us
  transfers between devices with their start and end apart: 15, of which 9 were waited for; matrix products, arithmetic and copies ran while one was open for 2% of the time, Pallas kernels for 8%

profile of v6, /device:TPU:1, one launch (start us, length us, event | category | flops | bytes accessed | tf_op | source)
XLA Modules:
  0.0 144.1 jit_solution(11417549814930217475)
XLA Ops:
  0.6 0.0 copy-start
  0.7 0.8 compare_convert_fusion
  1.4 0.9 convert_reduce_fusion.1
  2.3 0.0 copy-done
  2.3 1.6 %fusion.1 = bf16[2,128,256]{2,1,0:T(8,128)(2,1)S(1)} fusion(f32[2,128,256]{2,1,0:T(8,128)} %param.5, f32[2,256,256]{2,1,0:T(8,128)S(1)} %copy-done, f32[2,256]{1,0:T(2,128)S(1)} %compare_convert_fusion, f32[2]{0:T(128)S(1)} %convert_reduce_fusion.1), kind=kOutput, calls=%fused_computation.4 | convolution fusion | flops 201523200 | bytes 919560 | tf_op jit(solution)/shard_map/jib,jcb->jic/dot_general | solution.py:135
  3.9 0.0 copy-start.1
  4.0 1.1 broadcast_in_dim.10
  5.0 0.0 copy-done.1
  5.0 7.7 %all-to-all-start = ((bf16[8,128,512]{2,1,0:T(8,128)(2,1)}), bf16[8,128,512]{2,1,0:T(8,128)(2,1)S(1)}, u32[]{:S(2)}, u32[]{:S(2)}) async-start(bf16[8,128,512]{2,1,0:T(8,128)(2,1)} %broadcast_in_dim.10), calls=%async_computation | async-start | bytes 2097152 | tf_op jit(solution)/shard_map/all_to_all | solution.py:21
  12.7 0.0 copy-start.3
  12.7 3.3 %collective-permute-start = (bf16[128,512]{1,0:T(8,128)(2,1)S(1)}, bf16[128,512]{1,0:T(8,128)(2,1)S(1)}, u32[]{:S(2)}, u32[]{:S(2)}) collective-permute-start(bf16[128,512]{1,0:T(8,128)(2,1)S(1)} %pad_maximum_fusion.2), channel_id=1, source_target_pairs={{0,1},{1,2},{2,3},{3,0},{4,5},{5,6},{6,7},{7,4},{8,9},{9,10},{10,1... | collective-permute-start | bytes 393224 | tf_op jit(solution)/shard_map/ppermute | solution.py:147
  16.0 4.4 %collective-permute-start.1 = (bf16[128,512]{1,0:T(8,128)(2,1)S(1)}, bf16[128,512]{1,0:T(8,128)(2,1)S(1)}, u32[]{:S(2)}, u32[]{:S(2)}) collective-permute-start(bf16[128,512]{1,0:T(8,128)(2,1)S(1)} %pad_maximum_fusion.2), channel_id=1, source_target_pairs={{0,2},{1,3},{2,0},{3,1},{4,6},{5,7},{6,4},{7,5},{8,10},{9,11},{10,... | collective-permute-start | bytes 393224 | tf_op jit(solution)/shard_map/ppermute | solution.py:147
  20.3 3.1 %collective-permute-start.2 = (bf16[128,512]{1,0:T(8,128)(2,1)S(1)}, bf16[128,512]{1,0:T(8,128)(2,1)S(1)}, u32[]{:S(2)}, u32[]{:S(2)}) collective-permute-start(bf16[128,512]{1,0:T(8,128)(2,1)S(1)} %pad_maximum_fusion.2), channel_id=1, source_target_pairs={{0,3},{1,0},{2,1},{3,2},{4,7},{5,4},{6,5},{7,6},{8,11},{9,8},{10,9... | collective-permute-start | bytes 393224 | tf_op jit(solution)/shard_map/ppermute | solution.py:147
  23.4 16.5 %all-to-all-done = bf16[8,128,512]{2,1,0:T(8,128)(2,1)S(1)} async-done(((bf16[8,128,512]{2,1,0:T(8,128)(2,1)}), bf16[8,128,512]{2,1,0:T(8,128)(2,1)S(1)}, u32[]{:S(2)}, u32[]{:S(2)}) %all-to-all-start) | async-done | bytes 1048608 | tf_op jit(solution)/shard_map/all_to_all | solution.py:21
  39.9 0.0 collective-permute-done
  39.9 0.0 collective-permute-done.1
  39.9 0.0 collective-permute-done.2
  39.9 5.1 %collective-permute-start.3 = (bf16[128,512]{1,0:T(8,128)(2,1)S(1)}, bf16[128,512]{1,0:T(8,128)(2,1)S(1)}, u32[]{:S(2)}, u32[]{:S(2)}) collective-permute-start(bf16[128,512]{1,0:T(8,128)(2,1)S(1)} %slice_bitcast_fusion), channel_id=1, source_target_pairs={{0,1},{1,0},{4,5},{5,4},{8,9},{9,8},{12,13},{13,12},{16,17},{17,16... | collective-permute-start | bytes 393224 | tf_op jit(solution)/shard_map/ppermute | solution.py:143
  45.1 2.2 %collective-permute-start.4 = (bf16[128,512]{1,0:T(8,128)(2,1)S(1)}, bf16[128,512]{1,0:T(8,128)(2,1)S(1)}, u32[]{:S(2)}, u32[]{:S(2)}) collective-permute-start(bf16[128,512]{1,0:T(8,128)(2,1)S(1)} %slice_bitcast_fusion), channel_id=1, source_target_pairs={{0,2},{1,3},{4,6},{5,7},{8,10},{9,11},{12,14},{13,15},{16,18},{17,... | collective-permute-start | bytes 393224 | tf_op jit(solution)/shard_map/ppermute | solution.py:143
  47.3 1.3 collective-permute-start.5
  48.7 0.0 collective-permute-done.3
  48.7 2.0 %collective-permute-done.4 = bf16[128,512]{1,0:T(8,128)(2,1)S(1)} collective-permute-done((bf16[128,512]{1,0:T(8,128)(2,1)S(1)}, bf16[128,512]{1,0:T(8,128)(2,1)S(1)}, u32[]{:S(2)}, u32[]{:S(2)}) %collective-permute-start.4) | collective-permute-done | bytes 131104 | tf_op jit(solution)/shard_map/ppermute | solution.py:143
  50.6 3.0 %collective-permute-done.5 = bf16[128,512]{1,0:T(8,128)(2,1)S(1)} collective-permute-done((bf16[128,512]{1,0:T(8,128)(2,1)S(1)}, bf16[128,512]{1,0:T(8,128)(2,1)S(1)}, u32[]{:S(2)}, u32[]{:S(2)}) %collective-permute-start.5) | collective-permute-done | bytes 131104 | tf_op jit(solution)/shard_map/ppermute | solution.py:143
  53.6 0.0 copy-done.3
  53.6 0.9 convolution_subtract_fusion
  54.5 11.1 %all-to-all-start.1 = ((f32[16,16,128]{2,1,0:T(8,128)}), f32[16,16,128]{2,1,0:T(8,128)S(1)}, u32[]{:S(2)}, u32[]{:S(2)}) async-start(f32[16,16,128]{2,1,0:T(8,128)} %bitcast.3), calls=%async_computation.1 | async-start | bytes 262144 | tf_op jit(solution)/shard_map/all_to_all | solution.py:163
  65.6 0.1 select_select_fusion.3
  65.7 9.0 %all-to-all-done.1 = f32[16,16,128]{2,1,0:T(8,128)S(1)} async-done(((f32[16,16,128]{2,1,0:T(8,128)}), f32[16,16,128]{2,1,0:T(8,128)S(1)}, u32[]{:S(2)}, u32[]{:S(2)}) %all-to-all-start.1) | async-done | bytes 131104 | tf_op jit(solution)/shard_map/all_to_all | solution.py:163
  74.8 0.7 broadcast_in_dim.11
  75.5 5.1 %all-to-all-start.2 = ((f32[32,16,128]{2,1,0:T(8,128)}), f32[32,16,128]{2,1,0:T(8,128)S(1)}, u32[]{:S(2)}, u32[]{:S(2)}) async-start(f32[32,16,128]{2,1,0:T(8,128)} %broadcast_in_dim.11), calls=%async_computation.2 | async-start | bytes 524288 | tf_op jit(solution)/shard_map/all_to_all | solution.py:21
  80.6 0.1 select_select_fusion.2
  80.7 0.7 convolution_convert_fusion
  81.4 11.5 %all-to-all-done.2 = f32[32,16,128]{2,1,0:T(8,128)S(1)} async-done(((f32[32,16,128]{2,1,0:T(8,128)}), f32[32,16,128]{2,1,0:T(8,128)S(1)}, u32[]{:S(2)}, u32[]{:S(2)}) %all-to-all-start.2) | async-done | bytes 262176 | tf_op jit(solution)/shard_map/all_to_all | solution.py:21
  93.0 0.9 pad_maximum_fusion
  93.9 4.9 %all-to-all-start.3 = ((f32[16,16,640]{2,1,0:T(8,128)}), f32[16,16,640]{2,1,0:T(8,128)S(1)}, u32[]{:S(2)}, u32[]{:S(2)}) async-start(f32[16,16,640]{2,1,0:T(8,128)} %pad_maximum_fusion), calls=%async_computation.3 | async-start | bytes 1310720 | tf_op jit(solution)/shard_map/all_to_all | solution.py:189
  98.8 0.9 fusion.17
  99.7 3.3 %collective-permute-start.6 = (bf16[1024,128]{1,0:T(8,128)(2,1)}, bf16[1024,128]{1,0:T(8,128)(2,1)S(1)}, u32[]{:S(2)}, u32[]{:S(2)}) collective-permute-start(bf16[1024,128]{1,0:T(8,128)(2,1)} %get-tuple-element.24), channel_id=1, source_target_pairs={{0,0},{1,1},{2,32},{3,33},{32,2},{33,3},{34,34},{35,35},{4,4},{5,5... | collective-permute-start | bytes 786440 | tf_op jit(solution)/shard_map/ppermute | solution.py:181
  103.0 1.9 %collective-permute-start.7 = (bf16[1024,128]{1,0:T(8,128)(2,1)S(1)}, bf16[1024,128]{1,0:T(8,128)(2,1)S(1)}, u32[]{:S(2)}, u32[]{:S(2)}) collective-permute-start(bf16[1024,128]{1,0:T(8,128)(2,1)S(1)} %get-tuple-element.23), channel_id=1, source_target_pairs={{0,2},{1,3},{2,34},{3,35},{32,0},{33,1},{34,32},{35,33},{4,6},{5,7... | collective-permute-start | bytes 786440 | tf_op jit(solution)/shard_map/ppermute | solution.py:181
  105.0 3.0 %collective-permute-start.8 = (bf16[1024,128]{1,0:T(8,128)(2,1)S(1)}, bf16[1024,128]{1,0:T(8,128)(2,1)S(1)}, u32[]{:S(2)}, u32[]{:S(2)}) collective-permute-start(bf16[1024,128]{1,0:T(8,128)(2,1)S(1)} %get-tuple-element.21), channel_id=1, source_target_pairs={{0,1},{1,0},{2,33},{3,32},{32,3},{33,2},{34,35},{35,34},{4,5},{5,4... | collective-permute-start | bytes 786440 | tf_op jit(solution)/shard_map/ppermute | solution.py:181
  107.9 4.7 %collective-permute-start.9 = (bf16[1024,128]{1,0:T(8,128)(2,1)S(1)}, bf16[1024,128]{1,0:T(8,128)(2,1)S(1)}, u32[]{:S(2)}, u32[]{:S(2)}) collective-permute-start(bf16[1024,128]{1,0:T(8,128)(2,1)S(1)} %get-tuple-element.22), channel_id=1, source_target_pairs={{0,3},{1,2},{2,35},{3,34},{32,1},{33,0},{34,33},{35,32},{4,7},{5,6... | collective-permute-start | bytes 786440 | tf_op jit(solution)/shard_map/ppermute | solution.py:181
  112.6 0.0 collective-permute-done.6
  112.7 0.0 collective-permute-done.7
  112.7 3.5 %collective-permute-done.8 = bf16[1024,128]{1,0:T(8,128)(2,1)S(1)} collective-permute-done((bf16[1024,128]{1,0:T(8,128)(2,1)S(1)}, bf16[1024,128]{1,0:T(8,128)(2,1)S(1)}, u32[]{:S(2)}, u32[]{:S(2)}) %collective-permute-start.8) | collective-permute-done | bytes 262176 | tf_op jit(solution)/shard_map/ppermute | solution.py:181
  116.2 1.3 collective-permute-done.9
  117.5 0.2 broadcast_select_fusion.1
  117.7 0.9 pad_maximum_fusion.1
  118.5 0.3 all-to-all-done.3
  118.9 6.3 %all-to-all-start.4 = ((bf16[8,256,128]{2,1,0:T(8,128)(2,1)}), bf16[8,256,128]{2,1,0:T(8,128)(2,1)S(1)}, u32[]{:S(2)}, u32[]{:S(2)}) async-start(bf16[8,256,128]{2,1,0:T(8,128)(2,1)} %bitcast.15), calls=%async_computation.4 | async-start | bytes 1048576 | tf_op jit(solution)/shard_map/all_to_all | solution.py:192
  125.2 11.4 %inverse_factor.1 = f32[256,256]{1,0:T(8,128)S(1)} custom-call(f32[256,256]{1,0:T(8,128)S(1)} %slice.48.a_ref), custom_call_target="tpu_custom_call" | custom-call | flops 10000000000 | bytes 1000000 | tf_op jit(solution)/shard_map/inverse_factor/pallas_call | solution.py:118
  136.6 0.6 convolution_convert_fusion.1
  137.3 0.0 copy-start.2
  137.3 5.9 %all-to-all-done.4 = bf16[8,256,128]{2,1,0:T(8,128)(2,1)S(1)} async-done(((bf16[8,256,128]{2,1,0:T(8,128)(2,1)}), bf16[8,256,128]{2,1,0:T(8,128)(2,1)S(1)}, u32[]{:S(2)}, u32[]{:S(2)}) %all-to-all-start.4) | async-done | bytes 524320 | tf_op jit(solution)/shard_map/all_to_all | solution.py:192
  143.2 0.1 convert_reduce_fusion
  143.2 0.9 fusion.2
  144.1 0.0 copy-done.2
  (11 shorter events, 0.2 us)
Async XLA Ops:
  0.6 1.7 %copy-start = (f32[2,256,256]{2,1,0:T(8,128)S(1)}, f32[2,256,256]{2,1,0:T(8,128)}, u32[]{:S(2)}) copy-start(f32[2,256,256]{2,1,0:T(8,128)} %param.6) | copy-start | bytes 1572868
  3.9 1.1 copy-start.1
  5.0 34.8 %all-to-all-start = ((bf16[8,128,512]{2,1,0:T(8,128)(2,1)}), bf16[8,128,512]{2,1,0:T(8,128)(2,1)S(1)}, u32[]{:S(2)}, u32[]{:S(2)}) async-start(bf16[8,128,512]{2,1,0:T(8,128)(2,1)} %broadcast_in_dim.10), calls=%async_computation | async-start | bytes 2097152 | tf_op jit(solution)/shard_map/all_to_all | solution.py:21
  12.7 41.0 %copy-start.3 = (f32[256,128]{1,0:T(8,128)S(1)}, f32[256,128]{1,0:T(8,128)}, u32[]{:S(2)}) copy-start(f32[256,128]{1,0:T(8,128)} %param.9) | copy-start | bytes 393220
  12.7 27.2 %collective-permute-start = (bf16[128,512]{1,0:T(8,128)(2,1)S(1)}, bf16[128,512]{1,0:T(8,128)(2,1)S(1)}, u32[]{:S(2)}, u32[]{:S(2)}) collective-permute-start(bf16[128,512]{1,0:T(8,128)(2,1)S(1)} %pad_maximum_fusion.2), channel_id=1, source_target_pairs={{0,1},{1,2},{2,3},{3,0},{4,5},{5,6},{6,7},{7,4},{8,9},{9,10},{10,1... | collective-permute-start | bytes 393224 | tf_op jit(solution)/shard_map/ppermute | solution.py:147
  16.0 23.9 %collective-permute-start.1 = (bf16[128,512]{1,0:T(8,128)(2,1)S(1)}, bf16[128,512]{1,0:T(8,128)(2,1)S(1)}, u32[]{:S(2)}, u32[]{:S(2)}) collective-permute-start(bf16[128,512]{1,0:T(8,128)(2,1)S(1)} %pad_maximum_fusion.2), channel_id=1, source_target_pairs={{0,2},{1,3},{2,0},{3,1},{4,6},{5,7},{6,4},{7,5},{8,10},{9,11},{10,... | collective-permute-start | bytes 393224 | tf_op jit(solution)/shard_map/ppermute | solution.py:147
  20.3 19.6 %collective-permute-start.2 = (bf16[128,512]{1,0:T(8,128)(2,1)S(1)}, bf16[128,512]{1,0:T(8,128)(2,1)S(1)}, u32[]{:S(2)}, u32[]{:S(2)}) collective-permute-start(bf16[128,512]{1,0:T(8,128)(2,1)S(1)} %pad_maximum_fusion.2), channel_id=1, source_target_pairs={{0,3},{1,0},{2,1},{3,2},{4,7},{5,4},{6,5},{7,6},{8,11},{9,8},{10,9... | collective-permute-start | bytes 393224 | tf_op jit(solution)/shard_map/ppermute | solution.py:147
  39.9 8.7 %collective-permute-start.3 = (bf16[128,512]{1,0:T(8,128)(2,1)S(1)}, bf16[128,512]{1,0:T(8,128)(2,1)S(1)}, u32[]{:S(2)}, u32[]{:S(2)}) collective-permute-start(bf16[128,512]{1,0:T(8,128)(2,1)S(1)} %slice_bitcast_fusion), channel_id=1, source_target_pairs={{0,1},{1,0},{4,5},{5,4},{8,9},{9,8},{12,13},{13,12},{16,17},{17,16... | collective-permute-start | bytes 393224 | tf_op jit(solution)/shard_map/ppermute | solution.py:143
  45.1 5.6 %collective-permute-start.4 = (bf16[128,512]{1,0:T(8,128)(2,1)S(1)}, bf16[128,512]{1,0:T(8,128)(2,1)S(1)}, u32[]{:S(2)}, u32[]{:S(2)}) collective-permute-start(bf16[128,512]{1,0:T(8,128)(2,1)S(1)} %slice_bitcast_fusion), channel_id=1, source_target_pairs={{0,2},{1,3},{4,6},{5,7},{8,10},{9,11},{12,14},{13,15},{16,18},{17,... | collective-permute-start | bytes 393224 | tf_op jit(solution)/shard_map/ppermute | solution.py:143
  47.3 6.3 %collective-permute-start.5 = (bf16[128,512]{1,0:T(8,128)(2,1)S(1)}, bf16[128,512]{1,0:T(8,128)(2,1)S(1)}, u32[]{:S(2)}, u32[]{:S(2)}) collective-permute-start(bf16[128,512]{1,0:T(8,128)(2,1)S(1)} %slice_bitcast_fusion), channel_id=1, source_target_pairs={{0,3},{1,2},{4,7},{5,6},{8,11},{9,10},{12,15},{13,14},{16,19},{17,... | collective-permute-start | bytes 393224 | tf_op jit(solution)/shard_map/ppermute | solution.py:143
  54.5 20.2 %all-to-all-start.1 = ((f32[16,16,128]{2,1,0:T(8,128)}), f32[16,16,128]{2,1,0:T(8,128)S(1)}, u32[]{:S(2)}, u32[]{:S(2)}) async-start(f32[16,16,128]{2,1,0:T(8,128)} %bitcast.3), calls=%async_computation.1 | async-start | bytes 262144 | tf_op jit(solution)/shard_map/all_to_all | solution.py:163
  75.5 17.4 %all-to-all-start.2 = ((f32[32,16,128]{2,1,0:T(8,128)}), f32[32,16,128]{2,1,0:T(8,128)S(1)}, u32[]{:S(2)}, u32[]{:S(2)}) async-start(f32[32,16,128]{2,1,0:T(8,128)} %broadcast_in_dim.11), calls=%async_computation.2 | async-start | bytes 524288 | tf_op jit(solution)/shard_map/all_to_all | solution.py:21
  93.9 25.0 %all-to-all-start.3 = ((f32[16,16,640]{2,1,0:T(8,128)}), f32[16,16,640]{2,1,0:T(8,128)S(1)}, u32[]{:S(2)}, u32[]{:S(2)}) async-start(f32[16,16,640]{2,1,0:T(8,128)} %pad_maximum_fusion), calls=%async_computation.3 | async-start | bytes 1310720 | tf_op jit(solution)/shard_map/all_to_all | solution.py:189
  99.7 13.0 %collective-permute-start.6 = (bf16[1024,128]{1,0:T(8,128)(2,1)}, bf16[1024,128]{1,0:T(8,128)(2,1)S(1)}, u32[]{:S(2)}, u32[]{:S(2)}) collective-permute-start(bf16[1024,128]{1,0:T(8,128)(2,1)} %get-tuple-element.24), channel_id=1, source_target_pairs={{0,0},{1,1},{2,32},{3,33},{32,2},{33,3},{34,34},{35,35},{4,4},{5,5... | collective-permute-start | bytes 786440 | tf_op jit(solution)/shard_map/ppermute | solution.py:181
  103.0 9.6 %collective-permute-start.7 = (bf16[1024,128]{1,0:T(8,128)(2,1)S(1)}, bf16[1024,128]{1,0:T(8,128)(2,1)S(1)}, u32[]{:S(2)}, u32[]{:S(2)}) collective-permute-start(bf16[1024,128]{1,0:T(8,128)(2,1)S(1)} %get-tuple-element.23), channel_id=1, source_target_pairs={{0,2},{1,3},{2,34},{3,35},{32,0},{33,1},{34,32},{35,33},{4,6},{5,7... | collective-permute-start | bytes 786440 | tf_op jit(solution)/shard_map/ppermute | solution.py:181
  105.0 11.2 %collective-permute-start.8 = (bf16[1024,128]{1,0:T(8,128)(2,1)S(1)}, bf16[1024,128]{1,0:T(8,128)(2,1)S(1)}, u32[]{:S(2)}, u32[]{:S(2)}) collective-permute-start(bf16[1024,128]{1,0:T(8,128)(2,1)S(1)} %get-tuple-element.21), channel_id=1, source_target_pairs={{0,1},{1,0},{2,33},{3,32},{32,3},{33,2},{34,35},{35,34},{4,5},{5,4... | collective-permute-start | bytes 786440 | tf_op jit(solution)/shard_map/ppermute | solution.py:181
  107.9 9.6 %collective-permute-start.9 = (bf16[1024,128]{1,0:T(8,128)(2,1)S(1)}, bf16[1024,128]{1,0:T(8,128)(2,1)S(1)}, u32[]{:S(2)}, u32[]{:S(2)}) collective-permute-start(bf16[1024,128]{1,0:T(8,128)(2,1)S(1)} %get-tuple-element.22), channel_id=1, source_target_pairs={{0,3},{1,2},{2,35},{3,34},{32,1},{33,0},{34,33},{35,32},{4,7},{5,6... | collective-permute-start | bytes 786440 | tf_op jit(solution)/shard_map/ppermute | solution.py:181
  118.9 24.3 %all-to-all-start.4 = ((bf16[8,256,128]{2,1,0:T(8,128)(2,1)}), bf16[8,256,128]{2,1,0:T(8,128)(2,1)S(1)}, u32[]{:S(2)}, u32[]{:S(2)}) async-start(bf16[8,256,128]{2,1,0:T(8,128)(2,1)} %bitcast.15), calls=%async_computation.4 | async-start | bytes 1048576 | tf_op jit(solution)/shard_map/all_to_all | solution.py:192
  137.3 6.9 %copy-start.2 = (bf16[256,128]{1,0:T(8,128)(2,1)}, bf16[256,128]{1,0:T(8,128)(2,1)S(1)}, u32[]{:S(2)}) copy-start(bf16[256,128]{1,0:T(8,128)(2,1)S(1)} %slice.54) | copy-start | bytes 196612

commit v7 on v6

--- a/solution.py
+++ b/solution.py
@@ -139,54 +139,64 @@
     own = jnp.concatenate([panels[j] for j in range(count)], axis=1)
     depth = own.shape[1]
 
-    def send(array, pairs):
-        return lax.ppermute(array, ("y", "x"), [(X * ys + xs, X * yd + xd) for (ys, xs), (yd, xd) in pairs])
-
     along_y = share(own, "y", Y)
-    block = along_y[0]
-    shifted = [lax.ppermute(own, "x", [(i, (i + k) % X) for i in range(X)]) for k in range(1, X)]
-    block, *shifted = lax.optimization_barrier((block, *shifted))
-    one, two, three = (
-        send(block, [((ys, src), (ys, dst)) for ys in range(Y) for src, dst in moves])
-        for moves in (((0, 1), (1, 0)), ((0, 2), (1, 3)), ((0, 3), (1, 2)))
-    )
-    first = jnp.concatenate(
-        [
-            jnp.where(x == 0, block, jnp.where(x == 1, one, jnp.where(x == 2, two, three))),
-            jnp.where(x == 1, block, jnp.where(x == 0, one, jnp.where(x == 3, two, three))),
-        ],
-        axis=0,
-    )
-    slab = width // (Z * C)
-    base = jnp.where((z == 0) & (c == 0), separator, jnp.zeros_like(separator))
-    part = base - dot_t(first, own)
-    pieces = lax.all_to_all(part.reshape(Z * C, slab, rows), ("z", "c"), 0, 0, tiled=True)
+    shifted = [own] + [lax.ppermute(own, "x", [(i, (i + k) % X) for i in range(X)]) for k in range(1, X)]
+
+    def choose(blocks, place):
+        found = blocks[0]
+        for k in range(1, X):
+            found = jnp.where((x - place) % X == k, blocks[k], found)
+        return found
+
+    def gather_base(*moves):
+        rows_of = separator[:rows], separator[rows:]
+        to_lower = jnp.zeros((), bool)
+        for src, dst in moves:
+            to_lower |= (x == src) & (dst == 1)
+        pairs = [(X * ys + src, X * ys + dst) for ys in range(Y) for src, dst in moves]
+        return lax.ppermute(jnp.where(to_lower, rows_of[1], rows_of[0]), ("z", "c", "y", "x"), pairs)
+
+    swap, two, three = gather_base((0, 1), (1, 0)), gather_base((2, 0), (3, 1)), gather_base((3, 0), (2, 1))
+    mine = jnp.where(even, separator[:rows], separator[rows:])
+    base = [
+        jnp.where(even, mine, swap),
+        jnp.where(even, swap, mine),
+        jnp.where(even, two, three),
+        jnp.where(even, three, two),
+    ]
+    base = jnp.concatenate(base, axis=1)
+    base = jnp.where((z == 0) & (c == 0) & (x < 2), base, jnp.zeros_like(base))
+    block, base, *shifted = lax.optimization_barrier((along_y[0], base, *shifted))
+    cols = [choose(shifted, place) for place in range(X)]
+
+    strip_rows = rows // (Z * C)
+    part = base - dot_t(block, jnp.concatenate(cols, axis=0))
+    pieces = lax.all_to_all(part.reshape(Z * C, strip_rows, X * rows), ("z", "c"), 0, 0, tiled=True)
     strip = jnp.sum(pieces, axis=0)
-
-    strips = share(strip, ("y", "x"), Y * X)
-
-    shifted = [own] + shifted
-    cols = []
-    for k in range(X):
-        place = (2 * c + x % 2) ^ k
-        found = shifted[0]
-        for m in range(1, X):
-            found = jnp.where((x - place) % X == m, shifted[m], found)
-        cols.append(found)
-    terms = dot_t(along_y.reshape(Y * rows, depth), jnp.concatenate(cols, axis=0)).astype(BF16)
+    strips = share(strip, ("y", "x"), Y * X).reshape(Y, X, strip_rows, X, rows)[:, :2]
+
+    row_blocks = along_y.reshape(Y * rows, depth)
+    theirs = jnp.concatenate([choose(shifted, 2 - 2 * c), choose(shifted, 3 - 2 * c)], axis=0)
+    mine = jnp.concatenate([choose(shifted, 2 * c), choose(shifted, 2 * c + 1)], axis=0)
+    sent = lax.ppermute(dot_t(row_blocks, theirs).astype(BF16), "c", [(0, 1), (1, 0)])
+    terms = (dot_t(row_blocks, mine) + sent.astype(F32)).astype(BF16)
     strips, terms = lax.optimization_barrier((strips, terms))
-    moved = []
-    for k in range(X):
-        pairs = [(cs * X + xs, (xs // 2) * X + ((2 * cs + xs % 2) ^ k)) for cs in range(C) for xs in range(X)]
-        moved.append(lax.ppermute(terms[:, k * rows:(k + 1) * rows], ("c", "x"), pairs).astype(F32))
-    upper, lower = (moved[0] + moved[2]).astype(BF16), (moved[1] + moved[3]).astype(BF16)
-    terms = jnp.stack([jnp.where(even, upper, lower), jnp.where(even, lower, upper)])
-    terms = terms.reshape(2, Z, rows, rows).transpose(1, 0, 2, 3).reshape(Z, width, rows)
-
-    lead = jnp.concatenate([strips[0], strips[1], strip], axis=1)
-    groups = strips.reshape(Z * C, 2, slab, rows).transpose(0, 2, 1, 3).reshape(Z * C, slab, width)
-    top = jnp.concatenate([jnp.broadcast_to(lead[None], (Z * C,) + lead.shape), groups], axis=2)
-    top = lax.all_to_all(top, ("z", "c"), 0, 0, tiled=True).reshape(width, 5 * rows)
+
+    def place(k):
+        pairs = [(cs * X + xs, (xs // 2) * X + 2 * cs + ((xs % 2) ^ k)) for cs in range(C) for xs in range(X)]
+        block = jnp.where((x % 2) ^ k == 0, terms[:, :rows], terms[:, rows:])
+        return lax.ppermute(block, ("c", "x"), pairs).reshape(Z, rows, rows)
+
+    near, far = place(0), place(1)
+    terms = jnp.concatenate([jnp.where(even, near, far), jnp.where(even, far, near)], axis=1)
+
+    wide = strips.transpose(0, 3, 1, 2, 4)
+    lead = jnp.concatenate([wide[0, 0], wide[0, 1], wide[y, x]], axis=2)
+    lead = jnp.broadcast_to(lead[None], (Z * C,) + lead.shape)
+    wide = wide.reshape(Z * C, 2, 2, strip_rows, rows)
+    top = jnp.concatenate([lead, wide[:, 0], wide[:, 1]], axis=3).reshape(Z * C, 2 * strip_rows, 5 * rows)
+    top = lax.all_to_all(top, ("z", "c"), 0, 0, tiled=True)
+    top = top.reshape(Z * C, 2, strip_rows, 5 * rows).transpose(1, 0, 2, 3).reshape(width, 5 * rows)
     top, terms = lax.optimization_barrier((top, terms))
     top_own, top_rows = top[:, width:width + rows], top[:, width + rows:]
     update = jnp.sum(lax.all_to_all(terms, "z", 0, 0, tiled=True).astype(F32), axis=0)

time: 145 us -> 137 us (0.945)
  starting transfers between devices: 67.3 us -> 41.9 us
  blocking collectives: 0 us -> 24.3 us
  waiting for transfers between devices: 53 us -> 43.3 us
  local copies, waits for them, and re-layouts: 2.8 us -> 4.98 us
  matrix products: 4.71 us -> 6.16 us
  other arithmetic: 3.91 us -> 2.46 us
    all_to_all x0 -> x1, blocking collectives: none -> 24.3 us  [body(): lax.all_to_all(part.reshape(Z * C, strip_rows, X * rows), ('z', 'c'), 0,...]
    all_to_all x2 -> x1, starting transfers between devices: 16 us -> 3.94 us  [body(): top = lax.all_to_all(top, ('z', 'c'), 0, 0, tiled=True)]
    ppermute x7 -> x6, starting transfers between devices: 21.5 us -> 11.7 us  [the longest x2 7.85 us: place(): return lax.ppermute(block, ('c', 'x'), pairs).reshape(Z, rows, rows)]
    all_to_all x2 -> x1, waiting for transfers between devices: 9.33 us -> 4.94 us  [body(): top = lax.all_to_all(top, ('z', 'c'), 0, 0, tiled=True)]
    all_to_all x2, waiting for transfers between devices: 27.9 us -> 24 us  [share(): return lax.all_to_all(copies, axis, 0, 0, tiled=True)]
    all_to_all x1, starting transfers between devices: 6.34 us -> 3.5 us  [body(): lax.all_to_all(terms, 'z', 0, 0, tiled=True).astype(F32)]
    unnamed x8 -> x14, local copies, waits for them, and re-layouts: 0.03 us -> 2.84 us
    dot_general x2 -> x3, matrix products: 1.64 us -> 3.09 us  [dot_t(): lax.dot_general(a, b, (((1,), (1,)), ((), ())), preferred_element_type=out)]
  transfers between devices with their start and end apart: 15 -> 13, of which waited for: 9 -> 7; matrix products, arithmetic and copies ran while one was open for 2% -> 3% of each run, Pallas kernels for 8% -> 8%
where the time goes in v7:
time: 137 us; the launch traced here: 136 us
  waiting for transfers between devices  43.3 us (32%)
  starting transfers between devices  41.9 us (31%)
  blocking collectives  24.3 us (18%)
  Pallas kernels  11.4 us (8%)
  matrix products  6.16 us (4%)
  local copies, waits for them, and re-layouts  4.98 us (4%)
  other arithmetic  2.46 us (2%)
    all_to_all x1, blocking collectives, body(): lax.all_to_all(part.reshape(Z * C, strip_rows, X * rows), ('z', 'c'), 0,...  24.3 us
    all_to_all x2, waiting for transfers between devices, share(): return lax.all_to_all(copies, axis, 0, 0, tiled=True)  24 us
    all_to_all x2, starting transfers between devices, share(): return lax.all_to_all(copies, axis, 0, 0, tiled=True)  12.2 us
    pallas_call x1, Pallas kernels, in_vmem(): pl.pallas_call(body, out_shape=[jax.ShapeDtypeStruct(shape, F32) for shap...  11.4 us
    ppermute x3, starting transfers between devices, body(): lax.ppermute(own, 'x', [(i, (i + k) % X) for i in range(X)])  10.5 us
    ppermute x2, starting transfers between devices, place(): return lax.ppermute(block, ('c', 'x'), pairs).reshape(Z, rows, rows)  7.85 us
    ppermute x2, waiting for transfers between devices, place(): return lax.ppermute(block, ('c', 'x'), pairs).reshape(Z, rows, rows)  6.28 us
    all_to_all x1, waiting for transfers between devices, body(): lax.all_to_all(terms, 'z', 0, 0, tiled=True).astype(F32)  5.94 us
  transfers between devices with their start and end apart: 13, of which 7 were waited for; matrix products, arithmetic and copies ran while one was open for 3% of the time, Pallas kernels for 8%

profile of v7, /device:TPU:1, one launch (start us, length us, event | category | flops | bytes accessed | tf_op | source)
XLA Modules:
  0.0 135.8 jit_solution(5384271420665028393)
XLA Ops:
  0.6 0.0 copy-start
  0.7 0.0 copy-start.5
  0.7 0.7 copy-done.5
  1.4 0.1 compare_convert_fusion
  1.4 0.0 copy-start.4
  1.4 0.7 copy-done.4
  2.1 0.2 convert_reduce_fusion.1
  2.3 0.0 copy-done
  2.3 1.6 %fusion.1 = bf16[2,128,256]{2,1,0:T(8,128)(2,1)S(1)} fusion(f32[2,128,256]{2,1,0:T(8,128)} %param.5, f32[2,256,256]{2,1,0:T(8,128)S(1)} %copy-done, f32[2,256]{1,0:T(2,128)S(1)} %compare_convert_fusion, f32[2]{0:T(128)S(1)} %convert_reduce_fusion.1), kind=kOutput, calls=%fused_computation.4 | convolution fusion | flops 201523200 | bytes 919560 | tf_op jit(solution)/shard_map/jib,jcb->jic/dot_general | solution.py:135
  3.9 0.0 copy-start.2
  3.9 0.6 copy-done.2
  4.6 1.1 broadcast_in_dim.11
  5.7 0.0 copy-start.1
  5.7 7.8 %all-to-all-start = ((bf16[8,128,512]{2,1,0:T(8,128)(2,1)}), bf16[8,128,512]{2,1,0:T(8,128)(2,1)S(1)}, u32[]{:S(2)}, u32[]{:S(2)}) async-start(bf16[8,128,512]{2,1,0:T(8,128)(2,1)} %broadcast_in_dim.11), calls=%async_computation | async-start | bytes 2097152 | tf_op jit(solution)/shard_map/all_to_all | solution.py:21
  13.4 0.0 copy-done.1
  13.5 0.7 collective-permute-start
  14.2 0.0 collective-permute-done
  14.2 0.7 collective-permute-start.1
  14.9 0.7 collective-permute-start.2
  15.5 3.1 %collective-permute-start.3 = (bf16[128,512]{1,0:T(8,128)(2,1)S(1)}, bf16[128,512]{1,0:T(8,128)(2,1)S(1)}, u32[]{:S(2)}, u32[]{:S(2)}) collective-permute-start(bf16[128,512]{1,0:T(8,128)(2,1)S(1)} %pad_maximum_fusion.2), channel_id=1, source_target_pairs={{0,1},{1,2},{2,3},{3,0},{4,5},{5,6},{6,7},{7,4},{8,9},{9,10},{10,1... | collective-permute-start | bytes 393224 | tf_op jit(solution)/shard_map/ppermute | solution.py:143
  18.7 4.4 %collective-permute-start.4 = (bf16[128,512]{1,0:T(8,128)(2,1)S(1)}, bf16[128,512]{1,0:T(8,128)(2,1)S(1)}, u32[]{:S(2)}, u32[]{:S(2)}) collective-permute-start(bf16[128,512]{1,0:T(8,128)(2,1)S(1)} %pad_maximum_fusion.2), channel_id=1, source_target_pairs={{0,2},{1,3},{2,0},{3,1},{4,6},{5,7},{6,4},{7,5},{8,10},{9,11},{10,... | collective-permute-start | bytes 393224 | tf_op jit(solution)/shard_map/ppermute | solution.py:143
  23.0 3.1 %collective-permute-start.5 = (bf16[128,512]{1,0:T(8,128)(2,1)S(1)}, bf16[128,512]{1,0:T(8,128)(2,1)S(1)}, u32[]{:S(2)}, u32[]{:S(2)}) collective-permute-start(bf16[128,512]{1,0:T(8,128)(2,1)S(1)} %pad_maximum_fusion.2), channel_id=1, source_target_pairs={{0,3},{1,0},{2,1},{3,2},{4,7},{5,4},{6,5},{7,6},{8,11},{9,8},{10,9... | collective-permute-start | bytes 393224 | tf_op jit(solution)/shard_map/ppermute | solution.py:143
  26.3 0.0 collective-permute-done.1
  26.3 0.0 collective-permute-done.2
  26.4 14.3 %all-to-all-done = bf16[8,128,512]{2,1,0:T(8,128)(2,1)S(1)} async-done(((bf16[8,128,512]{2,1,0:T(8,128)(2,1)}), bf16[8,128,512]{2,1,0:T(8,128)(2,1)S(1)}, u32[]{:S(2)}, u32[]{:S(2)}) %all-to-all-start) | async-done | bytes 1048608 | tf_op jit(solution)/shard_map/all_to_all | solution.py:21
  40.6 0.0 collective-permute-done.3
  40.6 0.0 collective-permute-done.4
  40.7 0.0 collective-permute-done.5
  40.7 0.1 select_select_fusion.7
  40.7 0.1 select_select_fusion.3
  40.8 0.3 fusion.3
  41.2 24.3 %all_to_all.25 = f32[16,8,512]{2,1,0:T(8,128)S(1)} all-to-all(f32[16,8,512]{2,1,0:T(8,128)S(1)} %subtract_bitcast_fusion), channel_id=1, replica_groups=mesh['z'=8,'c'=2,'y'=8,'x'=4] {'z','c'}, dimensions={0} | all-to-all | bytes 524288 | tf_op jit(solution)/shard_map/all_to_all | solution.py:174
  65.5 0.9 broadcast_in_dim.13
  66.4 4.4 %all-to-all-start.2 = ((f32[32,8,512]{2,1,0:T(8,128)}), f32[32,8,512]{2,1,0:T(8,128)S(1)}, u32[]{:S(2)}, u32[]{:S(2)}) async-start(f32[32,8,512]{2,1,0:T(8,128)} %broadcast_in_dim.13), calls=%async_computation.2 | async-start | bytes 1048576 | tf_op jit(solution)/shard_map/all_to_all | solution.py:21
  70.8 1.3 convolution_convert_fusion
  72.1 1.9 %collective-permute-start.6 = (bf16[1024,256]{1,0:T(8,128)(2,1)}, bf16[1024,256]{1,0:T(8,128)(2,1)S(1)}, u32[]{:S(2)}, u32[]{:S(2)}) collective-permute-start(bf16[1024,256]{1,0:T(8,128)(2,1)} %convolution_convert_fusion), channel_id=1, source_target_pairs={{0,32},{32,0},{1,33},{33,1},{2,34},{34,2},{3,35},{35,3},{4,36},{36... | collective-permute-start | bytes 1572872 | tf_op jit(solution)/shard_map/ppermute | solution.py:181
  74.0 2.1 %collective-permute-done.6 = bf16[1024,256]{1,0:T(8,128)(2,1)S(1)} collective-permute-done((bf16[1024,256]{1,0:T(8,128)(2,1)}, bf16[1024,256]{1,0:T(8,128)(2,1)S(1)}, u32[]{:S(2)}, u32[]{:S(2)}) %collective-permute-start.6) | collective-permute-done | bytes 524320 | tf_op jit(solution)/shard_map/ppermute | solution.py:181
  76.1 0.0 copy-start.6
  76.1 0.8 copy-done.6
  76.9 1.5 %add_convert_fusion = bf16[1024,256]{1,0:T(8,128)(2,1)S(1)} fusion(bf16[1024,256]{1,0:T(8,128)(2,1)} %copy-done.6, bf16[1024,512]{1,0:T(8,128)(2,1)S(1)} %bitcast.39, bf16[128,512]{1,0:T(8,128)(2,1)S(1)} %get-tuple-element.30, bf16[128,512]{1,0:T(8,128)(2,1)S(1)} %get-tuple-element.27), kind=kOutput, calls=%fused_computation.8 | convolution fusion | flops 269746176 | bytes 2359296 | tf_op jit(solution)/shard_map/dot_general | solution.py:16
  78.4 9.8 %all-to-all-done.2 = f32[32,8,512]{2,1,0:T(8,128)S(1)} async-done(((f32[32,8,512]{2,1,0:T(8,128)}), f32[32,8,512]{2,1,0:T(8,128)S(1)}, u32[]{:S(2)}, u32[]{:S(2)}) %all-to-all-start.2) | async-done | bytes 524320 | tf_op jit(solution)/shard_map/all_to_all | solution.py:21
  88.4 0.9 pad_maximum_fusion
  89.3 3.9 %all-to-all-start.3 = ((f32[16,16,640]{2,1,0:T(8,128)}), f32[16,16,640]{2,1,0:T(8,128)S(1)}, u32[]{:S(2)}, u32[]{:S(2)}) async-start(f32[16,16,640]{2,1,0:T(8,128)} %pad_maximum_fusion), calls=%async_computation.3 | async-start | bytes 1310720 | tf_op jit(solution)/shard_map/all_to_all | solution.py:198
  93.3 4.9 %collective-permute-start.7 = (bf16[1024,128]{1,0:T(8,128)(2,1)S(1)}, bf16[1024,128]{1,0:T(8,128)(2,1)S(1)}, u32[]{:S(2)}, u32[]{:S(2)}) collective-permute-start(bf16[1024,128]{1,0:T(8,128)(2,1)S(1)} %get-tuple-element.25), channel_id=1, source_target_pairs={{0,0},{1,1},{2,32},{3,33},{32,2},{33,3},{34,34},{35,35},{4,4},{5,5... | collective-permute-start | bytes 786440 | tf_op jit(solution)/shard_map/ppermute | solution.py:188
  98.2 3.0 %collective-permute-start.8 = (bf16[1024,128]{1,0:T(8,128)(2,1)S(1)}, bf16[1024,128]{1,0:T(8,128)(2,1)S(1)}, u32[]{:S(2)}, u32[]{:S(2)}) collective-permute-start(bf16[1024,128]{1,0:T(8,128)(2,1)S(1)} %get-tuple-element.26), channel_id=1, source_target_pairs={{0,1},{1,0},{2,33},{3,32},{32,3},{33,2},{34,35},{35,34},{4,5},{5,4... | collective-permute-start | bytes 786440 | tf_op jit(solution)/shard_map/ppermute | solution.py:188
  101.1 3.5 %collective-permute-done.7 = bf16[1024,128]{1,0:T(8,128)(2,1)S(1)} collective-permute-done((bf16[1024,128]{1,0:T(8,128)(2,1)S(1)}, bf16[1024,128]{1,0:T(8,128)(2,1)S(1)}, u32[]{:S(2)}, u32[]{:S(2)}) %collective-permute-start.7) | collective-permute-done | bytes 262176 | tf_op jit(solution)/shard_map/ppermute | solution.py:188
  104.7 2.7 %collective-permute-done.8 = bf16[1024,128]{1,0:T(8,128)(2,1)S(1)} collective-permute-done((bf16[1024,128]{1,0:T(8,128)(2,1)S(1)}, bf16[1024,128]{1,0:T(8,128)(2,1)S(1)}, u32[]{:S(2)}, u32[]{:S(2)}) %collective-permute-start.8) | collective-permute-done | bytes 262176 | tf_op jit(solution)/shard_map/ppermute | solution.py:188
  107.5 0.9 pad_maximum_fusion.1
  108.3 4.9 %all-to-all-done.3 = f32[16,16,640]{2,1,0:T(8,128)S(1)} async-done(((f32[16,16,640]{2,1,0:T(8,128)}), f32[16,16,640]{2,1,0:T(8,128)S(1)}, u32[]{:S(2)}, u32[]{:S(2)}) %all-to-all-start.3) | async-done | bytes 655392 | tf_op jit(solution)/shard_map/all_to_all | solution.py:198
  113.3 3.5 %all-to-all-start.4 = ((bf16[8,256,128]{2,1,0:T(8,128)(2,1)}), bf16[8,256,128]{2,1,0:T(8,128)(2,1)S(1)}, u32[]{:S(2)}, u32[]{:S(2)}) async-start(bf16[8,256,128]{2,1,0:T(8,128)(2,1)} %pad_maximum_fusion.1), calls=%async_computation.4 | async-start | bytes 1048576 | tf_op jit(solution)/shard_map/all_to_all | solution.py:202
  116.8 11.4 %inverse_factor.1 = f32[256,256]{1,0:T(8,128)S(1)} custom-call(f32[256,256]{1,0:T(8,128)S(1)} %slice.68.a_ref), custom_call_target="tpu_custom_call" | custom-call | flops 10000000000 | bytes 1000000 | tf_op jit(solution)/shard_map/inverse_factor/pallas_call | solution.py:118
  128.3 0.6 convolution_convert_fusion.1
  128.9 0.0 copy-start.3
  128.9 5.9 %all-to-all-done.4 = bf16[8,256,128]{2,1,0:T(8,128)(2,1)S(1)} async-done(((bf16[8,256,128]{2,1,0:T(8,128)(2,1)}), bf16[8,256,128]{2,1,0:T(8,128)(2,1)S(1)}, u32[]{:S(2)}, u32[]{:S(2)}) %all-to-all-start.4) | async-done | bytes 524320 | tf_op jit(solution)/shard_map/all_to_all | solution.py:202
  134.9 0.1 convert_reduce_fusion
  134.9 0.0 copy-done.3
  134.9 0.9 fusion.2
  (21 shorter events, 0.4 us)
Async XLA Ops:
  0.6 1.7 %copy-start = (f32[2,256,256]{2,1,0:T(8,128)S(1)}, f32[2,256,256]{2,1,0:T(8,128)}, u32[]{:S(2)}) copy-start(f32[2,256,256]{2,1,0:T(8,128)} %param.6) | copy-start | bytes 1572868
  0.7 0.7 copy-start.5
  1.4 0.7 copy-start.4
  3.9 0.7 copy-start.2
  5.7 7.8 %copy-start.1 = (f32[256,128]{1,0:T(8,128)S(1)}, f32[256,128]{1,0:T(8,128)}, u32[]{:S(2)}) copy-start(f32[256,128]{1,0:T(8,128)} %param.9) | copy-start | bytes 393220
  5.7 35.0 %all-to-all-start = ((bf16[8,128,512]{2,1,0:T(8,128)(2,1)}), bf16[8,128,512]{2,1,0:T(8,128)(2,1)S(1)}, u32[]{:S(2)}, u32[]{:S(2)}) async-start(bf16[8,128,512]{2,1,0:T(8,128)(2,1)} %broadcast_in_dim.11), calls=%async_computation | async-start | bytes 2097152 | tf_op jit(solution)/shard_map/all_to_all | solution.py:21
  13.5 0.7 collective-permute-start
  14.2 12.1 %collective-permute-start.1 = (f32[128,128]{1,0:T(8,128)S(1)}, f32[128,128]{1,0:T(8,128)S(1)}, u32[]{:S(2)}, u32[]{:S(2)}) collective-permute-start(f32[128,128]{1,0:T(8,128)S(1)} %get-tuple-element.41), channel_id=1, source_target_pairs={{2,0},{3,1},{6,4},{7,5},{10,8},{11,9},{14,12},{15,13},{18,16},{19,... | collective-permute-start | bytes 196616 | tf_op jit(solution)/shard_map/ppermute | solution.py:157
  14.9 11.4 %collective-permute-start.2 = (f32[128,128]{1,0:T(8,128)S(1)}, f32[128,128]{1,0:T(8,128)S(1)}, u32[]{:S(2)}, u32[]{:S(2)}) collective-permute-start(f32[128,128]{1,0:T(8,128)S(1)} %get-tuple-element.42), channel_id=1, source_target_pairs={{3,0},{2,1},{7,4},{6,5},{11,8},{10,9},{15,12},{14,13},{19,16},{18,... | collective-permute-start | bytes 196616 | tf_op jit(solution)/shard_map/ppermute | solution.py:157
  15.5 25.1 %collective-permute-start.3 = (bf16[128,512]{1,0:T(8,128)(2,1)S(1)}, bf16[128,512]{1,0:T(8,128)(2,1)S(1)}, u32[]{:S(2)}, u32[]{:S(2)}) collective-permute-start(bf16[128,512]{1,0:T(8,128)(2,1)S(1)} %pad_maximum_fusion.2), channel_id=1, source_target_pairs={{0,1},{1,2},{2,3},{3,0},{4,5},{5,6},{6,7},{7,4},{8,9},{9,10},{10,1... | collective-permute-start | bytes 393224 | tf_op jit(solution)/shard_map/ppermute | solution.py:143
  18.7 22.0 %collective-permute-start.4 = (bf16[128,512]{1,0:T(8,128)(2,1)S(1)}, bf16[128,512]{1,0:T(8,128)(2,1)S(1)}, u32[]{:S(2)}, u32[]{:S(2)}) collective-permute-start(bf16[128,512]{1,0:T(8,128)(2,1)S(1)} %pad_maximum_fusion.2), channel_id=1, source_target_pairs={{0,2},{1,3},{2,0},{3,1},{4,6},{5,7},{6,4},{7,5},{8,10},{9,11},{10,... | collective-permute-start | bytes 393224 | tf_op jit(solution)/shard_map/ppermute | solution.py:143
  23.0 17.6 %collective-permute-start.5 = (bf16[128,512]{1,0:T(8,128)(2,1)S(1)}, bf16[128,512]{1,0:T(8,128)(2,1)S(1)}, u32[]{:S(2)}, u32[]{:S(2)}) collective-permute-start(bf16[128,512]{1,0:T(8,128)(2,1)S(1)} %pad_maximum_fusion.2), channel_id=1, source_target_pairs={{0,3},{1,0},{2,1},{3,2},{4,7},{5,4},{6,5},{7,6},{8,11},{9,8},{10,9... | collective-permute-start | bytes 393224 | tf_op jit(solution)/shard_map/ppermute | solution.py:143
  66.4 21.8 %all-to-all-start.2 = ((f32[32,8,512]{2,1,0:T(8,128)}), f32[32,8,512]{2,1,0:T(8,128)S(1)}, u32[]{:S(2)}, u32[]{:S(2)}) async-start(f32[32,8,512]{2,1,0:T(8,128)} %broadcast_in_dim.13), calls=%async_computation.2 | async-start | bytes 1048576 | tf_op jit(solution)/shard_map/all_to_all | solution.py:21
  72.1 4.0 %collective-permute-start.6 = (bf16[1024,256]{1,0:T(8,128)(2,1)}, bf16[1024,256]{1,0:T(8,128)(2,1)S(1)}, u32[]{:S(2)}, u32[]{:S(2)}) collective-permute-start(bf16[1024,256]{1,0:T(8,128)(2,1)} %convolution_convert_fusion), channel_id=1, source_target_pairs={{0,32},{32,0},{1,33},{33,1},{2,34},{34,2},{3,35},{35,3},{4,36},{36... | collective-permute-start | bytes 1572872 | tf_op jit(solution)/shard_map/ppermute | solution.py:181
  76.1 0.8 copy-start.6
  89.3 24.0 %all-to-all-start.3 = ((f32[16,16,640]{2,1,0:T(8,128)}), f32[16,16,640]{2,1,0:T(8,128)S(1)}, u32[]{:S(2)}, u32[]{:S(2)}) async-start(f32[16,16,640]{2,1,0:T(8,128)} %pad_maximum_fusion), calls=%async_computation.3 | async-start | bytes 1310720 | tf_op jit(solution)/shard_map/all_to_all | solution.py:198
  93.3 11.4 %collective-permute-start.7 = (bf16[1024,128]{1,0:T(8,128)(2,1)S(1)}, bf16[1024,128]{1,0:T(8,128)(2,1)S(1)}, u32[]{:S(2)}, u32[]{:S(2)}) collective-permute-start(bf16[1024,128]{1,0:T(8,128)(2,1)S(1)} %get-tuple-element.25), channel_id=1, source_target_pairs={{0,0},{1,1},{2,32},{3,33},{32,2},{33,3},{34,34},{35,35},{4,4},{5,5... | collective-permute-start | bytes 786440 | tf_op jit(solution)/shard_map/ppermute | solution.py:188
  98.2 9.3 %collective-permute-start.8 = (bf16[1024,128]{1,0:T(8,128)(2,1)S(1)}, bf16[1024,128]{1,0:T(8,128)(2,1)S(1)}, u32[]{:S(2)}, u32[]{:S(2)}) collective-permute-start(bf16[1024,128]{1,0:T(8,128)(2,1)S(1)} %get-tuple-element.26), channel_id=1, source_target_pairs={{0,1},{1,0},{2,33},{3,32},{32,3},{33,2},{34,35},{35,34},{4,5},{5,4... | collective-permute-start | bytes 786440 | tf_op jit(solution)/shard_map/ppermute | solution.py:188
  113.3 21.5 %all-to-all-start.4 = ((bf16[8,256,128]{2,1,0:T(8,128)(2,1)}), bf16[8,256,128]{2,1,0:T(8,128)(2,1)S(1)}, u32[]{:S(2)}, u32[]{:S(2)}) async-start(bf16[8,256,128]{2,1,0:T(8,128)(2,1)} %pad_maximum_fusion.1), calls=%async_computation.4 | async-start | bytes 1048576 | tf_op jit(solution)/shard_map/all_to_all | solution.py:202
  128.9 6.0 %copy-start.3 = (bf16[256,128]{1,0:T(8,128)(2,1)}, bf16[256,128]{1,0:T(8,128)(2,1)S(1)}, u32[]{:S(2)}) copy-start(bf16[256,128]{1,0:T(8,128)(2,1)S(1)} %slice.79) | copy-start | bytes 196612

commit v8 on v7

--- a/solution.py
+++ b/solution.py
@@ -6,6 +6,7 @@
 from jax.sharding import Mesh, PartitionSpec as P
 
 Z, C, Y, X = 8, 2, 8, 4
+GROUP = ("zh", "zl", "c")
 HI = lax.Precision.HIGHEST
 F32 = jnp.float32
 BF16 = jnp.bfloat16
@@ -127,19 +128,63 @@
     )(*args)
 
 
+def leaf_panels(
+    rows_hbm, inverse_hbm, pattern_hbm, widths_hbm, panels_ref, copies_ref,
+    rows_ref, inverse_ref, pattern_ref, widths_ref, sems
+):
+    moves = [
+        pltpu.make_async_copy(src, dst, sems.at[i])
+        for i, (src, dst) in enumerate((
+            (widths_hbm, widths_ref), (pattern_hbm, pattern_ref), (rows_hbm, rows_ref), (inverse_hbm, inverse_ref)
+        ))
+    ]
+    for move in moves:
+        move.start()
+    for move in moves:
+        move.wait()
+    count, rows, width = rows_ref.shape
+    at = 2 * lax.axis_index("y") + lax.div(lax.axis_index("x"), 2)
+    lanes = lax.broadcasted_iota(jnp.int32, (rows, width), 1)
+    for j in range(count):
+        product = lax.dot_general(
+            rows_ref[j], inverse_ref[j], (((1,), (1,)), ((), ())), precision=HI, preferred_element_type=F32
+        )
+        col_mask = (lanes < widths_ref[j]).astype(F32)
+        panel = (product * pattern_ref[j, at].astype(F32) * col_mask).astype(BF16)
+        panels_ref[j] = panel
+        for k in range(copies_ref.shape[0]):
+            copies_ref[k, :, j * width:(j + 1) * width] = panel
+
+
 def body(leaf_rows, leaf_inverse, block_pattern, leaf_widths, separator):
     count, rows, width = leaf_rows.shape
-    z, c, y, x = (lax.axis_index(a) for a in ("z", "c", "y", "x"))
+    zh, zl, c, y, x = (lax.axis_index(a) for a in GROUP + ("y", "x"))
+    z = 2 * zh + zl
     even = x % 2 == 0
 
-    product = jnp.einsum("jib,jcb->jic", leaf_rows, leaf_inverse, precision=HI)
-    row_mask = lax.dynamic_slice_in_dim(block_pattern, 2 * y + x // 2, 1, 1).astype(F32)
-    col_mask = (jnp.arange(width, dtype=jnp.int32)[None, :] < leaf_widths[:, None]).astype(F32)
-    panels = (product * row_mask[:, :, None] * col_mask[:, None, :]).astype(BF16)
-    own = jnp.concatenate([panels[j] for j in range(count)], axis=1)
-    depth = own.shape[1]
-
-    along_y = share(own, "y", Y)
+    depth = count * width
+    anywhere, vmem = pl.BlockSpec(memory_space=pl.ANY), pl.BlockSpec(memory_space=pltpu.VMEM)
+    panels, copies = pl.pallas_call(
+        leaf_panels,
+        out_shape=[
+            jax.ShapeDtypeStruct((count, rows, width), BF16),
+            jax.ShapeDtypeStruct((Y, rows, depth), BF16),
+        ],
+        in_specs=[anywhere] * 4,
+        out_specs=[vmem, vmem],
+        scratch_shapes=[
+            pltpu.VMEM(leaf_rows.shape, F32),
+            pltpu.VMEM(leaf_inverse.shape, F32),
+            pltpu.SMEM(block_pattern.shape, jnp.int32),
+            pltpu.SMEM(leaf_widths.shape, jnp.int32),
+            pltpu.SemaphoreType.DMA((4,)),
+        ],
+        compiler_params=pltpu.CompilerParams(vmem_limit_bytes=56 * 1024 * 1024),
+        name="leaf_panels",
+    )(leaf_rows, leaf_inverse, block_pattern, leaf_widths)
+    own = copies[0]
+
+    along_y = lax.all_to_all(copies, "y", 0, 0, tiled=True)
     shifted = [own] + [lax.ppermute(own, "x", [(i, (i + k) % X) for i in range(X)]) for k in range(1, X)]
 
     def choose(blocks, place):
@@ -154,7 +199,7 @@
         for src, dst in moves:
             to_lower |= (x == src) & (dst == 1)
         pairs = [(X * ys + src, X * ys + dst) for ys in range(Y) for src, dst in moves]
-        return lax.ppermute(jnp.where(to_lower, rows_of[1], rows_of[0]), ("z", "c", "y", "x"), pairs)
+        return lax.ppermute(jnp.where(to_lower, rows_of[1], rows_of[0]), GROUP + ("y", "x"), pairs)
 
     swap, two, three = gather_base((0, 1), (1, 0)), gather_base((2, 0), (3, 1)), gather_base((3, 0), (2, 1))
     mine = jnp.where(even, separator[:rows], separator[rows:])
@@ -171,7 +216,7 @@
 
     strip_rows = rows // (Z * C)
     part = base - dot_t(block, jnp.concatenate(cols, axis=0))
-    pieces = lax.all_to_all(part.reshape(Z * C, strip_rows, X * rows), ("z", "c"), 0, 0, tiled=True)
+    pieces = lax.all_to_all(part.reshape(Z * C, strip_rows, X * rows), GROUP, 0, 0, tiled=True)
     strip = jnp.sum(pieces, axis=0)
     strips = share(strip, ("y", "x"), Y * X).reshape(Y, X, strip_rows, X, rows)[:, :2]
 
@@ -180,12 +225,17 @@
     mine = jnp.concatenate([choose(shifted, 2 * c), choose(shifted, 2 * c + 1)], axis=0)
     sent = lax.ppermute(dot_t(row_blocks, theirs).astype(BF16), "c", [(0, 1), (1, 0)])
     terms = (dot_t(row_blocks, mine) + sent.astype(F32)).astype(BF16)
-    strips, terms = lax.optimization_barrier((strips, terms))
+    blocks = terms.reshape(Z // 2, 2, rows, 2 * rows)
+    give = jnp.where(zl == 0, blocks[:, 1], blocks[:, 0])
+    got = lax.ppermute(give, "zl", [(0, 1), (1, 0)])
+    strips, blocks, got = lax.optimization_barrier((strips, blocks, got))
+    terms = jnp.where(zl == 0, blocks[:, 0], blocks[:, 1]).astype(F32) + got.astype(F32)
+    terms = terms.astype(BF16).reshape(Z // 2 * rows, 2 * rows)
 
     def place(k):
         pairs = [(cs * X + xs, (xs // 2) * X + 2 * cs + ((xs % 2) ^ k)) for cs in range(C) for xs in range(X)]
         block = jnp.where((x % 2) ^ k == 0, terms[:, :rows], terms[:, rows:])
-        return lax.ppermute(block, ("c", "x"), pairs).reshape(Z, rows, rows)
+        return lax.ppermute(block, ("c", "x"), pairs).reshape(Z // 2, rows, rows)
 
     near, far = place(0), place(1)
     terms = jnp.concatenate([jnp.where(even, near, far), jnp.where(even, far, near)], axis=1)
@@ -195,29 +245,29 @@
     lead = jnp.broadcast_to(lead[None], (Z * C,) + lead.shape)
     wide = wide.reshape(Z * C, 2, 2, strip_rows, rows)
     top = jnp.concatenate([lead, wide[:, 0], wide[:, 1]], axis=3).reshape(Z * C, 2 * strip_rows, 5 * rows)
-    top = lax.all_to_all(top, ("z", "c"), 0, 0, tiled=True)
+    top = lax.all_to_all(top, GROUP, 0, 0, tiled=True)
     top = top.reshape(Z * C, 2, strip_rows, 5 * rows).transpose(1, 0, 2, 3).reshape(width, 5 * rows)
     top, terms = lax.optimization_barrier((top, terms))
     top_own, top_rows = top[:, width:width + rows], top[:, width + rows:]
-    update = jnp.sum(lax.all_to_all(terms, "z", 0, 0, tiled=True).astype(F32), axis=0)
+    update = jnp.sum(lax.all_to_all(terms, "zh", 0, 0, tiled=True).astype(F32), axis=0)
 
     (inverse,) = in_vmem(inverse_factor, [(width, width)], (width, 2 * width), "inverse_factor", top[:, :width])
+    inverse, update = lax.optimization_barrier((inverse, update))
     level = jnp.dot(inverse, jnp.concatenate([top_own, top_rows], axis=1), precision=HI).astype(BF16)
     level_own = level[:, :rows]
     level_rows = level[:, rows:]
 
-    schur = separator - update
     outer = lax.dot_general(
         level_rows, level_own, (((0,), (0,)), ((), ())), preferred_element_type=F32
     )
     keep = ((z > 0) | (c > 0)) & ((y > 0) | (x > 1))
-    schur_next = jnp.where(keep, schur - outer, jnp.float32(0.0))
+    schur_next = jnp.where(keep, (separator - update) - outer, jnp.float32(0.0))
     return (panels, level_own, schur_next)
 
 
 def solution(mesh):
-    fine = Mesh(mesh.devices.reshape(Z, C, Y, X), ("z", "c", "y", "x"))
-    grp, rd = ("z", "c"), ("y", "x")
+    fine = Mesh(mesh.devices.reshape(Z // 2, 2, C, Y, X), GROUP + ("y", "x"))
+    grp, rd = GROUP, ("y", "x")
     return jax.shard_map(
         body,
         mesh=fine,

time: 137 us -> 129 us (0.942)
  blocking collectives: 24.3 us -> 0 us
  starting transfers between devices: 41.9 us -> 56.7 us
  waiting for transfers between devices: 43.3 us -> 48.8 us
  matrix products: 6.16 us -> 2.72 us
  local copies, waits for them, and re-layouts: 4.98 us -> 1.97 us
  Pallas kernels: 11.4 us -> 14.3 us
    all_to_all x1 -> x0, blocking collectives: 24.3 us -> none  [body(): lax.all_to_all(part.reshape(Z * C, strip_rows, X * rows), ('z', 'c'), 0,...]
    all_to_all x2 -> x4, starting transfers between devices: 7.45 us -> 28 us  [the longest x1 12.8 us: body(): lax.all_to_all(part.reshape(Z * C, strip_rows, X * rows), GROUP, 0, 0, ti...]
    all_to_all x2 -> x4, waiting for transfers between devices: 10.9 us -> 29 us  [the longest x1 13.3 us: body(): along_y = lax.all_to_all(copies, 'y', 0, 0, tiled=True)]
    all_to_all x2 -> x1, waiting for transfers between devices: 24 us -> 14.9 us  [share(): return lax.all_to_all(copies, axis, 0, 0, tiled=True)]
    all_to_all x2 -> x1, starting transfers between devices: 12.2 us -> 4.41 us  [share(): return lax.all_to_all(copies, axis, 0, 0, tiled=True)]
    pallas_call x0 -> x1, Pallas kernels: none -> 2.9 us  [body(): pl.pallas_call(leaf_panels, out_shape=[jax.ShapeDtypeStruct((count, rows,...]
    unnamed x14 -> x4, local copies, waits for them, and re-layouts: 2.84 us -> 0.01 us
    ppermute x1, waiting for transfers between devices: 2.09 us -> 0.01 us  [body(): lax.ppermute(dot_t(row_blocks, theirs).astype(BF16), 'c', [(0, 1), (1, 0)])]
  transfers between devices with their start and end apart: 13 -> 15, of which waited for: 7 -> 6; matrix products, arithmetic and copies ran while one was open for 3% -> 3% of each run, Pallas kernels for 8% -> 9%
where the time goes in v8:
time: 129 us
  starting transfers between devices  56.7 us (44%)
  waiting for transfers between devices  48.8 us (38%)
  Pallas kernels  14.3 us (11%)
  other arithmetic  2.83 us (2%)
  matrix products  2.72 us (2%)
  local copies, waits for them, and re-layouts  1.97 us (2%)
    all_to_all x1, waiting for transfers between devices, share(): return lax.all_to_all(copies, axis, 0, 0, tiled=True)  14.9 us
    all_to_all x1, waiting for transfers between devices, body(): along_y = lax.all_to_all(copies, 'y', 0, 0, tiled=True)  13.3 us
    all_to_all x1, starting transfers between devices, body(): lax.all_to_all(part.reshape(Z * C, strip_rows, X * rows), GROUP, 0, 0, ti...  12.8 us
    pallas_call x1, Pallas kernels, in_vmem(): pl.pallas_call(body, out_shape=[jax.ShapeDtypeStruct(shape, F32) for shap...  11.4 us
    ppermute x3, starting transfers between devices, body(): lax.ppermute(own, 'x', [(i, (i + k) % X) for i in range(X)])  10.5 us
    all_to_all x1, waiting for transfers between devices, body(): lax.all_to_all(part.reshape(Z * C, strip_rows, X * rows), GROUP, 0, 0, ti...  9.23 us
    ppermute x2, starting transfers between devices, place(): return lax.ppermute(block, ('c', 'x'), pairs).reshape(Z // 2, rows, rows)  7.85 us
    all_to_all x1, starting transfers between devices, body(): along_y = lax.all_to_all(copies, 'y', 0, 0, tiled=True)  7.8 us
  transfers between devices with their start and end apart: 15, of which 6 were waited for; matrix products, arithmetic and copies ran while one was open for 3% of the time, Pallas kernels for 9%

profile of v8, /device:TPU:1, one launch (start us, length us, event | category | flops | bytes accessed | tf_op | source)
XLA Modules:
  0.0 128.6 jit_solution(4837275731157486161)
XLA Ops:
  0.6 2.9 %leaf_panels.1 = (bf16[2,128,256]{2,1,0:T(8,128)(2,1)}, bf16[8,128,512]{2,1,0:T(8,128)(2,1)}) custom-call(f32[2,128,256]{2,1,0:T(8,128)} %rows_hbm.1, f32[2,256,256]{2,1,0:T(8,128)} %inverse_hbm.1, s32[2,16]{1,0:T(2,128)} %pattern_hbm.1, s32[2]{0:T(128)} %widths_hbm.1), custom_call_target="tpu_custom_call" | custom-call | tf_op jit(solution)/shard_map/leaf_panels/pallas_call | solution.py:167
  3.5 0.0 copy-start
  3.5 7.8 %all-to-all-start = ((bf16[8,128,512]{2,1,0:T(8,128)(2,1)}), bf16[8,128,512]{2,1,0:T(8,128)(2,1)S(1)}, u32[]{:S(2)}, u32[]{:S(2)}) async-start(bf16[8,128,512]{2,1,0:T(8,128)(2,1)} %get-tuple-element.19), calls=%async_computation | async-start | bytes 2097152 | tf_op jit(solution)/shard_map/all_to_all | solution.py:187
  11.3 0.0 copy-done
  11.4 0.7 collective-permute-start
  12.1 0.0 collective-permute-done
  12.1 0.7 collective-permute-start.1
  12.8 0.7 collective-permute-start.2
  13.4 0.9 slice_bitcast_fusion.5
  14.4 3.1 %collective-permute-start.3 = (bf16[128,512]{1,0:T(8,128)(2,1)S(1)}, bf16[128,512]{1,0:T(8,128)(2,1)S(1)}, u32[]{:S(2)}, u32[]{:S(2)}) collective-permute-start(bf16[128,512]{1,0:T(8,128)(2,1)S(1)} %slice_bitcast_fusion.5), channel_id=1, source_target_pairs={{0,1},{1,2},{2,3},{3,0},{4,5},{5,6},{6,7},{7,4},{8,9},{9,10},{10,1... | collective-permute-start | bytes 393224 | tf_op jit(solution)/shard_map/ppermute | solution.py:188
  17.5 4.4 %collective-permute-start.4 = (bf16[128,512]{1,0:T(8,128)(2,1)S(1)}, bf16[128,512]{1,0:T(8,128)(2,1)S(1)}, u32[]{:S(2)}, u32[]{:S(2)}) collective-permute-start(bf16[128,512]{1,0:T(8,128)(2,1)S(1)} %slice_bitcast_fusion.5), channel_id=1, source_target_pairs={{0,2},{1,3},{2,0},{3,1},{4,6},{5,7},{6,4},{7,5},{8,10},{9,11},{10,... | collective-permute-start | bytes 393224 | tf_op jit(solution)/shard_map/ppermute | solution.py:188
  21.9 3.1 %collective-permute-start.5 = (bf16[128,512]{1,0:T(8,128)(2,1)S(1)}, bf16[128,512]{1,0:T(8,128)(2,1)S(1)}, u32[]{:S(2)}, u32[]{:S(2)}) collective-permute-start(bf16[128,512]{1,0:T(8,128)(2,1)S(1)} %slice_bitcast_fusion.5), channel_id=1, source_target_pairs={{0,3},{1,0},{2,1},{3,2},{4,7},{5,4},{6,5},{7,6},{8,11},{9,8},{10,9... | collective-permute-start | bytes 393224 | tf_op jit(solution)/shard_map/ppermute | solution.py:188
  25.1 0.0 collective-permute-done.1
  25.1 0.0 collective-permute-done.2
  25.2 13.3 %all-to-all-done = bf16[8,128,512]{2,1,0:T(8,128)(2,1)S(1)} async-done(((bf16[8,128,512]{2,1,0:T(8,128)(2,1)}), bf16[8,128,512]{2,1,0:T(8,128)(2,1)S(1)}, u32[]{:S(2)}, u32[]{:S(2)}) %all-to-all-start) | async-done | bytes 1048608 | tf_op jit(solution)/shard_map/all_to_all | solution.py:187
  38.5 0.0 collective-permute-done.3
  38.6 0.0 collective-permute-done.4
  38.6 0.0 collective-permute-done.5
  38.6 0.1 select_select_fusion.7
  38.6 0.1 select_select_fusion.3
  38.7 0.3 fusion.1
  39.0 0.7 subtract_bitcast_fusion
  39.8 12.8 %all-to-all-start.1 = ((f32[16,8,512]{2,1,0:T(8,128)}), f32[16,8,512]{2,1,0:T(8,128)S(1)}, u32[]{:S(2)}, u32[]{:S(2)}) async-start(f32[16,8,512]{2,1,0:T(8,128)} %subtract_bitcast_fusion), calls=%async_computation.1 | async-start | bytes 524288 | tf_op jit(solution)/shard_map/all_to_all | solution.py:219
  52.6 0.5 convolution_convert_fusion
  53.1 2.0 %collective-permute-start.6 = (bf16[1024,256]{1,0:T(8,128)(2,1)S(1)}, bf16[1024,256]{1,0:T(8,128)(2,1)S(1)}, u32[]{:S(2)}, u32[]{:S(2)}) collective-permute-start(bf16[1024,256]{1,0:T(8,128)(2,1)S(1)} %convolution_convert_fusion), channel_id=1, source_target_pairs={{0,32},{32,0},{1,33},{33,1},{2,34},{34,2},{3,35},{35,3},{4,36},{36... | collective-permute-start | bytes 1572872 | tf_op jit(solution)/shard_map/ppermute | solution.py:226
  55.1 9.2 %all-to-all-done.1 = f32[16,8,512]{2,1,0:T(8,128)S(1)} async-done(((f32[16,8,512]{2,1,0:T(8,128)}), f32[16,8,512]{2,1,0:T(8,128)S(1)}, u32[]{:S(2)}, u32[]{:S(2)}) %all-to-all-start.1) | async-done | bytes 262176 | tf_op jit(solution)/shard_map/all_to_all | solution.py:219
  64.3 0.9 broadcast_in_dim.20
  65.2 4.4 %all-to-all-start.2 = ((f32[32,8,512]{2,1,0:T(8,128)}), f32[32,8,512]{2,1,0:T(8,128)S(1)}, u32[]{:S(2)}, u32[]{:S(2)}) async-start(f32[32,8,512]{2,1,0:T(8,128)} %broadcast_in_dim.20), calls=%async_computation.2 | async-start | bytes 1048576 | tf_op jit(solution)/shard_map/all_to_all | solution.py:22
  69.6 0.0 collective-permute-done.6
  69.6 0.5 add_convert_fusion
  70.1 1.9 %collective-permute-start.7 = (bf16[4,128,256]{2,1,0:T(8,128)(2,1)S(1)}, bf16[4,128,256]{2,1,0:T(8,128)(2,1)S(1)}, u32[]{:S(2)}, u32[]{:S(2)}) collective-permute-start(bf16[4,128,256]{2,1,0:T(8,128)(2,1)S(1)} %fusion.13), channel_id=1, source_target_pairs={{0,64},{64,0},{1,65},{65,1},{2,66},{66,2},{3,67},{67,3},{4,68},{68... | collective-permute-start | bytes 786440 | tf_op jit(solution)/shard_map/ppermute | solution.py:230
  72.1 14.9 %all-to-all-done.2 = f32[32,8,512]{2,1,0:T(8,128)S(1)} async-done(((f32[32,8,512]{2,1,0:T(8,128)}), f32[32,8,512]{2,1,0:T(8,128)S(1)}, u32[]{:S(2)}, u32[]{:S(2)}) %all-to-all-start.2) | async-done | bytes 524320 | tf_op jit(solution)/shard_map/all_to_all | solution.py:22
  87.0 0.0 collective-permute-done.7
  87.2 0.9 pad_maximum_fusion
  88.1 3.9 %all-to-all-start.3 = ((f32[16,16,640]{2,1,0:T(8,128)}), f32[16,16,640]{2,1,0:T(8,128)S(1)}, u32[]{:S(2)}, u32[]{:S(2)}) async-start(f32[16,16,640]{2,1,0:T(8,128)} %pad_maximum_fusion), calls=%async_computation.3 | async-start | bytes 1310720 | tf_op jit(solution)/shard_map/all_to_all | solution.py:248
  92.0 0.1 fusion.9
  92.1 4.9 %collective-permute-start.8 = (bf16[512,128]{1,0:T(8,128)(2,1)S(1)}, bf16[512,128]{1,0:T(8,128)(2,1)S(1)}, u32[]{:S(2)}, u32[]{:S(2)}) collective-permute-start(bf16[512,128]{1,0:T(8,128)(2,1)S(1)} %get-tuple-element.43), channel_id=1, source_target_pairs={{0,0},{1,1},{2,32},{3,33},{32,2},{33,3},{34,34},{35,35},{4,4},{5,5... | collective-permute-start | bytes 393224 | tf_op jit(solution)/shard_map/ppermute | solution.py:238
  97.0 3.0 %collective-permute-start.9 = (bf16[512,128]{1,0:T(8,128)(2,1)S(1)}, bf16[512,128]{1,0:T(8,128)(2,1)S(1)}, u32[]{:S(2)}, u32[]{:S(2)}) collective-permute-start(bf16[512,128]{1,0:T(8,128)(2,1)S(1)} %get-tuple-element.44), channel_id=1, source_target_pairs={{0,1},{1,0},{2,33},{3,32},{32,3},{33,2},{34,35},{35,34},{4,5},{5,4... | collective-permute-start | bytes 393224 | tf_op jit(solution)/shard_map/ppermute | solution.py:238
  100.0 0.7 collective-permute-done.8
  100.8 4.1 %collective-permute-done.9 = bf16[512,128]{1,0:T(8,128)(2,1)S(1)} collective-permute-done((bf16[512,128]{1,0:T(8,128)(2,1)S(1)}, bf16[512,128]{1,0:T(8,128)(2,1)S(1)}, u32[]{:S(2)}, u32[]{:S(2)}) %collective-permute-start.9) | collective-permute-done | bytes 131104 | tf_op jit(solution)/shard_map/ppermute | solution.py:238
  104.9 0.7 pad_maximum_fusion.1
  105.6 6.5 %all-to-all-done.3 = f32[16,16,640]{2,1,0:T(8,128)S(1)} async-done(((f32[16,16,640]{2,1,0:T(8,128)}), f32[16,16,640]{2,1,0:T(8,128)S(1)}, u32[]{:S(2)}, u32[]{:S(2)}) %all-to-all-start.3) | async-done | bytes 655392 | tf_op jit(solution)/shard_map/all_to_all | solution.py:248
  112.1 3.4 %all-to-all-start.4 = ((bf16[4,256,128]{2,1,0:T(8,128)(2,1)}), bf16[4,256,128]{2,1,0:T(8,128)(2,1)S(1)}, u32[]{:S(2)}, u32[]{:S(2)}) async-start(bf16[4,256,128]{2,1,0:T(8,128)(2,1)} %pad_maximum_fusion.1), calls=%async_computation.4 | async-start | bytes 524288 | tf_op jit(solution)/shard_map/all_to_all | solution.py:252
  115.6 11.4 %inverse_factor.1 = f32[256,256]{1,0:T(8,128)S(1)} custom-call(f32[256,256]{1,0:T(8,128)S(1)} %slice.80.a_ref), custom_call_target="tpu_custom_call" | custom-call | flops 10000000000 | bytes 1000000 | tf_op jit(solution)/shard_map/inverse_factor/pallas_call | solution.py:119
  127.0 0.0 all-to-all-done.4
  127.0 0.6 convolution_convert_fusion.1
  127.7 0.0 copy-start.1
  127.7 0.9 fusion
  128.6 0.0 copy-done.1
  (20 shorter events, 0.4 us)
Async XLA Ops:
  3.5 7.8 %copy-start = (f32[256,128]{1,0:T(8,128)S(1)}, f32[256,128]{1,0:T(8,128)}, u32[]{:S(2)}) copy-start(f32[256,128]{1,0:T(8,128)} %param.9) | copy-start | bytes 393220
  3.5 35.0 %all-to-all-start = ((bf16[8,128,512]{2,1,0:T(8,128)(2,1)}), bf16[8,128,512]{2,1,0:T(8,128)(2,1)S(1)}, u32[]{:S(2)}, u32[]{:S(2)}) async-start(bf16[8,128,512]{2,1,0:T(8,128)(2,1)} %get-tuple-element.19), calls=%async_computation | async-start | bytes 2097152 | tf_op jit(solution)/shard_map/all_to_all | solution.py:187
  11.4 0.7 collective-permute-start
  12.1 13.0 %collective-permute-start.1 = (f32[128,128]{1,0:T(8,128)S(1)}, f32[128,128]{1,0:T(8,128)S(1)}, u32[]{:S(2)}, u32[]{:S(2)}) collective-permute-start(f32[128,128]{1,0:T(8,128)S(1)} %get-tuple-element.51), channel_id=1, source_target_pairs={{2,0},{3,1},{6,4},{7,5},{10,8},{11,9},{14,12},{15,13},{18,16},{19,... | collective-permute-start | bytes 196616 | tf_op jit(solution)/shard_map/ppermute | solution.py:202
  12.8 12.4 %collective-permute-start.2 = (f32[128,128]{1,0:T(8,128)S(1)}, f32[128,128]{1,0:T(8,128)S(1)}, u32[]{:S(2)}, u32[]{:S(2)}) collective-permute-start(f32[128,128]{1,0:T(8,128)S(1)} %get-tuple-element.52), channel_id=1, source_target_pairs={{3,0},{2,1},{7,4},{6,5},{11,8},{10,9},{15,12},{14,13},{19,16},{18,... | collective-permute-start | bytes 196616 | tf_op jit(solution)/shard_map/ppermute | solution.py:202
  14.4 24.2 %collective-permute-start.3 = (bf16[128,512]{1,0:T(8,128)(2,1)S(1)}, bf16[128,512]{1,0:T(8,128)(2,1)S(1)}, u32[]{:S(2)}, u32[]{:S(2)}) collective-permute-start(bf16[128,512]{1,0:T(8,128)(2,1)S(1)} %slice_bitcast_fusion.5), channel_id=1, source_target_pairs={{0,1},{1,2},{2,3},{3,0},{4,5},{5,6},{6,7},{7,4},{8,9},{9,10},{10,1... | collective-permute-start | bytes 393224 | tf_op jit(solution)/shard_map/ppermute | solution.py:188
  17.5 21.1 %collective-permute-start.4 = (bf16[128,512]{1,0:T(8,128)(2,1)S(1)}, bf16[128,512]{1,0:T(8,128)(2,1)S(1)}, u32[]{:S(2)}, u32[]{:S(2)}) collective-permute-start(bf16[128,512]{1,0:T(8,128)(2,1)S(1)} %slice_bitcast_fusion.5), channel_id=1, source_target_pairs={{0,2},{1,3},{2,0},{3,1},{4,6},{5,7},{6,4},{7,5},{8,10},{9,11},{10,... | collective-permute-start | bytes 393224 | tf_op jit(solution)/shard_map/ppermute | solution.py:188
  21.9 16.7 %collective-permute-start.5 = (bf16[128,512]{1,0:T(8,128)(2,1)S(1)}, bf16[128,512]{1,0:T(8,128)(2,1)S(1)}, u32[]{:S(2)}, u32[]{:S(2)}) collective-permute-start(bf16[128,512]{1,0:T(8,128)(2,1)S(1)} %slice_bitcast_fusion.5), channel_id=1, source_target_pairs={{0,3},{1,0},{2,1},{3,2},{4,7},{5,4},{6,5},{7,6},{8,11},{9,8},{10,9... | collective-permute-start | bytes 393224 | tf_op jit(solution)/shard_map/ppermute | solution.py:188
  39.8 24.5 %all-to-all-start.1 = ((f32[16,8,512]{2,1,0:T(8,128)}), f32[16,8,512]{2,1,0:T(8,128)S(1)}, u32[]{:S(2)}, u32[]{:S(2)}) async-start(f32[16,8,512]{2,1,0:T(8,128)} %subtract_bitcast_fusion), calls=%async_computation.1 | async-start | bytes 524288 | tf_op jit(solution)/shard_map/all_to_all | solution.py:219
  53.1 16.6 %collective-permute-start.6 = (bf16[1024,256]{1,0:T(8,128)(2,1)S(1)}, bf16[1024,256]{1,0:T(8,128)(2,1)S(1)}, u32[]{:S(2)}, u32[]{:S(2)}) collective-permute-start(bf16[1024,256]{1,0:T(8,128)(2,1)S(1)} %convolution_convert_fusion), channel_id=1, source_target_pairs={{0,32},{32,0},{1,33},{33,1},{2,34},{34,2},{3,35},{35,3},{4,36},{36... | collective-permute-start | bytes 1572872 | tf_op jit(solution)/shard_map/ppermute | solution.py:226
  65.2 21.8 %all-to-all-start.2 = ((f32[32,8,512]{2,1,0:T(8,128)}), f32[32,8,512]{2,1,0:T(8,128)S(1)}, u32[]{:S(2)}, u32[]{:S(2)}) async-start(f32[32,8,512]{2,1,0:T(8,128)} %broadcast_in_dim.20), calls=%async_computation.2 | async-start | bytes 1048576 | tf_op jit(solution)/shard_map/all_to_all | solution.py:22
  70.1 16.9 %collective-permute-start.7 = (bf16[4,128,256]{2,1,0:T(8,128)(2,1)S(1)}, bf16[4,128,256]{2,1,0:T(8,128)(2,1)S(1)}, u32[]{:S(2)}, u32[]{:S(2)}) collective-permute-start(bf16[4,128,256]{2,1,0:T(8,128)(2,1)S(1)} %fusion.13), channel_id=1, source_target_pairs={{0,64},{64,0},{1,65},{65,1},{2,66},{66,2},{3,67},{67,3},{4,68},{68... | collective-permute-start | bytes 786440 | tf_op jit(solution)/shard_map/ppermute | solution.py:230
  88.1 24.0 %all-to-all-start.3 = ((f32[16,16,640]{2,1,0:T(8,128)}), f32[16,16,640]{2,1,0:T(8,128)S(1)}, u32[]{:S(2)}, u32[]{:S(2)}) async-start(f32[16,16,640]{2,1,0:T(8,128)} %pad_maximum_fusion), calls=%async_computation.3 | async-start | bytes 1310720 | tf_op jit(solution)/shard_map/all_to_all | solution.py:248
  92.1 8.6 %collective-permute-start.8 = (bf16[512,128]{1,0:T(8,128)(2,1)S(1)}, bf16[512,128]{1,0:T(8,128)(2,1)S(1)}, u32[]{:S(2)}, u32[]{:S(2)}) collective-permute-start(bf16[512,128]{1,0:T(8,128)(2,1)S(1)} %get-tuple-element.43), channel_id=1, source_target_pairs={{0,0},{1,1},{2,32},{3,33},{32,2},{33,3},{34,34},{35,35},{4,4},{5,5... | collective-permute-start | bytes 393224 | tf_op jit(solution)/shard_map/ppermute | solution.py:238
  97.0 7.8 %collective-permute-start.9 = (bf16[512,128]{1,0:T(8,128)(2,1)S(1)}, bf16[512,128]{1,0:T(8,128)(2,1)S(1)}, u32[]{:S(2)}, u32[]{:S(2)}) collective-permute-start(bf16[512,128]{1,0:T(8,128)(2,1)S(1)} %get-tuple-element.44), channel_id=1, source_target_pairs={{0,1},{1,0},{2,33},{3,32},{32,3},{33,2},{34,35},{35,34},{4,5},{5,4... | collective-permute-start | bytes 393224 | tf_op jit(solution)/shard_map/ppermute | solution.py:238
  112.1 14.9 %all-to-all-start.4 = ((bf16[4,256,128]{2,1,0:T(8,128)(2,1)}), bf16[4,256,128]{2,1,0:T(8,128)(2,1)S(1)}, u32[]{:S(2)}, u32[]{:S(2)}) async-start(bf16[4,256,128]{2,1,0:T(8,128)(2,1)} %pad_maximum_fusion.1), calls=%async_computation.4 | async-start | bytes 524288 | tf_op jit(solution)/shard_map/all_to_all | solution.py:252
  127.7 0.9 copy-start.1

commit v9 on v8

--- a/solution.py
+++ b/solution.py
@@ -25,12 +25,15 @@
 def lane(tile, k):
     return jnp.broadcast_to(tile[:, k:k + 1], tile.shape)
 
+
 def sub(tile, s):
     return jnp.broadcast_to(tile[s:s + 1, :], tile.shape)
 
-def group_rows(tile, start):
+
+def group_rows(tile, start, after):
     r = [sub(tile, s) for s in range(SUB)]
     d = [[lane(r[i], start + j) if j >= i else None for j in range(SUB)] for i in range(SUB)]
+    c = [lane(after, start + j) for j in range(SUB)] if after is not None else None
     pairs = []
     for p in range(0, SUB, 2):
         a, b, e = d[p][p], d[p][p + 1], d[p + 1][p + 1]
@@ -45,12 +48,16 @@
             low[i] = (raw[i][0] * inv, raw[i][1] * inv)
             r[i] = r[i] - (low[i][0] * r[p] + low[i][1] * r[p + 1])
         pairs.append((a, b, e, ia, ib, ie, low))
+        if after is not None:
+            after = after - (c[p] * (ie * r[p] - ib * r[p + 1]) + c[p + 1] * (ia * r[p + 1] - ib * r[p]))
+            for i in range(p + 2, SUB):
+                c[i] = c[i] - (low[i][0] * c[p] + low[i][1] * c[p + 1])
     solved = [None] * SUB
     for p in range(SUB - 2, -1, -2):
         a, b, e, ia, ib, ie, low = pairs[p // 2]
         s0 = ie * r[p] - ib * r[p + 1]
         s1 = ia * r[p + 1] - ib * r[p]
-        for i in range(p + 2, SUB):
+        for i in range(SUB - 1, p + 1, -1):
             s0 = s0 - low[i][0] * solved[i]
             s1 = s1 - low[i][1] * solved[i]
         solved[p], solved[p + 1] = s0, s1
@@ -60,7 +67,8 @@
         ratio = b / a
         norm[p] = r[p] * lax.rsqrt(a)
         norm[p + 1] = (r[p + 1] - ratio * r[p]) * lax.rsqrt(e - ratio * b)
-    return norm, solved
+    return norm, solved, after
+
 
 def block_inverse(block):
     n = BLOCK
@@ -72,8 +80,11 @@
         unit = jnp.where(laneid == rowid + (n + t * SUB), 1.0, 0.0).astype(F32)
         tiles.append(wide[t * SUB:(t + 1) * SUB, :] + unit)
     for t in range(len(tiles)):
-        norm, solved = group_rows(tiles[t], t * SUB)
-        for u in range(t + 1, len(tiles)):
+        last = t + 1 == len(tiles)
+        norm, solved, after = group_rows(tiles[t], t * SUB, None if last else tiles[t + 1])
+        if not last:
+            tiles[t + 1] = after
+        for u in range(t + 2, len(tiles)):
             terms = [lane(tiles[u], t * SUB + s) * solved[s] for s in range(SUB)]
             while len(terms) > 1:
                 terms = [x + y for x, y in zip(terms[::2], terms[1::2])]
@@ -85,24 +96,9 @@
     return jnp.concatenate(tiles, axis=0)[:, n:]
 
 
-def eliminate(aug, w_ref, s_row, start):
-    n = aug.shape[1] // 2
-    count = aug.shape[0]
-    for k in range(0, w_ref.shape[0], BLOCK):
-        rows = aug[k:k + BLOCK, :]
-        inv = block_inverse(rows[:, start + k:start + k + BLOCK])
-        u = jnp.dot(inv, rows, precision=HI, preferred_element_type=F32)
-        w_ref[k:k + BLOCK, :] = u[:, n:] * s_row
-        for m in range(k + BLOCK, count, BLOCK):
-            left = u[:, start + m:start + m + BLOCK]
-            aug[m:m + BLOCK, :] = aug[m:m + BLOCK, :] - lax.dot_general(
-                left, u, (((0,), (0,)), ((), ())), precision=HI, preferred_element_type=F32
-            )
-
-
 def inverse_factor(a_ref, w_ref, aug):
     n = a_ref.shape[0]
-    a = a_ref[:, :n]
+    a = a_ref[...]
     a = a * 0.5 + a.T * 0.5
     ri = lax.broadcasted_iota(jnp.int32, (n, n), 0)
     ci = lax.broadcasted_iota(jnp.int32, (n, n), 1)
@@ -111,7 +107,18 @@
     s_col = lax.rsqrt(jnp.sum(diag, axis=1, keepdims=True))
     aug[:, :n] = a * s_col * s_row
     aug[:, n:] = jnp.where(ri == ci, 1.0, 0.0)
-    eliminate(aug, w_ref, s_row, 0)
+    for k in range(0, n, BLOCK):
+        low, high = k // LANES * LANES, n + k + BLOCK
+        rows = aug[k:k + BLOCK, low:high]
+        inv = block_inverse(rows[:, k - low:k - low + BLOCK])
+        u = jnp.dot(inv, rows, precision=HI, preferred_element_type=F32)
+        w_ref[k:k + BLOCK, :] = jnp.zeros((BLOCK, n), F32)
+        w_ref[k:k + BLOCK, :k + BLOCK] = u[:, n - low:] * s_row[:, :k + BLOCK]
+        for m in range(k + BLOCK, n, BLOCK):
+            left = u[:, m - low:m - low + BLOCK]
+            aug[m:m + BLOCK, low:high] = aug[m:m + BLOCK, low:high] - lax.dot_general(
+                left, u, (((0,), (0,)), ((), ())), precision=HI, preferred_element_type=F32
+            )
 
 
 def in_vmem(body, outs, scratch, name, *args):

time: 129 us -> 128 us (level)
  transfers between devices with their start and end apart: 15 -> 15, of which waited for: 6 -> 6; matrix products, arithmetic and copies ran while one was open for 3% -> 3% of each run, Pallas kernels for 9% -> 8%
where the time goes in v9:
time: 128 us
  starting transfers between devices  56.7 us (44%)
  waiting for transfers between devices  48.8 us (38%)
  Pallas kernels  13.5 us (11%)
  other arithmetic  2.83 us (2%)
  matrix products  2.72 us (2%)
  local copies, waits for them, and re-layouts  1.97 us (2%)
    all_to_all x1, waiting for transfers between devices, share(): return lax.all_to_all(copies, axis, 0, 0, tiled=True)  14.9 us
    all_to_all x1, waiting for transfers between devices, body(): along_y = lax.all_to_all(copies, 'y', 0, 0, tiled=True)  13.3 us
    all_to_all x1, starting transfers between devices, body(): lax.all_to_all(part.reshape(Z * C, strip_rows, X * rows), GROUP, 0, 0, ti...  12.8 us
    pallas_call x1, Pallas kernels, in_vmem(): pl.pallas_call(body, out_shape=[jax.ShapeDtypeStruct(shape, F32) for shap...  10.6 us
    ppermute x3, starting transfers between devices, body(): lax.ppermute(own, 'x', [(i, (i + k) % X) for i in range(X)])  10.5 us
    all_to_all x1, waiting for transfers between devices, body(): lax.all_to_all(part.reshape(Z * C, strip_rows, X * rows), GROUP, 0, 0, ti...  9.23 us
    ppermute x2, starting transfers between devices, place(): return lax.ppermute(block, ('c', 'x'), pairs).reshape(Z // 2, rows, rows)  7.85 us
    all_to_all x1, starting transfers between devices, body(): along_y = lax.all_to_all(copies, 'y', 0, 0, tiled=True)  7.8 us
  transfers between devices with their start and end apart: 15, of which 6 were waited for; matrix products, arithmetic and copies ran while one was open for 3% of the time, Pallas kernels for 8%

profile of v9, /device:TPU:1, one launch (start us, length us, event | category | flops | bytes accessed | tf_op | source)
XLA Modules:
  0.0 127.7 jit_solution(15235344457328403336)
XLA Ops:
  0.6 2.9 %leaf_panels.1 = (bf16[2,128,256]{2,1,0:T(8,128)(2,1)}, bf16[8,128,512]{2,1,0:T(8,128)(2,1)}) custom-call(f32[2,128,256]{2,1,0:T(8,128)} %rows_hbm.1, f32[2,256,256]{2,1,0:T(8,128)} %inverse_hbm.1, s32[2,16]{1,0:T(2,128)} %pattern_hbm.1, s32[2]{0:T(128)} %widths_hbm.1), custom_call_target="tpu_custom_call" | custom-call | tf_op jit(solution)/shard_map/leaf_panels/pallas_call | solution.py:174
  3.5 0.0 copy-start
  3.5 7.8 %all-to-all-start = ((bf16[8,128,512]{2,1,0:T(8,128)(2,1)}), bf16[8,128,512]{2,1,0:T(8,128)(2,1)S(1)}, u32[]{:S(2)}, u32[]{:S(2)}) async-start(bf16[8,128,512]{2,1,0:T(8,128)(2,1)} %get-tuple-element.19), calls=%async_computation | async-start | bytes 2097152 | tf_op jit(solution)/shard_map/all_to_all | solution.py:194
  11.3 0.0 copy-done
  11.4 0.7 collective-permute-start
  12.1 0.0 collective-permute-done
  12.1 0.7 collective-permute-start.1
  12.8 0.7 collective-permute-start.2
  13.4 0.9 slice_bitcast_fusion.5
  14.4 3.1 %collective-permute-start.3 = (bf16[128,512]{1,0:T(8,128)(2,1)S(1)}, bf16[128,512]{1,0:T(8,128)(2,1)S(1)}, u32[]{:S(2)}, u32[]{:S(2)}) collective-permute-start(bf16[128,512]{1,0:T(8,128)(2,1)S(1)} %slice_bitcast_fusion.5), channel_id=1, source_target_pairs={{0,1},{1,2},{2,3},{3,0},{4,5},{5,6},{6,7},{7,4},{8,9},{9,10},{10,1... | collective-permute-start | bytes 393224 | tf_op jit(solution)/shard_map/ppermute | solution.py:195
  17.5 4.4 %collective-permute-start.4 = (bf16[128,512]{1,0:T(8,128)(2,1)S(1)}, bf16[128,512]{1,0:T(8,128)(2,1)S(1)}, u32[]{:S(2)}, u32[]{:S(2)}) collective-permute-start(bf16[128,512]{1,0:T(8,128)(2,1)S(1)} %slice_bitcast_fusion.5), channel_id=1, source_target_pairs={{0,2},{1,3},{2,0},{3,1},{4,6},{5,7},{6,4},{7,5},{8,10},{9,11},{10,... | collective-permute-start | bytes 393224 | tf_op jit(solution)/shard_map/ppermute | solution.py:195
  21.9 3.1 %collective-permute-start.5 = (bf16[128,512]{1,0:T(8,128)(2,1)S(1)}, bf16[128,512]{1,0:T(8,128)(2,1)S(1)}, u32[]{:S(2)}, u32[]{:S(2)}) collective-permute-start(bf16[128,512]{1,0:T(8,128)(2,1)S(1)} %slice_bitcast_fusion.5), channel_id=1, source_target_pairs={{0,3},{1,0},{2,1},{3,2},{4,7},{5,4},{6,5},{7,6},{8,11},{9,8},{10,9... | collective-permute-start | bytes 393224 | tf_op jit(solution)/shard_map/ppermute | solution.py:195
  25.1 0.0 collective-permute-done.1
  25.1 0.0 collective-permute-done.2
  25.2 13.3 %all-to-all-done = bf16[8,128,512]{2,1,0:T(8,128)(2,1)S(1)} async-done(((bf16[8,128,512]{2,1,0:T(8,128)(2,1)}), bf16[8,128,512]{2,1,0:T(8,128)(2,1)S(1)}, u32[]{:S(2)}, u32[]{:S(2)}) %all-to-all-start) | async-done | bytes 1048608 | tf_op jit(solution)/shard_map/all_to_all | solution.py:194
  38.5 0.0 collective-permute-done.3
  38.6 0.0 collective-permute-done.4
  38.6 0.0 collective-permute-done.5
  38.6 0.1 select_select_fusion.7
  38.6 0.1 select_select_fusion.3
  38.7 0.3 fusion.1
  39.0 0.7 subtract_bitcast_fusion
  39.8 12.8 %all-to-all-start.1 = ((f32[16,8,512]{2,1,0:T(8,128)}), f32[16,8,512]{2,1,0:T(8,128)S(1)}, u32[]{:S(2)}, u32[]{:S(2)}) async-start(f32[16,8,512]{2,1,0:T(8,128)} %subtract_bitcast_fusion), calls=%async_computation.1 | async-start | bytes 524288 | tf_op jit(solution)/shard_map/all_to_all | solution.py:226
  52.6 0.5 convolution_convert_fusion
  53.1 2.0 %collective-permute-start.6 = (bf16[1024,256]{1,0:T(8,128)(2,1)S(1)}, bf16[1024,256]{1,0:T(8,128)(2,1)S(1)}, u32[]{:S(2)}, u32[]{:S(2)}) collective-permute-start(bf16[1024,256]{1,0:T(8,128)(2,1)S(1)} %convolution_convert_fusion), channel_id=1, source_target_pairs={{0,32},{32,0},{1,33},{33,1},{2,34},{34,2},{3,35},{35,3},{4,36},{36... | collective-permute-start | bytes 1572872 | tf_op jit(solution)/shard_map/ppermute | solution.py:233
  55.1 9.2 %all-to-all-done.1 = f32[16,8,512]{2,1,0:T(8,128)S(1)} async-done(((f32[16,8,512]{2,1,0:T(8,128)}), f32[16,8,512]{2,1,0:T(8,128)S(1)}, u32[]{:S(2)}, u32[]{:S(2)}) %all-to-all-start.1) | async-done | bytes 262176 | tf_op jit(solution)/shard_map/all_to_all | solution.py:226
  64.3 0.9 broadcast_in_dim.20
  65.2 4.4 %all-to-all-start.2 = ((f32[32,8,512]{2,1,0:T(8,128)}), f32[32,8,512]{2,1,0:T(8,128)S(1)}, u32[]{:S(2)}, u32[]{:S(2)}) async-start(f32[32,8,512]{2,1,0:T(8,128)} %broadcast_in_dim.20), calls=%async_computation.2 | async-start | bytes 1048576 | tf_op jit(solution)/shard_map/all_to_all | solution.py:22
  69.6 0.0 collective-permute-done.6
  69.6 0.5 add_convert_fusion
  70.1 1.9 %collective-permute-start.7 = (bf16[4,128,256]{2,1,0:T(8,128)(2,1)S(1)}, bf16[4,128,256]{2,1,0:T(8,128)(2,1)S(1)}, u32[]{:S(2)}, u32[]{:S(2)}) collective-permute-start(bf16[4,128,256]{2,1,0:T(8,128)(2,1)S(1)} %fusion.13), channel_id=1, source_target_pairs={{0,64},{64,0},{1,65},{65,1},{2,66},{66,2},{3,67},{67,3},{4,68},{68... | collective-permute-start | bytes 786440 | tf_op jit(solution)/shard_map/ppermute | solution.py:237
  72.1 14.9 %all-to-all-done.2 = f32[32,8,512]{2,1,0:T(8,128)S(1)} async-done(((f32[32,8,512]{2,1,0:T(8,128)}), f32[32,8,512]{2,1,0:T(8,128)S(1)}, u32[]{:S(2)}, u32[]{:S(2)}) %all-to-all-start.2) | async-done | bytes 524320 | tf_op jit(solution)/shard_map/all_to_all | solution.py:22
  87.0 0.0 collective-permute-done.7
  87.2 0.9 pad_maximum_fusion
  88.1 3.9 %all-to-all-start.3 = ((f32[16,16,640]{2,1,0:T(8,128)}), f32[16,16,640]{2,1,0:T(8,128)S(1)}, u32[]{:S(2)}, u32[]{:S(2)}) async-start(f32[16,16,640]{2,1,0:T(8,128)} %pad_maximum_fusion), calls=%async_computation.3 | async-start | bytes 1310720 | tf_op jit(solution)/shard_map/all_to_all | solution.py:255
  92.0 0.1 fusion.9
  92.1 4.9 %collective-permute-start.8 = (bf16[512,128]{1,0:T(8,128)(2,1)S(1)}, bf16[512,128]{1,0:T(8,128)(2,1)S(1)}, u32[]{:S(2)}, u32[]{:S(2)}) collective-permute-start(bf16[512,128]{1,0:T(8,128)(2,1)S(1)} %get-tuple-element.43), channel_id=1, source_target_pairs={{0,0},{1,1},{2,32},{3,33},{32,2},{33,3},{34,34},{35,35},{4,4},{5,5... | collective-permute-start | bytes 393224 | tf_op jit(solution)/shard_map/ppermute | solution.py:245
  97.0 3.0 %collective-permute-start.9 = (bf16[512,128]{1,0:T(8,128)(2,1)S(1)}, bf16[512,128]{1,0:T(8,128)(2,1)S(1)}, u32[]{:S(2)}, u32[]{:S(2)}) collective-permute-start(bf16[512,128]{1,0:T(8,128)(2,1)S(1)} %get-tuple-element.44), channel_id=1, source_target_pairs={{0,1},{1,0},{2,33},{3,32},{32,3},{33,2},{34,35},{35,34},{4,5},{5,4... | collective-permute-start | bytes 393224 | tf_op jit(solution)/shard_map/ppermute | solution.py:245
  100.0 0.7 collective-permute-done.8
  100.8 4.1 %collective-permute-done.9 = bf16[512,128]{1,0:T(8,128)(2,1)S(1)} collective-permute-done((bf16[512,128]{1,0:T(8,128)(2,1)S(1)}, bf16[512,128]{1,0:T(8,128)(2,1)S(1)}, u32[]{:S(2)}, u32[]{:S(2)}) %collective-permute-start.9) | collective-permute-done | bytes 131104 | tf_op jit(solution)/shard_map/ppermute | solution.py:245
  104.9 0.7 pad_maximum_fusion.1
  105.6 6.5 %all-to-all-done.3 = f32[16,16,640]{2,1,0:T(8,128)S(1)} async-done(((f32[16,16,640]{2,1,0:T(8,128)}), f32[16,16,640]{2,1,0:T(8,128)S(1)}, u32[]{:S(2)}, u32[]{:S(2)}) %all-to-all-start.3) | async-done | bytes 655392 | tf_op jit(solution)/shard_map/all_to_all | solution.py:255
  112.1 3.4 %all-to-all-start.4 = ((bf16[4,256,128]{2,1,0:T(8,128)(2,1)}), bf16[4,256,128]{2,1,0:T(8,128)(2,1)S(1)}, u32[]{:S(2)}, u32[]{:S(2)}) async-start(bf16[4,256,128]{2,1,0:T(8,128)(2,1)} %pad_maximum_fusion.1), calls=%async_computation.4 | async-start | bytes 524288 | tf_op jit(solution)/shard_map/all_to_all | solution.py:259
  115.6 10.6 %inverse_factor.1 = f32[256,256]{1,0:T(8,128)S(1)} custom-call(f32[256,256]{1,0:T(8,128)S(1)} %slice.80.a_ref), custom_call_target="tpu_custom_call" | custom-call | flops 10000000000 | bytes 1000000 | tf_op jit(solution)/shard_map/inverse_factor/pallas_call | solution.py:126
  126.1 0.0 all-to-all-done.4
  126.2 0.6 convolution_convert_fusion.1
  126.8 0.0 copy-start.1
  126.8 0.9 fusion
  127.7 0.0 copy-done.1
  (20 shorter events, 0.4 us)
Async XLA Ops:
  3.5 7.8 %copy-start = (f32[256,128]{1,0:T(8,128)S(1)}, f32[256,128]{1,0:T(8,128)}, u32[]{:S(2)}) copy-start(f32[256,128]{1,0:T(8,128)} %param.9) | copy-start | bytes 393220
  3.5 35.0 %all-to-all-start = ((bf16[8,128,512]{2,1,0:T(8,128)(2,1)}), bf16[8,128,512]{2,1,0:T(8,128)(2,1)S(1)}, u32[]{:S(2)}, u32[]{:S(2)}) async-start(bf16[8,128,512]{2,1,0:T(8,128)(2,1)} %get-tuple-element.19), calls=%async_computation | async-start | bytes 2097152 | tf_op jit(solution)/shard_map/all_to_all | solution.py:194
  11.4 0.7 collective-permute-start
  12.1 13.0 %collective-permute-start.1 = (f32[128,128]{1,0:T(8,128)S(1)}, f32[128,128]{1,0:T(8,128)S(1)}, u32[]{:S(2)}, u32[]{:S(2)}) collective-permute-start(f32[128,128]{1,0:T(8,128)S(1)} %get-tuple-element.51), channel_id=1, source_target_pairs={{2,0},{3,1},{6,4},{7,5},{10,8},{11,9},{14,12},{15,13},{18,16},{19,... | collective-permute-start | bytes 196616 | tf_op jit(solution)/shard_map/ppermute | solution.py:209
  12.8 12.4 %collective-permute-start.2 = (f32[128,128]{1,0:T(8,128)S(1)}, f32[128,128]{1,0:T(8,128)S(1)}, u32[]{:S(2)}, u32[]{:S(2)}) collective-permute-start(f32[128,128]{1,0:T(8,128)S(1)} %get-tuple-element.52), channel_id=1, source_target_pairs={{3,0},{2,1},{7,4},{6,5},{11,8},{10,9},{15,12},{14,13},{19,16},{18,... | collective-permute-start | bytes 196616 | tf_op jit(solution)/shard_map/ppermute | solution.py:209
  14.4 24.2 %collective-permute-start.3 = (bf16[128,512]{1,0:T(8,128)(2,1)S(1)}, bf16[128,512]{1,0:T(8,128)(2,1)S(1)}, u32[]{:S(2)}, u32[]{:S(2)}) collective-permute-start(bf16[128,512]{1,0:T(8,128)(2,1)S(1)} %slice_bitcast_fusion.5), channel_id=1, source_target_pairs={{0,1},{1,2},{2,3},{3,0},{4,5},{5,6},{6,7},{7,4},{8,9},{9,10},{10,1... | collective-permute-start | bytes 393224 | tf_op jit(solution)/shard_map/ppermute | solution.py:195
  17.5 21.1 %collective-permute-start.4 = (bf16[128,512]{1,0:T(8,128)(2,1)S(1)}, bf16[128,512]{1,0:T(8,128)(2,1)S(1)}, u32[]{:S(2)}, u32[]{:S(2)}) collective-permute-start(bf16[128,512]{1,0:T(8,128)(2,1)S(1)} %slice_bitcast_fusion.5), channel_id=1, source_target_pairs={{0,2},{1,3},{2,0},{3,1},{4,6},{5,7},{6,4},{7,5},{8,10},{9,11},{10,... | collective-permute-start | bytes 393224 | tf_op jit(solution)/shard_map/ppermute | solution.py:195
  21.9 16.7 %collective-permute-start.5 = (bf16[128,512]{1,0:T(8,128)(2,1)S(1)}, bf16[128,512]{1,0:T(8,128)(2,1)S(1)}, u32[]{:S(2)}, u32[]{:S(2)}) collective-permute-start(bf16[128,512]{1,0:T(8,128)(2,1)S(1)} %slice_bitcast_fusion.5), channel_id=1, source_target_pairs={{0,3},{1,0},{2,1},{3,2},{4,7},{5,4},{6,5},{7,6},{8,11},{9,8},{10,9... | collective-permute-start | bytes 393224 | tf_op jit(solution)/shard_map/ppermute | solution.py:195
  39.8 24.5 %all-to-all-start.1 = ((f32[16,8,512]{2,1,0:T(8,128)}), f32[16,8,512]{2,1,0:T(8,128)S(1)}, u32[]{:S(2)}, u32[]{:S(2)}) async-start(f32[16,8,512]{2,1,0:T(8,128)} %subtract_bitcast_fusion), calls=%async_computation.1 | async-start | bytes 524288 | tf_op jit(solution)/shard_map/all_to_all | solution.py:226
  53.1 16.6 %collective-permute-start.6 = (bf16[1024,256]{1,0:T(8,128)(2,1)S(1)}, bf16[1024,256]{1,0:T(8,128)(2,1)S(1)}, u32[]{:S(2)}, u32[]{:S(2)}) collective-permute-start(bf16[1024,256]{1,0:T(8,128)(2,1)S(1)} %convolution_convert_fusion), channel_id=1, source_target_pairs={{0,32},{32,0},{1,33},{33,1},{2,34},{34,2},{3,35},{35,3},{4,36},{36... | collective-permute-start | bytes 1572872 | tf_op jit(solution)/shard_map/ppermute | solution.py:233
  65.2 21.8 %all-to-all-start.2 = ((f32[32,8,512]{2,1,0:T(8,128)}), f32[32,8,512]{2,1,0:T(8,128)S(1)}, u32[]{:S(2)}, u32[]{:S(2)}) async-start(f32[32,8,512]{2,1,0:T(8,128)} %broadcast_in_dim.20), calls=%async_computation.2 | async-start | bytes 1048576 | tf_op jit(solution)/shard_map/all_to_all | solution.py:22
  70.1 16.9 %collective-permute-start.7 = (bf16[4,128,256]{2,1,0:T(8,128)(2,1)S(1)}, bf16[4,128,256]{2,1,0:T(8,128)(2,1)S(1)}, u32[]{:S(2)}, u32[]{:S(2)}) collective-permute-start(bf16[4,128,256]{2,1,0:T(8,128)(2,1)S(1)} %fusion.13), channel_id=1, source_target_pairs={{0,64},{64,0},{1,65},{65,1},{2,66},{66,2},{3,67},{67,3},{4,68},{68... | collective-permute-start | bytes 786440 | tf_op jit(solution)/shard_map/ppermute | solution.py:237
  88.1 24.0 %all-to-all-start.3 = ((f32[16,16,640]{2,1,0:T(8,128)}), f32[16,16,640]{2,1,0:T(8,128)S(1)}, u32[]{:S(2)}, u32[]{:S(2)}) async-start(f32[16,16,640]{2,1,0:T(8,128)} %pad_maximum_fusion), calls=%async_computation.3 | async-start | bytes 1310720 | tf_op jit(solution)/shard_map/all_to_all | solution.py:255
  92.1 8.6 %collective-permute-start.8 = (bf16[512,128]{1,0:T(8,128)(2,1)S(1)}, bf16[512,128]{1,0:T(8,128)(2,1)S(1)}, u32[]{:S(2)}, u32[]{:S(2)}) collective-permute-start(bf16[512,128]{1,0:T(8,128)(2,1)S(1)} %get-tuple-element.43), channel_id=1, source_target_pairs={{0,0},{1,1},{2,32},{3,33},{32,2},{33,3},{34,34},{35,35},{4,4},{5,5... | collective-permute-start | bytes 393224 | tf_op jit(solution)/shard_map/ppermute | solution.py:245
  97.0 7.8 %collective-permute-start.9 = (bf16[512,128]{1,0:T(8,128)(2,1)S(1)}, bf16[512,128]{1,0:T(8,128)(2,1)S(1)}, u32[]{:S(2)}, u32[]{:S(2)}) collective-permute-start(bf16[512,128]{1,0:T(8,128)(2,1)S(1)} %get-tuple-element.44), channel_id=1, source_target_pairs={{0,1},{1,0},{2,33},{3,32},{32,3},{33,2},{34,35},{35,34},{4,5},{5,4... | collective-permute-start | bytes 393224 | tf_op jit(solution)/shard_map/ppermute | solution.py:245
  112.1 14.0 %all-to-all-start.4 = ((bf16[4,256,128]{2,1,0:T(8,128)(2,1)}), bf16[4,256,128]{2,1,0:T(8,128)(2,1)S(1)}, u32[]{:S(2)}, u32[]{:S(2)}) async-start(bf16[4,256,128]{2,1,0:T(8,128)(2,1)} %pad_maximum_fusion.1), calls=%async_computation.4 | async-start | bytes 524288 | tf_op jit(solution)/shard_map/all_to_all | solution.py:259
  126.8 0.9 copy-start.1

commit v10 on v9

--- a/solution.py
+++ b/solution.py
@@ -96,9 +96,10 @@
     return jnp.concatenate(tiles, axis=0)[:, n:]
 
 
-def inverse_factor(a_ref, w_ref, aug):
-    n = a_ref.shape[0]
-    a = a_ref[...]
+def inverse_factor(upper_ref, lower_ref, w_ref, aug):
+    n = lower_ref.shape[1]
+    corner = lower_ref[:, :n // 2].T
+    a = jnp.concatenate([jnp.concatenate([upper_ref[...], corner], axis=1), lower_ref[...]], axis=0)
     a = a * 0.5 + a.T * 0.5
     ri = lax.broadcasted_iota(jnp.int32, (n, n), 0)
     ci = lax.broadcasted_iota(jnp.int32, (n, n), 1)
@@ -133,6 +134,25 @@
         cost_estimate=pl.CostEstimate(flops=10**10, bytes_accessed=10**6, transcendentals=0),
         name=name,
     )(*args)
+
+
+def first_rows(strips_ref, top_ref, unused):
+    y, x = lax.axis_index("y"), lax.axis_index("x")
+    lane_at = pl.ds(pl.multiple_of(x * LANES, LANES), LANES)
+
+    def cut(line, row, at):
+        return strips_ref[X * line + row, :, at * LANES:(at + 1) * LANES]
+
+    common = []
+    for row in range(2):
+        lead = [cut(0, row, at) for at in range(row + 1)]
+        common.append(lead + [strips_ref[X * y + row, :, lane_at]])
+    for g in range(top_ref.shape[0]):
+        parts = []
+        for row in range(2):
+            parts += common[row] + [cut(g // 2, row, 2 * (g % 2) + b) for b in range(2)]
+        for i, part in enumerate(parts):
+            top_ref[g, :, i * LANES:(i + 1) * LANES] = part
 
 
 def leaf_panels(
@@ -225,7 +245,7 @@
     part = base - dot_t(block, jnp.concatenate(cols, axis=0))
     pieces = lax.all_to_all(part.reshape(Z * C, strip_rows, X * rows), GROUP, 0, 0, tiled=True)
     strip = jnp.sum(pieces, axis=0)
-    strips = share(strip, ("y", "x"), Y * X).reshape(Y, X, strip_rows, X, rows)[:, :2]
+    strips = share(strip, ("y", "x"), Y * X)
 
     row_blocks = along_y.reshape(Y * rows, depth)
     theirs = jnp.concatenate([choose(shifted, 2 - 2 * c), choose(shifted, 3 - 2 * c)], axis=0)
@@ -247,20 +267,15 @@
     near, far = place(0), place(1)
     terms = jnp.concatenate([jnp.where(even, near, far), jnp.where(even, far, near)], axis=1)
 
-    wide = strips.transpose(0, 3, 1, 2, 4)
-    lead = jnp.concatenate([wide[0, 0], wide[0, 1], wide[y, x]], axis=2)
-    lead = jnp.broadcast_to(lead[None], (Z * C,) + lead.shape)
-    wide = wide.reshape(Z * C, 2, 2, strip_rows, rows)
-    top = jnp.concatenate([lead, wide[:, 0], wide[:, 1]], axis=3).reshape(Z * C, 2 * strip_rows, 5 * rows)
-    top = lax.all_to_all(top, GROUP, 0, 0, tiled=True)
-    top = top.reshape(Z * C, 2, strip_rows, 5 * rows).transpose(1, 0, 2, 3).reshape(width, 5 * rows)
+    (top,) = in_vmem(first_rows, [(Z * C, strip_rows, 9 * rows)], (SUB, LANES), "first_rows", strips)
+    top = lax.all_to_all(top, GROUP, 0, 0, tiled=True).reshape(rows, 9 * rows)
     top, terms = lax.optimization_barrier((top, terms))
-    top_own, top_rows = top[:, width:width + rows], top[:, width + rows:]
+    top_cols = jnp.concatenate([top[:, rows:4 * rows], top[:, 6 * rows:]], axis=0)
     update = jnp.sum(lax.all_to_all(terms, "zh", 0, 0, tiled=True).astype(F32), axis=0)
 
-    (inverse,) = in_vmem(inverse_factor, [(width, width)], (width, 2 * width), "inverse_factor", top[:, :width])
+    (inverse,) = in_vmem(inverse_factor, [(width, width)], (width, 2 * width), "inverse_factor", top[:, :rows], top[:, 4 * rows:6 * rows])
     inverse, update = lax.optimization_barrier((inverse, update))
-    level = jnp.dot(inverse, jnp.concatenate([top_own, top_rows], axis=1), precision=HI).astype(BF16)
+    level = jnp.dot(inverse, top_cols, precision=HI).astype(BF16)
     level_own = level[:, :rows]
     level_rows = level[:, rows:]
 

time: 128 us -> 127 us (level)
  waiting for transfers between devices: 48.8 us -> 47.4 us
    ppermute x1, waiting for transfers between devices: 0.01 us -> 7.97 us  [body(): got = lax.ppermute(give, 'zl', [(0, 1), (1, 0)])]
    all_to_all x1, waiting for transfers between devices: 14.9 us -> 6.95 us  [share(): return lax.all_to_all(copies, axis, 0, 0, tiled=True)]
    all_to_all x1, waiting for transfers between devices: 6.45 us -> 5.06 us  [body(): top = lax.all_to_all(top, GROUP, 0, 0, tiled=True).reshape(rows, 9 * rows)]
    pallas_call x1 -> x2, Pallas kernels: 10.6 us -> 11.6 us  [in_vmem(): pl.pallas_call(body, out_shape=[jax.ShapeDtypeStruct(shape, F32) for shap...]
  transfers between devices with their start and end apart: 15 -> 15, of which waited for: 6 -> 7; matrix products, arithmetic and copies ran while one was open for 3% -> 3% of each run, Pallas kernels for 8% -> 9%
where the time goes in v10:
time: 127 us; the launch traced here: 126 us
  starting transfers between devices  56.7 us (45%)
  waiting for transfers between devices  47.4 us (37%)
  Pallas kernels  14.5 us (11%)
  matrix products  2.71 us (2%)
  other arithmetic  1.93 us (2%)
  local copies, waits for them, and re-layouts  1.85 us (1%)
    all_to_all x1, waiting for transfers between devices, body(): along_y = lax.all_to_all(copies, 'y', 0, 0, tiled=True)  13.3 us
    all_to_all x1, starting transfers between devices, body(): lax.all_to_all(part.reshape(Z * C, strip_rows, X * rows), GROUP, 0, 0, ti...  12.8 us
    pallas_call x2, Pallas kernels, in_vmem(): pl.pallas_call(body, out_shape=[jax.ShapeDtypeStruct(shape, F32) for shap...  11.6 us
    ppermute x3, starting transfers between devices, body(): lax.ppermute(own, 'x', [(i, (i + k) % X) for i in range(X)])  10.5 us
    all_to_all x1, waiting for transfers between devices, body(): lax.all_to_all(part.reshape(Z * C, strip_rows, X * rows), GROUP, 0, 0, ti...  9.22 us
    ppermute x1, waiting for transfers between devices, body(): got = lax.ppermute(give, 'zl', [(0, 1), (1, 0)])  7.97 us
    ppermute x2, starting transfers between devices, place(): return lax.ppermute(block, ('c', 'x'), pairs).reshape(Z // 2, rows, rows)  7.85 us
    all_to_all x1, starting transfers between devices, body(): along_y = lax.all_to_all(copies, 'y', 0, 0, tiled=True)  7.8 us
  transfers between devices with their start and end apart: 15, of which 7 were waited for; matrix products, arithmetic and copies ran while one was open for 3% of the time, Pallas kernels for 9%

profile of v10, /device:TPU:1, one launch (start us, length us, event | category | flops | bytes accessed | tf_op | source)
XLA Modules:
  0.0 126.3 jit_solution(15540967857886694954)
XLA Ops:
  0.6 2.9 %leaf_panels.1 = (bf16[2,128,256]{2,1,0:T(8,128)(2,1)}, bf16[8,128,512]{2,1,0:T(8,128)(2,1)}) custom-call(f32[2,128,256]{2,1,0:T(8,128)} %rows_hbm.1, f32[2,256,256]{2,1,0:T(8,128)} %inverse_hbm.1, s32[2,16]{1,0:T(2,128)} %pattern_hbm.1, s32[2]{0:T(128)} %widths_hbm.1), custom_call_target="tpu_custom_call" | custom-call | tf_op jit(solution)/shard_map/leaf_panels/pallas_call | solution.py:194
  3.5 0.0 copy-start
  3.5 7.8 %all-to-all-start = ((bf16[8,128,512]{2,1,0:T(8,128)(2,1)}), bf16[8,128,512]{2,1,0:T(8,128)(2,1)S(1)}, u32[]{:S(2)}, u32[]{:S(2)}) async-start(bf16[8,128,512]{2,1,0:T(8,128)(2,1)} %get-tuple-element.19), calls=%async_computation | async-start | bytes 2097152 | tf_op jit(solution)/shard_map/all_to_all | solution.py:214
  11.3 0.0 copy-done
  11.4 0.7 collective-permute-start
  12.0 0.0 collective-permute-done
  12.1 0.7 collective-permute-start.1
  12.8 0.7 collective-permute-start.2
  13.4 0.9 slice_bitcast_fusion.3
  14.3 3.1 %collective-permute-start.3 = (bf16[128,512]{1,0:T(8,128)(2,1)S(1)}, bf16[128,512]{1,0:T(8,128)(2,1)S(1)}, u32[]{:S(2)}, u32[]{:S(2)}) collective-permute-start(bf16[128,512]{1,0:T(8,128)(2,1)S(1)} %slice_bitcast_fusion.3), channel_id=1, source_target_pairs={{0,1},{1,2},{2,3},{3,0},{4,5},{5,6},{6,7},{7,4},{8,9},{9,10},{10,1... | collective-permute-start | bytes 393224 | tf_op jit(solution)/shard_map/ppermute | solution.py:215
  17.5 4.4 %collective-permute-start.4 = (bf16[128,512]{1,0:T(8,128)(2,1)S(1)}, bf16[128,512]{1,0:T(8,128)(2,1)S(1)}, u32[]{:S(2)}, u32[]{:S(2)}) collective-permute-start(bf16[128,512]{1,0:T(8,128)(2,1)S(1)} %slice_bitcast_fusion.3), channel_id=1, source_target_pairs={{0,2},{1,3},{2,0},{3,1},{4,6},{5,7},{6,4},{7,5},{8,10},{9,11},{10,... | collective-permute-start | bytes 393224 | tf_op jit(solution)/shard_map/ppermute | solution.py:215
  21.8 3.1 %collective-permute-start.5 = (bf16[128,512]{1,0:T(8,128)(2,1)S(1)}, bf16[128,512]{1,0:T(8,128)(2,1)S(1)}, u32[]{:S(2)}, u32[]{:S(2)}) collective-permute-start(bf16[128,512]{1,0:T(8,128)(2,1)S(1)} %slice_bitcast_fusion.3), channel_id=1, source_target_pairs={{0,3},{1,0},{2,1},{3,2},{4,7},{5,4},{6,5},{7,6},{8,11},{9,8},{10,9... | collective-permute-start | bytes 393224 | tf_op jit(solution)/shard_map/ppermute | solution.py:215
  25.1 0.0 collective-permute-done.1
  25.1 0.0 collective-permute-done.2
  25.2 13.3 %all-to-all-done = bf16[8,128,512]{2,1,0:T(8,128)(2,1)S(1)} async-done(((bf16[8,128,512]{2,1,0:T(8,128)(2,1)}), bf16[8,128,512]{2,1,0:T(8,128)(2,1)S(1)}, u32[]{:S(2)}, u32[]{:S(2)}) %all-to-all-start) | async-done | bytes 1048608 | tf_op jit(solution)/shard_map/all_to_all | solution.py:214
  38.5 0.0 collective-permute-done.3
  38.5 0.0 collective-permute-done.4
  38.5 0.0 collective-permute-done.5
  38.6 0.1 select_select_fusion.7
  38.6 0.1 select_select_fusion.3
  38.7 0.3 fusion.1
  39.0 0.8 subtract_bitcast_fusion
  39.8 12.8 %all-to-all-start.1 = ((f32[16,8,512]{2,1,0:T(8,128)}), f32[16,8,512]{2,1,0:T(8,128)S(1)}, u32[]{:S(2)}, u32[]{:S(2)}) async-start(f32[16,8,512]{2,1,0:T(8,128)} %subtract_bitcast_fusion), calls=%async_computation.1 | async-start | bytes 524288 | tf_op jit(solution)/shard_map/all_to_all | solution.py:246
  52.6 0.5 convolution_convert_fusion
  53.1 2.0 %collective-permute-start.6 = (bf16[1024,256]{1,0:T(8,128)(2,1)S(1)}, bf16[1024,256]{1,0:T(8,128)(2,1)S(1)}, u32[]{:S(2)}, u32[]{:S(2)}) collective-permute-start(bf16[1024,256]{1,0:T(8,128)(2,1)S(1)} %convolution_convert_fusion), channel_id=1, source_target_pairs={{0,32},{32,0},{1,33},{33,1},{2,34},{34,2},{3,35},{35,3},{4,36},{36... | collective-permute-start | bytes 1572872 | tf_op jit(solution)/shard_map/ppermute | solution.py:253
  55.1 9.2 %all-to-all-done.1 = f32[16,8,512]{2,1,0:T(8,128)S(1)} async-done(((f32[16,8,512]{2,1,0:T(8,128)}), f32[16,8,512]{2,1,0:T(8,128)S(1)}, u32[]{:S(2)}, u32[]{:S(2)}) %all-to-all-start.1) | async-done | bytes 262176 | tf_op jit(solution)/shard_map/all_to_all | solution.py:246
  64.3 0.9 broadcast_in_dim.14
  65.2 4.4 %all-to-all-start.2 = ((f32[32,8,512]{2,1,0:T(8,128)}), f32[32,8,512]{2,1,0:T(8,128)S(1)}, u32[]{:S(2)}, u32[]{:S(2)}) async-start(f32[32,8,512]{2,1,0:T(8,128)} %broadcast_in_dim.14), calls=%async_computation.2 | async-start | bytes 1048576 | tf_op jit(solution)/shard_map/all_to_all | solution.py:22
  69.6 0.0 collective-permute-done.6
  69.6 0.5 add_convert_fusion
  70.1 1.9 %collective-permute-start.7 = (bf16[4,128,256]{2,1,0:T(8,128)(2,1)S(1)}, bf16[4,128,256]{2,1,0:T(8,128)(2,1)S(1)}, u32[]{:S(2)}, u32[]{:S(2)}) collective-permute-start(bf16[4,128,256]{2,1,0:T(8,128)(2,1)S(1)} %fusion.15), channel_id=1, source_target_pairs={{0,64},{64,0},{1,65},{65,1},{2,66},{66,2},{3,67},{67,3},{4,68},{68... | collective-permute-start | bytes 786440 | tf_op jit(solution)/shard_map/ppermute | solution.py:257
  72.1 8.0 %collective-permute-done.7 = bf16[4,128,256]{2,1,0:T(8,128)(2,1)S(1)} collective-permute-done((bf16[4,128,256]{2,1,0:T(8,128)(2,1)S(1)}, bf16[4,128,256]{2,1,0:T(8,128)(2,1)S(1)}, u32[]{:S(2)}, u32[]{:S(2)}) %collective-permute-start.7) | collective-permute-done | bytes 262176 | tf_op jit(solution)/shard_map/ppermute | solution.py:257
  80.1 7.0 %all-to-all-done.2.strips_ref = f32[32,8,512]{2,1,0:T(8,128)S(1)} async-done(((f32[32,8,512]{2,1,0:T(8,128)}), f32[32,8,512]{2,1,0:T(8,128)S(1)}, u32[]{:S(2)}, u32[]{:S(2)}) %all-to-all-start.2) | async-done | bytes 524320 | tf_op jit(solution)/shard_map/all_to_all | solution.py:22
  87.0 0.9 first_rows.1
  87.9 3.9 %all-to-all-start.3 = ((f32[16,8,1152]{2,1,0:T(8,128)}), f32[16,8,1152]{2,1,0:T(8,128)S(1)}, u32[]{:S(2)}, u32[]{:S(2)}) async-start(f32[16,8,1152]{2,1,0:T(8,128)} %first_rows.1), calls=%async_computation.3 | async-start | bytes 1179648 | tf_op jit(solution)/shard_map/all_to_all | solution.py:271
  91.8 0.1 fusion.9
  91.9 4.9 %collective-permute-start.8 = (bf16[512,128]{1,0:T(8,128)(2,1)S(1)}, bf16[512,128]{1,0:T(8,128)(2,1)S(1)}, u32[]{:S(2)}, u32[]{:S(2)}) collective-permute-start(bf16[512,128]{1,0:T(8,128)(2,1)S(1)} %get-tuple-element.45), channel_id=1, source_target_pairs={{0,0},{1,1},{2,32},{3,33},{32,2},{33,3},{34,34},{35,35},{4,4},{5,5... | collective-permute-start | bytes 393224 | tf_op jit(solution)/shard_map/ppermute | solution.py:265
  96.8 3.0 %collective-permute-start.9 = (bf16[512,128]{1,0:T(8,128)(2,1)S(1)}, bf16[512,128]{1,0:T(8,128)(2,1)S(1)}, u32[]{:S(2)}, u32[]{:S(2)}) collective-permute-start(bf16[512,128]{1,0:T(8,128)(2,1)S(1)} %get-tuple-element.46), channel_id=1, source_target_pairs={{0,1},{1,0},{2,33},{3,32},{32,3},{33,2},{34,35},{35,34},{4,5},{5,4... | collective-permute-start | bytes 393224 | tf_op jit(solution)/shard_map/ppermute | solution.py:265
  99.8 0.7 collective-permute-done.8
  100.6 4.1 %collective-permute-done.9 = bf16[512,128]{1,0:T(8,128)(2,1)S(1)} collective-permute-done((bf16[512,128]{1,0:T(8,128)(2,1)S(1)}, bf16[512,128]{1,0:T(8,128)(2,1)S(1)}, u32[]{:S(2)}, u32[]{:S(2)}) %collective-permute-start.9) | collective-permute-done | bytes 131104 | tf_op jit(solution)/shard_map/ppermute | solution.py:265
  104.7 0.7 pad_maximum_fusion
  105.4 5.1 %all-to-all-done.3 = f32[16,8,1152]{2,1,0:T(8,128)S(1)} async-done(((f32[16,8,1152]{2,1,0:T(8,128)}), f32[16,8,1152]{2,1,0:T(8,128)S(1)}, u32[]{:S(2)}, u32[]{:S(2)}) %all-to-all-start.3) | async-done | bytes 589856 | tf_op jit(solution)/shard_map/all_to_all | solution.py:271
  110.5 3.4 %all-to-all-start.4 = ((bf16[4,256,128]{2,1,0:T(8,128)(2,1)}), bf16[4,256,128]{2,1,0:T(8,128)(2,1)S(1)}, u32[]{:S(2)}, u32[]{:S(2)}) async-start(bf16[4,256,128]{2,1,0:T(8,128)(2,1)} %pad_maximum_fusion), calls=%async_computation.4 | async-start | bytes 524288 | tf_op jit(solution)/shard_map/all_to_all | solution.py:274
  113.9 10.8 %inverse_factor.1 = f32[256,256]{1,0:T(8,128)S(1)} custom-call(f32[128,128]{1,0:T(8,128)S(1)} %slice.66.upper_ref, f32[128,256]{1,0:T(8,128)S(1)} %slice.67.lower_ref), custom_call_target="tpu_custom_call" | custom-call | flops 10000000000 | bytes 1000000 | tf_op jit(solution)/shard_map/inverse_factor/pallas_call | solution.py:127
  124.7 0.0 all-to-all-done.4
  124.7 0.6 convolution_convert_fusion.1
  125.4 0.0 copy-start.1
  125.4 0.9 fusion
  126.3 0.0 copy-done.1
  (14 shorter events, 0.3 us)
Async XLA Ops:
  3.5 7.8 %copy-start = (f32[256,128]{1,0:T(8,128)S(1)}, f32[256,128]{1,0:T(8,128)}, u32[]{:S(2)}) copy-start(f32[256,128]{1,0:T(8,128)} %param.9) | copy-start | bytes 393220
  3.5 35.0 %all-to-all-start = ((bf16[8,128,512]{2,1,0:T(8,128)(2,1)}), bf16[8,128,512]{2,1,0:T(8,128)(2,1)S(1)}, u32[]{:S(2)}, u32[]{:S(2)}) async-start(bf16[8,128,512]{2,1,0:T(8,128)(2,1)} %get-tuple-element.19), calls=%async_computation | async-start | bytes 2097152 | tf_op jit(solution)/shard_map/all_to_all | solution.py:214
  11.4 0.7 collective-permute-start
  12.1 13.0 %collective-permute-start.1 = (f32[128,128]{1,0:T(8,128)S(1)}, f32[128,128]{1,0:T(8,128)S(1)}, u32[]{:S(2)}, u32[]{:S(2)}) collective-permute-start(f32[128,128]{1,0:T(8,128)S(1)} %get-tuple-element.49), channel_id=1, source_target_pairs={{2,0},{3,1},{6,4},{7,5},{10,8},{11,9},{14,12},{15,13},{18,16},{19,... | collective-permute-start | bytes 196616 | tf_op jit(solution)/shard_map/ppermute | solution.py:229
  12.8 12.4 %collective-permute-start.2 = (f32[128,128]{1,0:T(8,128)S(1)}, f32[128,128]{1,0:T(8,128)S(1)}, u32[]{:S(2)}, u32[]{:S(2)}) collective-permute-start(f32[128,128]{1,0:T(8,128)S(1)} %get-tuple-element.50), channel_id=1, source_target_pairs={{3,0},{2,1},{7,4},{6,5},{11,8},{10,9},{15,12},{14,13},{19,16},{18,... | collective-permute-start | bytes 196616 | tf_op jit(solution)/shard_map/ppermute | solution.py:229
  14.3 24.2 %collective-permute-start.3 = (bf16[128,512]{1,0:T(8,128)(2,1)S(1)}, bf16[128,512]{1,0:T(8,128)(2,1)S(1)}, u32[]{:S(2)}, u32[]{:S(2)}) collective-permute-start(bf16[128,512]{1,0:T(8,128)(2,1)S(1)} %slice_bitcast_fusion.3), channel_id=1, source_target_pairs={{0,1},{1,2},{2,3},{3,0},{4,5},{5,6},{6,7},{7,4},{8,9},{9,10},{10,1... | collective-permute-start | bytes 393224 | tf_op jit(solution)/shard_map/ppermute | solution.py:215
  17.5 21.1 %collective-permute-start.4 = (bf16[128,512]{1,0:T(8,128)(2,1)S(1)}, bf16[128,512]{1,0:T(8,128)(2,1)S(1)}, u32[]{:S(2)}, u32[]{:S(2)}) collective-permute-start(bf16[128,512]{1,0:T(8,128)(2,1)S(1)} %slice_bitcast_fusion.3), channel_id=1, source_target_pairs={{0,2},{1,3},{2,0},{3,1},{4,6},{5,7},{6,4},{7,5},{8,10},{9,11},{10,... | collective-permute-start | bytes 393224 | tf_op jit(solution)/shard_map/ppermute | solution.py:215
  21.8 16.7 %collective-permute-start.5 = (bf16[128,512]{1,0:T(8,128)(2,1)S(1)}, bf16[128,512]{1,0:T(8,128)(2,1)S(1)}, u32[]{:S(2)}, u32[]{:S(2)}) collective-permute-start(bf16[128,512]{1,0:T(8,128)(2,1)S(1)} %slice_bitcast_fusion.3), channel_id=1, source_target_pairs={{0,3},{1,0},{2,1},{3,2},{4,7},{5,4},{6,5},{7,6},{8,11},{9,8},{10,9... | collective-permute-start | bytes 393224 | tf_op jit(solution)/shard_map/ppermute | solution.py:215
  39.8 24.5 %all-to-all-start.1 = ((f32[16,8,512]{2,1,0:T(8,128)}), f32[16,8,512]{2,1,0:T(8,128)S(1)}, u32[]{:S(2)}, u32[]{:S(2)}) async-start(f32[16,8,512]{2,1,0:T(8,128)} %subtract_bitcast_fusion), calls=%async_computation.1 | async-start | bytes 524288 | tf_op jit(solution)/shard_map/all_to_all | solution.py:246
  53.1 16.6 %collective-permute-start.6 = (bf16[1024,256]{1,0:T(8,128)(2,1)S(1)}, bf16[1024,256]{1,0:T(8,128)(2,1)S(1)}, u32[]{:S(2)}, u32[]{:S(2)}) collective-permute-start(bf16[1024,256]{1,0:T(8,128)(2,1)S(1)} %convolution_convert_fusion), channel_id=1, source_target_pairs={{0,32},{32,0},{1,33},{33,1},{2,34},{34,2},{3,35},{35,3},{4,36},{36... | collective-permute-start | bytes 1572872 | tf_op jit(solution)/shard_map/ppermute | solution.py:253
  65.2 21.8 %all-to-all-start.2 = ((f32[32,8,512]{2,1,0:T(8,128)}), f32[32,8,512]{2,1,0:T(8,128)S(1)}, u32[]{:S(2)}, u32[]{:S(2)}) async-start(f32[32,8,512]{2,1,0:T(8,128)} %broadcast_in_dim.14), calls=%async_computation.2 | async-start | bytes 1048576 | tf_op jit(solution)/shard_map/all_to_all | solution.py:22
  70.1 9.9 %collective-permute-start.7 = (bf16[4,128,256]{2,1,0:T(8,128)(2,1)S(1)}, bf16[4,128,256]{2,1,0:T(8,128)(2,1)S(1)}, u32[]{:S(2)}, u32[]{:S(2)}) collective-permute-start(bf16[4,128,256]{2,1,0:T(8,128)(2,1)S(1)} %fusion.15), channel_id=1, source_target_pairs={{0,64},{64,0},{1,65},{65,1},{2,66},{66,2},{3,67},{67,3},{4,68},{68... | collective-permute-start | bytes 786440 | tf_op jit(solution)/shard_map/ppermute | solution.py:257
  87.9 22.6 %all-to-all-start.3 = ((f32[16,8,1152]{2,1,0:T(8,128)}), f32[16,8,1152]{2,1,0:T(8,128)S(1)}, u32[]{:S(2)}, u32[]{:S(2)}) async-start(f32[16,8,1152]{2,1,0:T(8,128)} %first_rows.1), calls=%async_computation.3 | async-start | bytes 1179648 | tf_op jit(solution)/shard_map/all_to_all | solution.py:271
  91.9 8.6 %collective-permute-start.8 = (bf16[512,128]{1,0:T(8,128)(2,1)S(1)}, bf16[512,128]{1,0:T(8,128)(2,1)S(1)}, u32[]{:S(2)}, u32[]{:S(2)}) collective-permute-start(bf16[512,128]{1,0:T(8,128)(2,1)S(1)} %get-tuple-element.45), channel_id=1, source_target_pairs={{0,0},{1,1},{2,32},{3,33},{32,2},{33,3},{34,34},{35,35},{4,4},{5,5... | collective-permute-start | bytes 393224 | tf_op jit(solution)/shard_map/ppermute | solution.py:265
  96.8 7.8 %collective-permute-start.9 = (bf16[512,128]{1,0:T(8,128)(2,1)S(1)}, bf16[512,128]{1,0:T(8,128)(2,1)S(1)}, u32[]{:S(2)}, u32[]{:S(2)}) collective-permute-start(bf16[512,128]{1,0:T(8,128)(2,1)S(1)} %get-tuple-element.46), channel_id=1, source_target_pairs={{0,1},{1,0},{2,33},{3,32},{32,3},{33,2},{34,35},{35,34},{4,5},{5,4... | collective-permute-start | bytes 393224 | tf_op jit(solution)/shard_map/ppermute | solution.py:265
  110.5 14.2 %all-to-all-start.4 = ((bf16[4,256,128]{2,1,0:T(8,128)(2,1)}), bf16[4,256,128]{2,1,0:T(8,128)(2,1)S(1)}, u32[]{:S(2)}, u32[]{:S(2)}) async-start(bf16[4,256,128]{2,1,0:T(8,128)(2,1)} %pad_maximum_fusion), calls=%async_computation.4 | async-start | bytes 524288 | tf_op jit(solution)/shard_map/all_to_all | solution.py:274
  125.4 0.9 copy-start.1

commit v11 on v10

--- a/solution.py
+++ b/solution.py
@@ -15,11 +15,6 @@
 
 def dot_t(a, b, out=F32):
     return lax.dot_general(a, b, (((1,), (1,)), ((), ())), preferred_element_type=out)
-
-
-def share(array, axis, size):
-    copies = jnp.broadcast_to(array[None], (size,) + array.shape)
-    return lax.all_to_all(copies, axis, 0, 0, tiled=True)
 
 
 def lane(tile, k):
@@ -136,6 +131,14 @@
     )(*args)
 
 
+def strip_copies(pieces_ref, copies_ref, unused):
+    strip = pieces_ref[0]
+    for g in range(1, pieces_ref.shape[0]):
+        strip = strip + pieces_ref[g]
+    for k in range(copies_ref.shape[0]):
+        copies_ref[k] = strip
+
+
 def first_rows(strips_ref, top_ref, unused):
     y, x = lax.axis_index("y"), lax.axis_index("x")
     lane_at = pl.ds(pl.multiple_of(x * LANES, LANES), LANES)
@@ -244,8 +247,8 @@
     strip_rows = rows // (Z * C)
     part = base - dot_t(block, jnp.concatenate(cols, axis=0))
     pieces = lax.all_to_all(part.reshape(Z * C, strip_rows, X * rows), GROUP, 0, 0, tiled=True)
-    strip = jnp.sum(pieces, axis=0)
-    strips = share(strip, ("y", "x"), Y * X)
+    (strips,) = in_vmem(strip_copies, [(Y * X, strip_rows, X * rows)], (SUB, LANES), "strip_copies", pieces)
+    strips = lax.all_to_all(strips, ("y", "x"), 0, 0, tiled=True)
 
     row_blocks = along_y.reshape(Y * rows, depth)
     theirs = jnp.concatenate([choose(shifted, 2 - 2 * c), choose(shifted, 3 - 2 * c)], axis=0)

time: 127 us -> 127 us (level)
    pallas_call x2 -> x3, Pallas kernels: 11.6 us -> 12.5 us  [in_vmem(): pl.pallas_call(body, out_shape=[jax.ShapeDtypeStruct(shape, F32) for shap...]
  transfers between devices with their start and end apart: 15 -> 15, of which waited for: 7 -> 7; matrix products, arithmetic and copies ran while one was open for 3% -> 2% of each run, Pallas kernels for 9% -> 9%
where the time goes in v11:
time: 127 us; the launch traced here: 126 us
  starting transfers between devices  56.7 us (45%)
  waiting for transfers between devices  47.4 us (37%)
  Pallas kernels  15.4 us (12%)
  matrix products  2.71 us (2%)
  other arithmetic  1.89 us (1%)
    all_to_all x1, waiting for transfers between devices, body(): along_y = lax.all_to_all(copies, 'y', 0, 0, tiled=True)  13.3 us
    all_to_all x1, starting transfers between devices, body(): lax.all_to_all(part.reshape(Z * C, strip_rows, X * rows), GROUP, 0, 0, ti...  12.8 us
    pallas_call x3, Pallas kernels, in_vmem(): pl.pallas_call(body, out_shape=[jax.ShapeDtypeStruct(shape, F32) for shap...  12.5 us
    ppermute x3, starting transfers between devices, body(): lax.ppermute(own, 'x', [(i, (i + k) % X) for i in range(X)])  10.5 us
    all_to_all x1, waiting for transfers between devices, body(): lax.all_to_all(part.reshape(Z * C, strip_rows, X * rows), GROUP, 0, 0, ti...  9.23 us
    ppermute x1, waiting for transfers between devices, body(): got = lax.ppermute(give, 'zl', [(0, 1), (1, 0)])  7.98 us
    ppermute x2, starting transfers between devices, place(): return lax.ppermute(block, ('c', 'x'), pairs).reshape(Z // 2, rows, rows)  7.85 us
    all_to_all x1, starting transfers between devices, body(): along_y = lax.all_to_all(copies, 'y', 0, 0, tiled=True)  7.8 us
  transfers between devices with their start and end apart: 15, of which 7 were waited for; matrix products, arithmetic and copies ran while one was open for 2% of the time, Pallas kernels for 9%

profile of v11, /device:TPU:1, one launch (start us, length us, event | category | flops | bytes accessed | tf_op | source)
XLA Modules:
  0.0 126.3 jit_solution(13208812215579036057)
XLA Ops:
  0.6 2.9 %leaf_panels.1 = (bf16[2,128,256]{2,1,0:T(8,128)(2,1)}, bf16[8,128,512]{2,1,0:T(8,128)(2,1)}) custom-call(f32[2,128,256]{2,1,0:T(8,128)} %rows_hbm.1, f32[2,256,256]{2,1,0:T(8,128)} %inverse_hbm.1, s32[2,16]{1,0:T(2,128)} %pattern_hbm.1, s32[2]{0:T(128)} %widths_hbm.1), custom_call_target="tpu_custom_call" | custom-call | tf_op jit(solution)/shard_map/leaf_panels/pallas_call | solution.py:197
  3.5 0.0 copy-start
  3.6 7.8 %all-to-all-start = ((bf16[8,128,512]{2,1,0:T(8,128)(2,1)}), bf16[8,128,512]{2,1,0:T(8,128)(2,1)S(1)}, u32[]{:S(2)}, u32[]{:S(2)}) async-start(bf16[8,128,512]{2,1,0:T(8,128)(2,1)} %get-tuple-element.19), calls=%async_computation | async-start | bytes 2097152 | tf_op jit(solution)/shard_map/all_to_all | solution.py:217
  11.4 0.0 copy-done
  11.4 0.7 collective-permute-start
  12.1 0.0 collective-permute-done
  12.1 0.7 collective-permute-start.1
  12.8 0.7 collective-permute-start.2
  13.4 0.9 slice_bitcast_fusion.3
  14.4 3.1 %collective-permute-start.3 = (bf16[128,512]{1,0:T(8,128)(2,1)S(1)}, bf16[128,512]{1,0:T(8,128)(2,1)S(1)}, u32[]{:S(2)}, u32[]{:S(2)}) collective-permute-start(bf16[128,512]{1,0:T(8,128)(2,1)S(1)} %slice_bitcast_fusion.3), channel_id=1, source_target_pairs={{0,1},{1,2},{2,3},{3,0},{4,5},{5,6},{6,7},{7,4},{8,9},{9,10},{10,1... | collective-permute-start | bytes 393224 | tf_op jit(solution)/shard_map/ppermute | solution.py:218
  17.5 4.4 %collective-permute-start.4 = (bf16[128,512]{1,0:T(8,128)(2,1)S(1)}, bf16[128,512]{1,0:T(8,128)(2,1)S(1)}, u32[]{:S(2)}, u32[]{:S(2)}) collective-permute-start(bf16[128,512]{1,0:T(8,128)(2,1)S(1)} %slice_bitcast_fusion.3), channel_id=1, source_target_pairs={{0,2},{1,3},{2,0},{3,1},{4,6},{5,7},{6,4},{7,5},{8,10},{9,11},{10,... | collective-permute-start | bytes 393224 | tf_op jit(solution)/shard_map/ppermute | solution.py:218
  21.9 3.1 %collective-permute-start.5 = (bf16[128,512]{1,0:T(8,128)(2,1)S(1)}, bf16[128,512]{1,0:T(8,128)(2,1)S(1)}, u32[]{:S(2)}, u32[]{:S(2)}) collective-permute-start(bf16[128,512]{1,0:T(8,128)(2,1)S(1)} %slice_bitcast_fusion.3), channel_id=1, source_target_pairs={{0,3},{1,0},{2,1},{3,2},{4,7},{5,4},{6,5},{7,6},{8,11},{9,8},{10,9... | collective-permute-start | bytes 393224 | tf_op jit(solution)/shard_map/ppermute | solution.py:218
  25.1 0.0 collective-permute-done.1
  25.1 0.0 collective-permute-done.2
  25.2 13.3 %all-to-all-done = bf16[8,128,512]{2,1,0:T(8,128)(2,1)S(1)} async-done(((bf16[8,128,512]{2,1,0:T(8,128)(2,1)}), bf16[8,128,512]{2,1,0:T(8,128)(2,1)S(1)}, u32[]{:S(2)}, u32[]{:S(2)}) %all-to-all-start) | async-done | bytes 1048608 | tf_op jit(solution)/shard_map/all_to_all | solution.py:217
  38.5 0.0 collective-permute-done.3
  38.6 0.0 collective-permute-done.4
  38.6 0.0 collective-permute-done.5
  38.6 0.1 select_select_fusion.7
  38.6 0.1 select_select_fusion.3
  38.7 0.3 fusion.1
  39.0 0.7 subtract_bitcast_fusion
  39.8 12.8 %all-to-all-start.1 = ((f32[16,8,512]{2,1,0:T(8,128)}), f32[16,8,512]{2,1,0:T(8,128)S(1)}, u32[]{:S(2)}, u32[]{:S(2)}) async-start(f32[16,8,512]{2,1,0:T(8,128)} %subtract_bitcast_fusion), calls=%async_computation.1 | async-start | bytes 524288 | tf_op jit(solution)/shard_map/all_to_all | solution.py:249
  52.6 0.5 convolution_convert_fusion
  53.1 2.0 %collective-permute-start.6 = (bf16[1024,256]{1,0:T(8,128)(2,1)S(1)}, bf16[1024,256]{1,0:T(8,128)(2,1)S(1)}, u32[]{:S(2)}, u32[]{:S(2)}) collective-permute-start(bf16[1024,256]{1,0:T(8,128)(2,1)S(1)} %convolution_convert_fusion), channel_id=1, source_target_pairs={{0,32},{32,0},{1,33},{33,1},{2,34},{34,2},{3,35},{35,3},{4,36},{36... | collective-permute-start | bytes 1572872 | tf_op jit(solution)/shard_map/ppermute | solution.py:256
  55.1 9.2 %all-to-all-done.1.pieces_ref = f32[16,8,512]{2,1,0:T(8,128)S(1)} async-done(((f32[16,8,512]{2,1,0:T(8,128)}), f32[16,8,512]{2,1,0:T(8,128)S(1)}, u32[]{:S(2)}, u32[]{:S(2)}) %all-to-all-start.1) | async-done | bytes 262176 | tf_op jit(solution)/shard_map/all_to_all | solution.py:249
  64.3 0.9 strip_copies.1
  65.2 4.4 %all-to-all-start.2 = ((f32[32,8,512]{2,1,0:T(8,128)}), f32[32,8,512]{2,1,0:T(8,128)S(1)}, u32[]{:S(2)}, u32[]{:S(2)}) async-start(f32[32,8,512]{2,1,0:T(8,128)} %strip_copies.1), calls=%async_computation.2 | async-start | bytes 1048576 | tf_op jit(solution)/shard_map/all_to_all | solution.py:251
  69.6 0.0 collective-permute-done.6
  69.6 0.5 add_convert_fusion
  70.2 1.9 %collective-permute-start.7 = (bf16[4,128,256]{2,1,0:T(8,128)(2,1)S(1)}, bf16[4,128,256]{2,1,0:T(8,128)(2,1)S(1)}, u32[]{:S(2)}, u32[]{:S(2)}) collective-permute-start(bf16[4,128,256]{2,1,0:T(8,128)(2,1)S(1)} %fusion.15), channel_id=1, source_target_pairs={{0,64},{64,0},{1,65},{65,1},{2,66},{66,2},{3,67},{67,3},{4,68},{68... | collective-permute-start | bytes 786440 | tf_op jit(solution)/shard_map/ppermute | solution.py:260
  72.1 8.0 %collective-permute-done.7 = bf16[4,128,256]{2,1,0:T(8,128)(2,1)S(1)} collective-permute-done((bf16[4,128,256]{2,1,0:T(8,128)(2,1)S(1)}, bf16[4,128,256]{2,1,0:T(8,128)(2,1)S(1)}, u32[]{:S(2)}, u32[]{:S(2)}) %collective-permute-start.7) | collective-permute-done | bytes 262176 | tf_op jit(solution)/shard_map/ppermute | solution.py:260
  80.1 6.9 %all-to-all-done.2.strips_ref = f32[32,8,512]{2,1,0:T(8,128)S(1)} async-done(((f32[32,8,512]{2,1,0:T(8,128)}), f32[32,8,512]{2,1,0:T(8,128)S(1)}, u32[]{:S(2)}, u32[]{:S(2)}) %all-to-all-start.2) | async-done | bytes 524320 | tf_op jit(solution)/shard_map/all_to_all | solution.py:251
  87.0 0.9 first_rows.1
  87.9 3.9 %all-to-all-start.3 = ((f32[16,8,1152]{2,1,0:T(8,128)}), f32[16,8,1152]{2,1,0:T(8,128)S(1)}, u32[]{:S(2)}, u32[]{:S(2)}) async-start(f32[16,8,1152]{2,1,0:T(8,128)} %first_rows.1), calls=%async_computation.3 | async-start | bytes 1179648 | tf_op jit(solution)/shard_map/all_to_all | solution.py:274
  91.8 0.1 fusion.9
  92.0 4.9 %collective-permute-start.8 = (bf16[512,128]{1,0:T(8,128)(2,1)S(1)}, bf16[512,128]{1,0:T(8,128)(2,1)S(1)}, u32[]{:S(2)}, u32[]{:S(2)}) collective-permute-start(bf16[512,128]{1,0:T(8,128)(2,1)S(1)} %get-tuple-element.45), channel_id=1, source_target_pairs={{0,0},{1,1},{2,32},{3,33},{32,2},{33,3},{34,34},{35,35},{4,4},{5,5... | collective-permute-start | bytes 393224 | tf_op jit(solution)/shard_map/ppermute | solution.py:268
  96.9 3.0 %collective-permute-start.9 = (bf16[512,128]{1,0:T(8,128)(2,1)S(1)}, bf16[512,128]{1,0:T(8,128)(2,1)S(1)}, u32[]{:S(2)}, u32[]{:S(2)}) collective-permute-start(bf16[512,128]{1,0:T(8,128)(2,1)S(1)} %get-tuple-element.46), channel_id=1, source_target_pairs={{0,1},{1,0},{2,33},{3,32},{32,3},{33,2},{34,35},{35,34},{4,5},{5,4... | collective-permute-start | bytes 393224 | tf_op jit(solution)/shard_map/ppermute | solution.py:268
  99.8 0.7 collective-permute-done.8
  100.6 4.1 %collective-permute-done.9 = bf16[512,128]{1,0:T(8,128)(2,1)S(1)} collective-permute-done((bf16[512,128]{1,0:T(8,128)(2,1)S(1)}, bf16[512,128]{1,0:T(8,128)(2,1)S(1)}, u32[]{:S(2)}, u32[]{:S(2)}) %collective-permute-start.9) | collective-permute-done | bytes 131104 | tf_op jit(solution)/shard_map/ppermute | solution.py:268
  104.7 0.7 pad_maximum_fusion
  105.4 5.1 %all-to-all-done.3 = f32[16,8,1152]{2,1,0:T(8,128)S(1)} async-done(((f32[16,8,1152]{2,1,0:T(8,128)}), f32[16,8,1152]{2,1,0:T(8,128)S(1)}, u32[]{:S(2)}, u32[]{:S(2)}) %all-to-all-start.3) | async-done | bytes 589856 | tf_op jit(solution)/shard_map/all_to_all | solution.py:274
  110.5 3.4 %all-to-all-start.4 = ((bf16[4,256,128]{2,1,0:T(8,128)(2,1)}), bf16[4,256,128]{2,1,0:T(8,128)(2,1)S(1)}, u32[]{:S(2)}, u32[]{:S(2)}) async-start(bf16[4,256,128]{2,1,0:T(8,128)(2,1)} %pad_maximum_fusion), calls=%async_computation.4 | async-start | bytes 524288 | tf_op jit(solution)/shard_map/all_to_all | solution.py:277
  113.9 10.8 %inverse_factor.1 = f32[256,256]{1,0:T(8,128)S(1)} custom-call(f32[128,128]{1,0:T(8,128)S(1)} %slice.66.upper_ref, f32[128,256]{1,0:T(8,128)S(1)} %slice.67.lower_ref), custom_call_target="tpu_custom_call" | custom-call | flops 10000000000 | bytes 1000000 | tf_op jit(solution)/shard_map/inverse_factor/pallas_call | solution.py:122
  124.7 0.0 all-to-all-done.4
  124.8 0.6 convolution_convert_fusion.1
  125.4 0.0 copy-start.1
  125.4 0.9 fusion
  126.3 0.0 copy-done.1
  (13 shorter events, 0.2 us)
Async XLA Ops:
  3.5 7.8 %copy-start = (f32[256,128]{1,0:T(8,128)S(1)}, f32[256,128]{1,0:T(8,128)}, u32[]{:S(2)}) copy-start(f32[256,128]{1,0:T(8,128)} %param.9) | copy-start | bytes 393220
  3.6 35.0 %all-to-all-start = ((bf16[8,128,512]{2,1,0:T(8,128)(2,1)}), bf16[8,128,512]{2,1,0:T(8,128)(2,1)S(1)}, u32[]{:S(2)}, u32[]{:S(2)}) async-start(bf16[8,128,512]{2,1,0:T(8,128)(2,1)} %get-tuple-element.19), calls=%async_computation | async-start | bytes 2097152 | tf_op jit(solution)/shard_map/all_to_all | solution.py:217
  11.4 0.7 collective-permute-start
  12.1 13.0 %collective-permute-start.1 = (f32[128,128]{1,0:T(8,128)S(1)}, f32[128,128]{1,0:T(8,128)S(1)}, u32[]{:S(2)}, u32[]{:S(2)}) collective-permute-start(f32[128,128]{1,0:T(8,128)S(1)} %get-tuple-element.49), channel_id=1, source_target_pairs={{2,0},{3,1},{6,4},{7,5},{10,8},{11,9},{14,12},{15,13},{18,16},{19,... | collective-permute-start | bytes 196616 | tf_op jit(solution)/shard_map/ppermute | solution.py:232
  12.8 12.4 %collective-permute-start.2 = (f32[128,128]{1,0:T(8,128)S(1)}, f32[128,128]{1,0:T(8,128)S(1)}, u32[]{:S(2)}, u32[]{:S(2)}) collective-permute-start(f32[128,128]{1,0:T(8,128)S(1)} %get-tuple-element.50), channel_id=1, source_target_pairs={{3,0},{2,1},{7,4},{6,5},{11,8},{10,9},{15,12},{14,13},{19,16},{18,... | collective-permute-start | bytes 196616 | tf_op jit(solution)/shard_map/ppermute | solution.py:232
  14.4 24.2 %collective-permute-start.3 = (bf16[128,512]{1,0:T(8,128)(2,1)S(1)}, bf16[128,512]{1,0:T(8,128)(2,1)S(1)}, u32[]{:S(2)}, u32[]{:S(2)}) collective-permute-start(bf16[128,512]{1,0:T(8,128)(2,1)S(1)} %slice_bitcast_fusion.3), channel_id=1, source_target_pairs={{0,1},{1,2},{2,3},{3,0},{4,5},{5,6},{6,7},{7,4},{8,9},{9,10},{10,1... | collective-permute-start | bytes 393224 | tf_op jit(solution)/shard_map/ppermute | solution.py:218
  17.5 21.1 %collective-permute-start.4 = (bf16[128,512]{1,0:T(8,128)(2,1)S(1)}, bf16[128,512]{1,0:T(8,128)(2,1)S(1)}, u32[]{:S(2)}, u32[]{:S(2)}) collective-permute-start(bf16[128,512]{1,0:T(8,128)(2,1)S(1)} %slice_bitcast_fusion.3), channel_id=1, source_target_pairs={{0,2},{1,3},{2,0},{3,1},{4,6},{5,7},{6,4},{7,5},{8,10},{9,11},{10,... | collective-permute-start | bytes 393224 | tf_op jit(solution)/shard_map/ppermute | solution.py:218
  21.9 16.7 %collective-permute-start.5 = (bf16[128,512]{1,0:T(8,128)(2,1)S(1)}, bf16[128,512]{1,0:T(8,128)(2,1)S(1)}, u32[]{:S(2)}, u32[]{:S(2)}) collective-permute-start(bf16[128,512]{1,0:T(8,128)(2,1)S(1)} %slice_bitcast_fusion.3), channel_id=1, source_target_pairs={{0,3},{1,0},{2,1},{3,2},{4,7},{5,4},{6,5},{7,6},{8,11},{9,8},{10,9... | collective-permute-start | bytes 393224 | tf_op jit(solution)/shard_map/ppermute | solution.py:218
  39.8 24.5 %all-to-all-start.1 = ((f32[16,8,512]{2,1,0:T(8,128)}), f32[16,8,512]{2,1,0:T(8,128)S(1)}, u32[]{:S(2)}, u32[]{:S(2)}) async-start(f32[16,8,512]{2,1,0:T(8,128)} %subtract_bitcast_fusion), calls=%async_computation.1 | async-start | bytes 524288 | tf_op jit(solution)/shard_map/all_to_all | solution.py:249
  53.1 16.6 %collective-permute-start.6 = (bf16[1024,256]{1,0:T(8,128)(2,1)S(1)}, bf16[1024,256]{1,0:T(8,128)(2,1)S(1)}, u32[]{:S(2)}, u32[]{:S(2)}) collective-permute-start(bf16[1024,256]{1,0:T(8,128)(2,1)S(1)} %convolution_convert_fusion), channel_id=1, source_target_pairs={{0,32},{32,0},{1,33},{33,1},{2,34},{34,2},{3,35},{35,3},{4,36},{36... | collective-permute-start | bytes 1572872 | tf_op jit(solution)/shard_map/ppermute | solution.py:256
  65.2 21.8 %all-to-all-start.2 = ((f32[32,8,512]{2,1,0:T(8,128)}), f32[32,8,512]{2,1,0:T(8,128)S(1)}, u32[]{:S(2)}, u32[]{:S(2)}) async-start(f32[32,8,512]{2,1,0:T(8,128)} %strip_copies.1), calls=%async_computation.2 | async-start | bytes 1048576 | tf_op jit(solution)/shard_map/all_to_all | solution.py:251
  70.2 9.9 %collective-permute-start.7 = (bf16[4,128,256]{2,1,0:T(8,128)(2,1)S(1)}, bf16[4,128,256]{2,1,0:T(8,128)(2,1)S(1)}, u32[]{:S(2)}, u32[]{:S(2)}) collective-permute-start(bf16[4,128,256]{2,1,0:T(8,128)(2,1)S(1)} %fusion.15), channel_id=1, source_target_pairs={{0,64},{64,0},{1,65},{65,1},{2,66},{66,2},{3,67},{67,3},{4,68},{68... | collective-permute-start | bytes 786440 | tf_op jit(solution)/shard_map/ppermute | solution.py:260
  87.9 22.6 %all-to-all-start.3 = ((f32[16,8,1152]{2,1,0:T(8,128)}), f32[16,8,1152]{2,1,0:T(8,128)S(1)}, u32[]{:S(2)}, u32[]{:S(2)}) async-start(f32[16,8,1152]{2,1,0:T(8,128)} %first_rows.1), calls=%async_computation.3 | async-start | bytes 1179648 | tf_op jit(solution)/shard_map/all_to_all | solution.py:274
  92.0 8.6 %collective-permute-start.8 = (bf16[512,128]{1,0:T(8,128)(2,1)S(1)}, bf16[512,128]{1,0:T(8,128)(2,1)S(1)}, u32[]{:S(2)}, u32[]{:S(2)}) collective-permute-start(bf16[512,128]{1,0:T(8,128)(2,1)S(1)} %get-tuple-element.45), channel_id=1, source_target_pairs={{0,0},{1,1},{2,32},{3,33},{32,2},{33,3},{34,34},{35,35},{4,4},{5,5... | collective-permute-start | bytes 393224 | tf_op jit(solution)/shard_map/ppermute | solution.py:268
  96.9 7.8 %collective-permute-start.9 = (bf16[512,128]{1,0:T(8,128)(2,1)S(1)}, bf16[512,128]{1,0:T(8,128)(2,1)S(1)}, u32[]{:S(2)}, u32[]{:S(2)}) collective-permute-start(bf16[512,128]{1,0:T(8,128)(2,1)S(1)} %get-tuple-element.46), channel_id=1, source_target_pairs={{0,1},{1,0},{2,33},{3,32},{32,3},{33,2},{34,35},{35,34},{4,5},{5,4... | collective-permute-start | bytes 393224 | tf_op jit(solution)/shard_map/ppermute | solution.py:268
  110.5 14.2 %all-to-all-start.4 = ((bf16[4,256,128]{2,1,0:T(8,128)(2,1)}), bf16[4,256,128]{2,1,0:T(8,128)(2,1)S(1)}, u32[]{:S(2)}, u32[]{:S(2)}) async-start(bf16[4,256,128]{2,1,0:T(8,128)(2,1)} %pad_maximum_fusion), calls=%async_computation.4 | async-start | bytes 524288 | tf_op jit(solution)/shard_map/all_to_all | solution.py:277
  125.4 0.9 copy-start.1
